TPU v7x, 32 devices: a whole 2x2x4 slice. The times are simulated.
32 devices in a mesh: dp: 16 (over z, x, core), tensor: 2 (over y).
Axes of the slice: x: 2, y: 2, z: 4, core: 2. Of those that a mesh axis runs over, the one named last changes fastest.
Arguments:
- tokens: bfloat16 [8192, 1536], P('dp'), may hold values from -6 to 6
- cotangent: bfloat16 [8192, 1536], P('dp'), may hold values from -6 to 6
- doc_ids: int32 [8192], P('dp'), may hold values from -1 to 3, as said below
- norm_gains: float32 [2, 1536], replicated, may hold values from 0.5 to 1.5
- qkv_weight: float32 [1536, 2048], P('dp', 'tensor'), may hold values from -0.15625 to 0.15625
- qkv_bias: float32 [2048], P('tensor'), may hold values from -7 to 7
- out_weight: float32 [1536, 1536], P('dp', 'tensor'), may hold values from -0.4375 to 0.4375
- gate_up_weight: float32 [2, 1536, 8960], P(None, 'dp', 'tensor'), may hold values from -0.15625 to 0.15625
- down_weight: float32 [1536, 8960], P('dp', 'tensor'), may hold values from -0.0625 to 0.0625
- gains_moment: float32 [2, 1536], replicated, may hold values from -256 to 256
- qkv_moment: float32 [1536, 2048], P('dp', 'tensor'), may hold values from -320 to 320
- bias_moment: float32 [2048], P('tensor'), may hold values from -56 to 56
- out_moment: float32 [1536, 1536], P('dp', 'tensor'), may hold values from -28 to 28
- gate_up_moment: float32 [2, 1536, 8960], P(None, 'dp', 'tensor'), may hold values from -28 to 28
- down_moment: float32 [1536, 8960], P('dp', 'tensor'), may hold values from -56 to 56
Outputs:
- layer_out: float32 [8192, 1536], P('dp')
- tokens_grad: float32 [8192, 1536], P('dp')
- gains_grad: float32 [2, 1536], replicated
- qkv_grad: float32 [1536, 2048], P('dp', 'tensor')
- bias_grad: float32 [2048], P('tensor')
- out_grad: float32 [1536, 1536], P('dp', 'tensor')
- gate_up_grad: float32 [2, 1536, 8960], P(None, 'dp', 'tensor')
- down_grad: float32 [1536, 8960], P('dp', 'tensor')
- gains_new: float32 [2, 1536], replicated
- qkv_new: float32 [1536, 2048], P('dp', 'tensor')
- bias_new: float32 [2048], P('tensor')
- out_new: float32 [1536, 1536], P('dp', 'tensor')
- gate_up_new: float32 [2, 1536, 8960], P(None, 'dp', 'tensor')
- down_new: float32 [1536, 8960], P('dp', 'tensor')
- gains_moment_new: float32 [2, 1536], replicated
- qkv_moment_new: float32 [1536, 2048], P('dp', 'tensor')
- bias_moment_new: float32 [2048], P('tensor')
- out_moment_new: float32 [1536, 1536], P('dp', 'tensor')
- gate_up_moment_new: float32 [2, 1536, 8960], P(None, 'dp', 'tensor')
- down_moment_new: float32 [1536, 8960], P('dp', 'tensor')
Inputs may be any that keep to these rules, and one draw needn't show every extreme that they name: `doc_ids`: within each block of 512 slots (one index of dp) the filled slots come first, as whole sequences numbered upward from 0 (numbers may be skipped), followed by empty slots marked -1; a block holds at most 4 sequences; in every draw one block is a single sequence of 512 tokens and one block holds 4 sequences.
All inputs are finite; a program needn't handle non-finite values.
Results may differ from a plain program's by a relative error of at most 0.018.
The roundings to bfloat16 on the way count: a program that leaves them out, or rounds other values in their place, can miss the bound.
Values may be sent and summed in bfloat16 or wider, within the bound.
A program may use at most 384 MiB of HBM per device.

v0:
```python
import jax
import jax.numpy as jnp
from jax import lax
from jax.sharding import PartitionSpec as P

HD = 128
FFB = 896
NSI = 5


EPS = 1e-06
THETA = 1000000.0
MOMENTUM = 0.5
LR_MATRIX = 0.2
LR_OUT = 0.8
LR_VECTOR = 0.1
LR_BIAS = 1.0
NS_A = 3.4445
NS_B = -4.775
NS_C = 2.0315
HIGH = lax.Precision.HIGHEST
FLOAT = jnp.float32
BFLOAT = jnp.bfloat16


def as_sent(value):
    return jax.tree.map(lambda a: a.astype(jnp.bfloat16) if a.dtype == jnp.float32 else a, value)


def contract(left, right, left_dim, right_dim):
    return lax.dot_general(
        left, right, (((left_dim,), (right_dim,)), ((), ())), preferred_element_type=FLOAT
    )


def positions_of(block_ids):
    index = jnp.arange(block_ids.shape[0], dtype=jnp.int32)
    change = jnp.concatenate([jnp.ones((1,), dtype=bool), block_ids[1:] != block_ids[:-1]])
    start = lax.cummax(jnp.where(change, index, jnp.zeros_like(index)), axis=0)
    return index - start


def rotate(values, cosine, sine, direction):
    half = values.shape[-1] // 2
    first = values[..., :half]
    second = values[..., half:]
    cosine = cosine[:, None, :]
    sine = sine[:, None, :] * direction
    return jnp.concatenate(
        [first * cosine - second * sine, second * cosine + first * sine], axis=-1
    )


def rms_scale(values):
    return lax.rsqrt(jnp.mean(values * values, axis=-1, keepdims=True) + EPS)


def norm_back(grad, values, scale, gain):
    scaled = grad * gain
    return scale * scaled - values * scale * scale * scale * jnp.mean(
        scaled * values, axis=-1, keepdims=True
    )


def newton(block):
    ortho = block / (jnp.sqrt(jnp.sum(block * block)) + 1e-07)
    for step in range(NSI):
        gram = jnp.dot(ortho.T, ortho, precision=HIGH, preferred_element_type=FLOAT)
        polynomial = NS_B * gram + NS_C * jnp.dot(
            gram, gram, precision=HIGH, preferred_element_type=FLOAT
        )
        ortho = NS_A * ortho + jnp.dot(
            ortho, polynomial, precision=HIGH, preferred_element_type=FLOAT
        )
    return ortho


def solve_items(items):
    solved = jax.vmap(newton, in_axes=1, out_axes=1)(items[:, 0])
    return solved[:, None]


def padded(matrix):
    return jnp.pad(matrix, ((0, 0), (0, FFB - matrix.shape[1])))


def vector_step(param, moment_new, rate):
    return param - rate * moment_new * lax.rsqrt(
        jnp.mean(moment_new * moment_new, axis=-1, keepdims=True) + EPS
    )


def fetch_attention(qkv_weight, out_weight):
    return (
        lax.all_gather(qkv_weight.astype(BFLOAT), "dp", axis=0, tiled=True),
        lax.all_gather(out_weight.astype(BFLOAT), "dp", axis=0, tiled=True),
    )


def fetch_ffn(gate_up_weight, down_weight):
    return (
        lax.all_gather(gate_up_weight.astype(BFLOAT), "dp", axis=1, tiled=True),
        lax.all_gather(down_weight.astype(BFLOAT), "dp", axis=0, tiled=True),
    )


def shards(
    tokens,
    cotangent,
    doc_ids,
    norm_gains,
    qkv_weight,
    qkv_bias,
    out_weight,
    gate_up_weight,
    down_weight,
    gains_moment,
    qkv_moment,
    bias_moment,
    out_moment,
    gate_up_moment,
    down_moment,
):
    rows = qkv_weight.shape[0]
    count = tokens.shape[0]
    query_width = out_weight.shape[1]
    heads = query_width // HD
    group_width = qkv_weight.shape[1]
    kv_heads = (group_width - query_width) // (2 * HD)
    share = heads // kv_heads
    kv_width = kv_heads * HD
    scale = HD ** (-0.5)
    qkv_full, out_full = fetch_attention(qkv_weight, out_weight)
    gate_up_full, down_full = fetch_ffn(gate_up_weight, down_weight)
    positions = positions_of(doc_ids)
    freq = THETA ** (-(2.0 / HD) * jnp.arange(HD // 2, dtype=FLOAT))
    angle = positions.astype(FLOAT)[:, None] * freq[None, :]
    cosine = jnp.cos(angle)
    sine = jnp.sin(angle)
    index = jnp.arange(count)
    allowed = (doc_ids[:, None] == doc_ids[None, :]) & (index[None, :] <= index[:, None])
    inputs = tokens.astype(FLOAT)
    scale_one = rms_scale(inputs)
    normed = (inputs * scale_one * norm_gains[0]).astype(BFLOAT)
    qkv = (jnp.dot(normed, qkv_full, preferred_element_type=FLOAT) + qkv_bias).reshape(
        count, heads + 2 * kv_heads, HD
    )
    query = (
        rotate(qkv[:, :heads], cosine, sine, 1.0).astype(BFLOAT).reshape(count, kv_heads, share, HD)
    )
    keys = rotate(qkv[:, heads : heads + kv_heads], cosine, sine, 1.0).astype(BFLOAT)
    values = qkv[:, heads + kv_heads :].astype(BFLOAT)

    def scores_of():
        raw = jnp.einsum("qngd,knd->ngqk", query, keys, preferred_element_type=FLOAT) * scale
        return jnp.where(allowed[None, None], raw, -1e30)

    scores = scores_of()
    top = jnp.max(scores, axis=-1, keepdims=True)
    log_total = top + jnp.log(jnp.sum(jnp.exp(scores - top), axis=-1, keepdims=True))
    probs_low = jnp.exp(scores - log_total).astype(BFLOAT)
    attn = jnp.einsum("ngqk,knd->qngd", probs_low, values, preferred_element_type=FLOAT)
    attn = attn.reshape(count, query_width).astype(BFLOAT)
    branch = lax.psum(contract(attn, out_full, 1, 1).astype(jnp.bfloat16), "tensor").astype(
        jnp.float32
    )
    hidden1 = inputs + branch
    scale_two = rms_scale(hidden1)
    normed2 = (hidden1 * scale_two * norm_gains[1]).astype(BFLOAT)
    gate = jnp.dot(normed2, gate_up_full[0], preferred_element_type=FLOAT)
    up = jnp.dot(normed2, gate_up_full[1], preferred_element_type=FLOAT)
    sigma = jax.nn.sigmoid(gate)
    activated = gate * sigma
    hid = (activated * up).astype(BFLOAT)
    down = lax.psum(contract(hid, down_full, 1, 1).astype(jnp.bfloat16), "tensor").astype(
        jnp.float32
    )
    layer_out = hidden1 + down
    gate_up_full, down_full = (
        lax.all_gather(gate_up_weight.astype(BFLOAT), "dp", axis=1, tiled=True),
        lax.all_gather(down_weight.astype(BFLOAT), "dp", axis=0, tiled=True),
    )
    live = (doc_ids >= 0).astype(FLOAT)
    grad_out = cotangent.astype(FLOAT) * live[:, None]
    grad_low = grad_out.astype(BFLOAT)
    down_term = contract(grad_low, hid, 0, 0)
    dhid = jnp.dot(grad_low, down_full, preferred_element_type=FLOAT)
    dgate = (dhid * up * sigma * (1.0 + gate * (1.0 - sigma))).astype(BFLOAT)
    dup = (dhid * activated).astype(BFLOAT)
    gate_term = contract(normed2, dgate, 0, 0)
    up_term = contract(normed2, dup, 0, 0)
    dnormed2 = contract(dgate, gate_up_full[0], 1, 1) + contract(dup, gate_up_full[1], 1, 1)
    dnormed2 = lax.psum(dnormed2.astype(jnp.bfloat16), "tensor").astype(jnp.float32)
    dhidden1 = grad_out + norm_back(dnormed2, hidden1, scale_two, norm_gains[1])
    gain_two = jnp.sum(dnormed2 * hidden1 * scale_two, axis=0)
    qkv_full, out_full = (
        lax.all_gather(qkv_weight.astype(BFLOAT), "dp", axis=0, tiled=True),
        lax.all_gather(out_weight.astype(BFLOAT), "dp", axis=0, tiled=True),
    )
    dbranch = dhidden1.astype(BFLOAT)
    out_term = contract(dbranch, attn, 0, 0)
    dattn = (
        jnp.dot(dbranch, out_full, preferred_element_type=FLOAT)
        .astype(BFLOAT)
        .reshape(count, kv_heads, share, HD)
    )
    scores = scores_of()
    probs = jnp.exp(scores - log_total)
    probs_low = probs.astype(BFLOAT)
    dprobs = jnp.einsum("qngd,knd->ngqk", dattn, values, preferred_element_type=FLOAT)
    dscores = (probs * (dprobs - jnp.sum(probs * dprobs, axis=-1, keepdims=True))).astype(BFLOAT)
    dquery = jnp.einsum("ngqk,knd->qngd", dscores, keys, preferred_element_type=FLOAT) * scale
    dkeys = jnp.einsum("ngqk,qngd->knd", dscores, query, preferred_element_type=FLOAT) * scale
    dvalues = jnp.einsum("ngqk,qngd->knd", probs_low, dattn, preferred_element_type=FLOAT)
    dquery = rotate(dquery.reshape(count, heads, HD), cosine, sine, -1.0)
    dkeys = rotate(dkeys, cosine, sine, -1.0)
    dqkv = (
        jnp.concatenate([dquery, dkeys, dvalues], axis=1).reshape(count, group_width).astype(BFLOAT)
    )
    bias_term = jnp.sum(dqkv.astype(FLOAT), axis=0)
    qkv_term = contract(normed, dqkv, 0, 0)
    dnormed = contract(dqkv, qkv_full, 1, 1)
    gate_up_shard, down_shard, qkv_shard, out_shard = (
        lax.psum_scatter(jnp.stack([gate_term, up_term]), "dp", scatter_dimension=1, tiled=True),
        lax.psum_scatter(down_term, "dp", scatter_dimension=0, tiled=True),
        lax.psum_scatter(qkv_term, "dp", scatter_dimension=0, tiled=True),
        lax.psum_scatter(out_term, "dp", scatter_dimension=0, tiled=True),
    )
    dnormed = lax.psum(dnormed.astype(jnp.bfloat16), "tensor").astype(jnp.float32)
    tokens_grad = dhidden1 + norm_back(dnormed, inputs, scale_one, norm_gains[0])
    gain_one = jnp.sum(dnormed * inputs * scale_one, axis=0)
    gains_grad, bias_grad = lax.psum((jnp.stack([gain_one, gain_two]), bias_term), "dp")
    gains_m = MOMENTUM * gains_moment + gains_grad
    bias_m = MOMENTUM * bias_moment + bias_grad
    qkv_m = MOMENTUM * qkv_moment + qkv_shard
    out_m = MOMENTUM * out_moment + out_shard
    gate_up_m = MOMENTUM * gate_up_moment + gate_up_shard
    down_m = MOMENTUM * down_moment + down_shard
    units = gate_up_m.shape[2]
    heads_blocks = jnp.stack(
        [
            padded(qkv_m[:, :query_width]),
            padded(qkv_m[:, query_width : query_width + kv_width]),
            padded(qkv_m[:, query_width + kv_width :]),
            padded(out_m),
        ],
        axis=1,
    )
    packed = jnp.concatenate(
        [
            heads_blocks,
            gate_up_m[0].reshape(rows, -1, FFB),
            gate_up_m[1].reshape(rows, -1, FFB),
            down_m.reshape(rows, -1, FFB),
        ],
        axis=1,
    )
    devices = lax.axis_size("dp")
    total = packed.shape[1]
    per_owner = (total + devices - 1) // devices
    packed = jnp.pad(packed, ((0, 0), (0, per_owner * devices - total), (0, 0)))
    packed = packed.reshape(rows, devices, per_owner, FFB)
    ortho = solve_items(
        lax.all_to_all(
            packed.astype(jnp.bfloat16), "dp", split_axis=1, concat_axis=0, tiled=True
        ).astype(packed.dtype)
    )
    returned = lax.all_to_all(as_sent(ortho), "dp", split_axis=0, concat_axis=1, tiled=True).astype(
        ortho.dtype
    )
    returned = returned.reshape(rows, devices * per_owner, FFB)
    runs = units // FFB
    qkv_update = jnp.concatenate(
        [returned[:, 0, :query_width], returned[:, 1, :kv_width], returned[:, 2, :kv_width]], axis=1
    )
    out_update = returned[:, 3, :query_width]
    gate_update = returned[:, 4 : 4 + runs].reshape(rows, units)
    up_update = returned[:, 4 + runs : 4 + 2 * runs].reshape(rows, units)
    down_update = returned[:, 4 + 2 * runs : 4 + 3 * runs].reshape(rows, units)
    gains_new = vector_step(norm_gains, gains_m, LR_VECTOR)
    bias_new = vector_step(qkv_bias, bias_m, LR_BIAS)
    return (
        layer_out,
        tokens_grad,
        gains_grad,
        qkv_shard,
        bias_grad,
        out_shard,
        gate_up_shard,
        down_shard,
        gains_new,
        qkv_weight - LR_MATRIX * qkv_update,
        bias_new,
        out_weight - LR_OUT * out_update,
        gate_up_weight - LR_MATRIX * jnp.stack([gate_update, up_update]),
        down_weight - LR_MATRIX * down_update,
        gains_m,
        qkv_m,
        bias_m,
        out_m,
        gate_up_m,
        down_m,
    )


def solution(mesh):
    placed = (
        P("dp", None),
        P("dp", None),
        P("dp"),
        P(),
        P("dp", "tensor"),
        P("tensor"),
        P("dp", "tensor"),
        P(None, "dp", "tensor"),
        P("dp", "tensor"),
        P(),
        P("dp", "tensor"),
        P("tensor"),
        P("dp", "tensor"),
        P(None, "dp", "tensor"),
        P("dp", "tensor"),
    )
    return jax.shard_map(
        shards,
        mesh=mesh,
        in_specs=placed,
        out_specs=(
            P("dp", None),
            P("dp", None),
            P(),
            P("dp", "tensor"),
            P("tensor"),
            P("dp", "tensor"),
            P(None, "dp", "tensor"),
            P("dp", "tensor"),
            P(),
            P("dp", "tensor"),
            P("tensor"),
            P("dp", "tensor"),
            P(None, "dp", "tensor"),
            P("dp", "tensor"),
            P(),
            P("dp", "tensor"),
            P("tensor"),
            P("dp", "tensor"),
            P(None, "dp", "tensor"),
            P("dp", "tensor"),
        ),
        check_vma=False,
    )
```

profile of v0, /device:TPU:27, one launch (start us, length us, event | category | flops | bytes accessed | tf_op | source)
XLA Modules:
  0.0 2503.9 jit_solution(9074016766171609348)
XLA Ops:
  18.2 37.1 %all-gather.5.cloned.1.call-done = bf16[1536,1024]{1,0:T(8,128)(2,1)} async-done(((bf16[96,1024]{1,0:T(8,128)(2,1)}), bf16[1536,1024]{1,0:T(8,128)(2,1)}) %all-gather.5.cloned.1.call-update) | async-done | bytes 3145744 | tf_op jit(solution)/shard_map/all_gather | solution.py:95
  109.2 46.6 %all-reduce.10.cloned.1.call-done = bf16[512,1536]{1,0:T(8,128)(2,1)} async-done(((bf16[512,1536]{1,0:T(8,128)(2,1)}), bf16[512,1536]{1,0:T(8,128)(2,1)}) %all-reduce.10.cloned.1.call-update) | async-done | bytes 1572880 | tf_op jit(solution)/shard_map/psum | solution.py:164
  159.8 137.3 %all-gather.9.cloned.1.call-done = bf16[2,1536,4480]{2,1,0:T(8,128)(2,1)} async-done(((bf16[2,96,4480]{2,1,0:T(8,128)(2,1)}), bf16[2,1536,4480]{2,1,0:T(8,128)(2,1)}) %all-gather.9.cloned.1.call-update) | async-done | bytes 27525136 | tf_op jit(solution)/shard_map/all_gather | solution.py:102
  322.9 83.3 %all-gather.11.cloned.1.call-done = bf16[1536,4480]{1,0:T(8,128)(2,1)} async-done(((bf16[96,4480]{1,0:T(8,128)(2,1)}), bf16[1536,4480]{1,0:T(8,128)(2,1)}) %all-gather.11.cloned.1.call-update) | async-done | bytes 13762576 | tf_op jit(solution)/shard_map/all_gather | solution.py:103
  451.9 52.3 %all-reduce.12.cloned.1.call-done = bf16[512,1536]{1,0:T(8,128)(2,1)} async-done(((bf16[512,1536]{1,0:T(8,128)(2,1)}), bf16[512,1536]{1,0:T(8,128)(2,1)}) %all-reduce.12.cloned.1.call-update) | async-done | bytes 1572880 | tf_op jit(solution)/shard_map/psum | solution.py:193
  592.1 38.2 %pad_maximum_fusion = f32[2,1536,4480]{2,1,0:T(8,128)} fusion(f32[1,1536,4480]{2,1,0:T(8,128)} %convolution_bitcast_fusion, f32[1,1536,4480]{2,1,0:T(8,128)} %convolution_bitcast_fusion.1), kind=kLoop, calls=%fused_computation | loop fusion | flops 13762560 | bytes 110100480 | tf_op jit(solution)/shard_map/stack | solution.py:224
  633.2 44.3 %reduce-scatter.5.cloned.1.call-done = f32[96,1024]{1,0:T(8,128)} async-done(((f32[1536,1024]{1,0:T(8,128)}), f32[96,1024]{1,0:T(8,128)}) %reduce-scatter.5.cloned.1.call-update) | async-done | bytes 393232 | tf_op jit(solution)/shard_map/reduce_scatter | solution.py:226
  682.8 261.8 %reduce-scatter.11.cloned.1.call-done = f32[96,4480]{1,0:T(8,128)} async-done(((f32[1536,4480]{1,0:T(8,128)}), f32[96,4480]{1,0:T(8,128)}) %reduce-scatter.11.cloned.1.call-update) | async-done | bytes 1720336 | tf_op jit(solution)/shard_map/reduce_scatter | solution.py:225
  949.0 506.4 %reduce-scatter.9.cloned.1.call-done = f32[2,96,4480]{2,1,0:T(8,128)} async-done(((f32[2,1536,4480]{2,1,0:T(8,128)}), f32[2,96,4480]{2,1,0:T(8,128)}) %reduce-scatter.9.cloned.1.call-update) | async-done | bytes 3440656 | tf_op jit(solution)/shard_map/reduce_scatter | solution.py:224
  1485.7 126.3 %all_to_all.8 = bf16[96,16,2,896]{3,0,2,1:T(8,128)(2,1)S(1)} all-to-all(bf16[96,16,2,896]{3,0,2,1:T(8,128)(2,1)} %copy.130), channel_id=1, replica_groups=mesh['dp'=16,'tensor'=2] {'dp'}, dimensions={1} | all-to-all | bytes 11010048 | tf_op jit(solution)/shard_map/all_to_all | solution.py:264
  1627.9 44.1 %fusion.12 = f32[2,896,896]{2,1,0:T(8,128)S(1)} fusion(f32[1536,2,896]{2,0,1:T(8,128)} %bitcast.269, f32[2]{0:T(128)S(1)} %sqrt_add_fusion), kind=kOutput, calls=%fused_computation.26 | convolution fusion | flops 29597761536 | bytes 17432584 | tf_op jit(solution)/shard_map/vmap()/dot_general | solution.py:68
  1694.8 46.6 %fusion.10 = f32[2,1536,896]{2,1,0:T(8,128)} fusion(f32[2,896,896]{2,1,0:T(8,128)S(1)} %fusion.152, f32[2,896,896]{2,1,0:T(8,128)S(1)} %fusion.12, f32[1536,2,896]{2,0,1:T(8,128)S(1)} %bitcast.274, f32[2]{0:T(128)S(1)} %sqrt_add_fusion), kind=kOutput, calls=%fused_computation.24 | convolution fusion | flops 29602578432 | bytes 34865160 | tf_op jit(solution)/shard_map/vmap()/dot_general | solution.py:72
  1741.4 45.8 %fusion.142 = f32[2,896,896]{2,1,0:T(8,128)S(1)} fusion(f32[2,1536,896]{2,1,0:T(8,128)} %fusion.10, f32[1536,2,896]{2,0,1:T(8,128)S(1)} %bitcast.275, f32[2]{0:T(128)S(1)} %sqrt_add_fusion), kind=kOutput, calls=%fused_computation.239 | convolution fusion | flops 29603266560 | bytes 28442632 | tf_op jit(solution)/shard_map/vmap()/dot_general | solution.py:68
  1814.8 52.5 %multiply_add_fusion.2 = (f32[2,1536,896]{2,1,0:T(8,128)}, f32[2,1536,896]{2,1,0:T(8,128)}) fusion(f32[2,1536,896]{2,1,0:T(8,128)} %fusion.10, f32[1536,2,896]{2,0,1:T(8,128)} %bitcast.270, f32[2]{0:T(128)S(1)} %sqrt_add_fusion, f32[2,896,896]{2,1,0:T(8,128)} %fusion.153, f32[2,896,896]{2,1,0:T(8,128)} %copy-done.8), kind=kOutput, calls=%fused_computation.31 | convolution fusion | flops 29621846016 | bytes 56885256 | tf_op jit(solution)/shard_map/vmap()/dot_general | solution.py:72
  1867.3 44.4 %fusion.154 = f32[2,896,896]{2,1,0:T(8,128)} fusion(f32[2,1536,896]{2,1,0:T(8,128)} %get-tuple-element.117), kind=kOutput, calls=%fused_computation.250 | convolution fusion | flops 29595009024 | bytes 17432576 | tf_op jit(solution)/shard_map/vmap()/dot_general | solution.py:68
  1911.7 29.3 %fusion.155 = f32[2,896,896]{2,1,0:T(8,128)} fusion(f32[2,896,896]{2,1,0:T(8,128)} %fusion.154), kind=kOutput, calls=%fused_computation.251 | convolution fusion | flops 17263755264 | bytes 12845056 | tf_op jit(solution)/shard_map/vmap()/dot_general | solution.py:69
  1941.1 58.6 %fusion.26 = f32[2,1536,896]{2,1,0:T(8,128)S(1)} fusion(f32[2,1536,896]{2,1,0:T(8,128)S(1)} %bitcast.258, f32[2,896,896]{2,1,0:T(8,128)} %fusion.155, f32[2,896,896]{2,1,0:T(8,128)} %fusion.154), kind=kOutput, calls=%fused_computation.45 | convolution fusion | flops 29599825920 | bytes 34865152 | tf_op jit(solution)/shard_map/vmap()/dot_general | solution.py:72
  1999.7 37.7 %fusion.140 = f32[2,896,896]{2,1,0:T(8,128)} fusion(f32[2,1536,896]{2,1,0:T(8,128)S(1)} %fusion.26, f32[2,1536,896]{2,1,0:T(8,128)S(1)} %bitcast.258), kind=kOutput, calls=%fused_computation.238 | convolution fusion | flops 29600514048 | bytes 28442624 | tf_op jit(solution)/shard_map/vmap()/dot_general | solution.py:68
  2066.5 47.0 %fusion.22 = f32[2,1536,896]{2,1,0:T(8,128)} fusion(f32[2,896,896]{2,1,0:T(8,128)} %fusion.156, f32[2,896,896]{2,1,0:T(8,128)} %fusion.140, f32[2,1536,896]{2,1,0:T(8,128)} %copy-done, f32[2,1536,896]{2,1,0:T(8,128)S(1)} %bitcast.258), kind=kOutput, calls=%fused_computation.41 | convolution fusion | flops 29605330944 | bytes 45875200 | tf_op jit(solution)/shard_map/vmap()/dot_general | solution.py:72
  2113.5 46.7 %fusion.40 = f32[2,896,896]{2,1,0:T(8,128)} fusion(f32[2,1536,896]{2,1,0:T(8,128)} %fusion.22, f32[2,1536,896]{2,1,0:T(8,128)} %copy-done, f32[2,1536,896]{2,1,0:T(8,128)S(1)} %bitcast.258), kind=kOutput, calls=%fused_computation.69 | convolution fusion | flops 29606019072 | bytes 39452672 | tf_op jit(solution)/shard_map/vmap()/dot_general | solution.py:68
  2160.2 29.8 %fusion.157 = f32[2,896,896]{2,1,0:T(8,128)} fusion(f32[2,896,896]{2,1,0:T(8,128)} %fusion.40), kind=kOutput, calls=%fused_computation.253 | convolution fusion | flops 17263755264 | bytes 12845056 | tf_op jit(solution)/shard_map/vmap()/dot_general | solution.py:69
  2190.0 55.5 %fusion.43 = bf16[1536,1,2,896]{3,0,2,1:T(8,128)(2,1)} fusion(f32[2,896,896]{2,1,0:T(8,128)} %fusion.157, f32[2,896,896]{2,1,0:T(8,128)} %fusion.40, f32[2,1536,896]{2,1,0:T(8,128)} %fusion.22, f32[2,1536,896]{2,1,0:T(8,128)} %copy-done, f32[2,1536,896]{2,1,0:T(8,128)} %get-tuple-element.118, f32[2,1536,896]{2,1,0:T(8,128)} %fusion.10, ...), kind=kOutput, calls=%fused_computation.74 | convolution fusion | flops 29643866112 | bytes 84410376 | tf_op jit(solution)/shard_map/vmap()/dot_general | solution.py:72
  2301.9 77.7 %all-reduce.14.cloned.1.call-done = (bf16[512,1536]{1,0:T(8,128)(2,1)}, bf16[512,1536]{1,0:T(8,128)(2,1)}) async-done(((bf16[512,1536]{1,0:T(8,128)(2,1)}, bf16[512,1536]{1,0:T(8,128)(2,1)}), (bf16[512,1536]{1,0:T(8,128)(2,1)}, bf16[512,1536]{1,0:T(8,128)(2,1)})) %all-reduce.14.cloned.1.call-update) | async-done | bytes 3145744 | tf_op jit(solution)/shard_map/psum | solution.py:175
  2382.2 57.2 %all-reduce.4 = (f32[2,1536]{1,0:T(2,128)S(1)}, f32[1024]{0:T(1024)S(1)}) all-reduce(f32[2,1536]{1,0:T(2,128)S(1)} %pad_maximum_fusion.4, f32[1024]{0:T(1024)S(1)} %bitcast.289), channel_id=1, replica_groups=mesh['dp'=16,'tensor'=2] {'dp'}, use_global_device_ids=true, to_apply=%region_15.16 | all-reduce | flops 4096 | bytes 32768 | tf_op jit(solution)/shard_map/psum | solution.py:232
  (297 shorter events, 481.4 us)
Async XLA Ops:
  7.2 48.2 %all-gather.5.cloned.1.call-start = ((), (), s32[]{:S(2)}) async-start(), calls=%async_computation.6 | async-start | bytes 3342336 | tf_op jit(solution)/shard_map/all_gather | solution.py:95
  9.0 90.4 %all-gather.7.cloned.1.call-start = ((), (), s32[]{:S(2)}) async-start(), calls=%async_computation.7 | async-start | bytes 2506752 | tf_op jit(solution)/shard_map/all_gather | solution.py:96
  10.7 145.1 %all-reduce.10.cloned.1.call-start = ((), (), s32[]{:S(2)}) async-start(), calls=%async_computation.8 | async-start | bytes 3145728 | tf_op jit(solution)/shard_map/psum | solution.py:164
  103.7 193.4 %all-gather.9.cloned.1.call-start = ((), (), s32[]{:S(2)}) async-start(), calls=%async_computation.9 | async-start | bytes 29245440 | tf_op jit(solution)/shard_map/all_gather | solution.py:102
  107.2 299.0 %all-gather.11.cloned.1.call-start = ((), (), s32[]{:S(2)}) async-start(), calls=%async_computation.10 | async-start | bytes 14622720 | tf_op jit(solution)/shard_map/all_gather | solution.py:103
  108.3 395.9 %all-reduce.12.cloned.1.call-start = ((), (), s32[]{:S(2)}) async-start(), calls=%async_computation.11 | async-start | bytes 3145728 | tf_op jit(solution)/shard_map/psum | solution.py:193
  109.2 398.3 %copy-start.56 = (f32[512]{0:T(512)}, f32[512]{0:T(512)S(1)}, u32[]{:S(2)}) copy-start(f32[512]{0:T(512)S(1)} %compare_convert_fusion) | copy-start | bytes 6148
  159.8 150.0 %copy-start.20 = (bf16[512,1536]{1,0:T(8,128)(2,1)}, bf16[512,1536]{1,0:T(8,128)(2,1)S(1)}, u32[]{:S(2)}) copy-start(bf16[512,1536]{1,0:T(8,128)(2,1)S(1)} %multiply_convert_fusion.3) | copy-start | bytes 4718596
  451.9 178.6 %reduce-scatter.7.cloned.1.call-start = ((), (), s32[]{:S(2)}) async-start(), calls=%async_computation.13 | async-start | bytes 5013504 | tf_op jit(solution)/shard_map/reduce_scatter | solution.py:227
  514.4 163.1 %reduce-scatter.5.cloned.1.call-start = ((), (), s32[]{:S(2)}) async-start(), calls=%async_computation.12 | async-start | bytes 6684672 | tf_op jit(solution)/shard_map/reduce_scatter | solution.py:226
  544.9 399.6 %reduce-scatter.11.cloned.1.call-start = ((), (), s32[]{:S(2)}) async-start(), calls=%async_computation.15 | async-start | bytes 29245440 | tf_op jit(solution)/shard_map/reduce_scatter | solution.py:225
  561.2 894.2 %reduce-scatter.9.cloned.1.call-start = ((), (), s32[]{:S(2)}) async-start(), calls=%async_computation.14 | async-start | bytes 58490880 | tf_op jit(solution)/shard_map/reduce_scatter | solution.py:224
  1867.3 73.8 %slice-start.1 = ((s8[11010048]{0:T(1024)(128)(4,1)}), s8[4194304]{0:T(1024)(128)(4,1)S(1)}, s32[]{:S(2)}) async-start(s8[11010048]{0:T(1024)(128)(4,1)} %bitcast.257), calls=%async_computation.18 | async-start | bytes 8388608
  2270.5 178.7 %all-to-all-start.1 = ((bf16[1536,1,2,896]{3,2,1,0:T(2,128)(2,1)}), bf16[1536,1,2,896]{3,2,1,0:T(2,128)(2,1)}, u32[]{:S(2)}, u32[]{:S(2)}) async-start(bf16[1536,1,2,896]{3,2,1,0:T(2,128)(2,1)} %copy.137), calls=%async_computation.5 | async-start | bytes 11010048 | tf_op jit(solution)/shard_map/all_to_all | solution.py:268
  2276.6 103.0 %all-reduce.14.cloned.1.call-start = ((), (), s32[]{:S(2)}) async-start(), calls=%async_computation.16 | async-start | bytes 6291456 | tf_op jit(solution)/shard_map/psum | solution.py:175
  2292.9 86.7 %copy-start.4 = (bf16[512,1536]{1,0:T(8,128)(2,1)S(1)}, bf16[512,1536]{1,0:T(8,128)(2,1)}, u32[]{:S(2)}) copy-start(bf16[512,1536]{1,0:T(8,128)(2,1)} %param.15) | copy-start | bytes 4718596
  2292.9 86.7 %copy-start.43 = (f32[1536]{0:T(1024)S(1)}, f32[1536]{0:T(1024)}, u32[]{:S(2)}) copy-start(f32[1536]{0:T(1024)} %copy-done.41) | copy-start | bytes 18436
  2292.9 86.7 %copy-start.51 = (f32[512]{0:T(512)S(1)}, f32[512]{0:T(512)}, u32[]{:S(2)}) copy-start(f32[512]{0:T(512)} %copy-done.49) | copy-start | bytes 6148
  2298.5 83.7 %copy-start.52 = (f32[8,128]{1,0:T(8,128)S(1)}, f32[8,128]{1,0:T(8,128)}, u32[]{:S(2)}) copy-start(f32[8,128]{1,0:T(8,128)} %get-tuple-element.82) | copy-start | bytes 12292
  2298.5 140.9 %copy-start.60 = (f32[1024]{0:T(1024)S(1)}, f32[1024]{0:T(1024)}, u32[]{:S(2)}) copy-start(f32[1024]{0:T(1024)} %param.26) | copy-start | bytes 12292
  2298.5 142.2 %copy-start.54 = (f32[2,1536]{1,0:T(2,128)S(1)}, f32[2,1536]{1,0:T(2,128)}, u32[]{:S(2)}) copy-start(f32[2,1536]{1,0:T(2,128)} %param.24) | copy-start | bytes 36868
  2298.5 142.4 %copy-start.61 = (f32[1024]{0:T(1024)S(1)}, f32[1024]{0:T(1024)}, u32[]{:S(2)}) copy-start(f32[1024]{0:T(1024)} %param.20) | copy-start | bytes 12292
  2298.5 143.0 %copy-start.44 = (f32[2,1536]{1,0:T(2,128)S(1)}, f32[2,1536]{1,0:T(2,128)}, u32[]{:S(2)}) copy-start(f32[2,1536]{1,0:T(2,128)} %param.18) | copy-start | bytes 36868
  2298.5 143.7 %copy-start.7 = (bf16[512,1536]{1,0:T(8,128)(2,1)S(1)}, bf16[512,1536]{1,0:T(8,128)(2,1)}, u32[]{:S(2)}) copy-start(bf16[512,1536]{1,0:T(8,128)(2,1)} %all-reduce.10.cloned.1.call-done) | copy-start | bytes 4718596
  (62 other events, 1107.2 us)
Sparse Core Ops, SparseCore 0:
  10.9 44.4 all-gather.4
  58.2 41.0 all-gather.6
  103.8 51.9 all-reduce.9
  157.8 139.1 all-gather.8
  300.0 106.1 all-gather.10
  452.0 52.1 all-reduce.11
  514.5 72.4 reduce-scatter.6
  592.0 85.4 reduce-scatter.4
  682.2 262.2 reduce-scatter.10
  949.8 505.6 reduce-scatter.8
  2293.0 86.5 all-reduce.13
where the time goes:
time: 2520 us; the launch traced here: 2500 us
  waiting for transfers between devices  1280 us (51%)
  matrix products  784 us (31%)
  blocking collectives  183 us (7%)
  other arithmetic  124 us (5%)
  local copies, waits for them, and re-layouts  115 us (5%)
    reduce_scatter x1, waiting for transfers between devices, shards(): lax.psum_scatter(jnp.stack([gate_term, up_term]), 'dp', scatter_dimension...  506 us
    reduce_scatter x1, waiting for transfers between devices, shards(): lax.psum_scatter(down_term, 'dp', scatter_dimension=0, tiled=True)  262 us
    dot_general x5, matrix products, newton(): jnp.dot(ortho, polynomial, precision=HIGH, preferred_element_type=FLOAT)  260 us
    dot_general x5, matrix products, newton(): gram = jnp.dot(ortho.T, ortho, precision=HIGH, preferred_element_type=FLOAT)  219 us
    all_gather x1, waiting for transfers between devices, fetch_ffn(): lax.all_gather(gate_up_weight.astype(BFLOAT), 'dp', axis=1, tiled=True)  137 us
    dot_general x5, matrix products, newton(): jnp.dot(gram, gram, precision=HIGH, preferred_element_type=FLOAT)  136 us
    all_to_all x1, blocking collectives, shards(): lax.all_to_all(packed.astype(jnp.bfloat16), 'dp', split_axis=1, concat_ax...  126 us
    dot_general x10, matrix products, contract(): lax.dot_general(left, right, (((left_dim,), (right_dim,)), ((), ())), pre...  97.8 us
  transfers between devices with their start and end apart: 12, of which 10 were waited for; matrix products, arithmetic and copies ran while one was open for 9% of the time, Pallas kernels for 0%

commit v1 on v0

v1 whole, which is shorter than its diff:
```python
import jax
import jax.numpy as jnp
from jax import lax
from jax.sharding import PartitionSpec as P

HD = 128
FFB = 896
NSI = 5


EPS = 1e-06
THETA = 1000000.0
MOMENTUM = 0.5
LR_MATRIX = 0.2
LR_OUT = 0.8
LR_VECTOR = 0.1
LR_BIAS = 1.0
NS_A = 3.4445
NS_B = -4.775
NS_C = 2.0315
HIGH = lax.Precision.HIGHEST
FLOAT = jnp.float32
BFLOAT = jnp.bfloat16


def contract(left, right, left_dim, right_dim):
    return lax.dot_general(
        left, right, (((left_dim,), (right_dim,)), ((), ())), preferred_element_type=FLOAT
    )


def positions_of(block_ids):
    index = jnp.arange(block_ids.shape[0], dtype=jnp.int32)
    change = jnp.concatenate([jnp.ones((1,), dtype=bool), block_ids[1:] != block_ids[:-1]])
    start = lax.cummax(jnp.where(change, index, jnp.zeros_like(index)), axis=0)
    return index - start


def rotate(values, cosine, sine, direction):
    half = values.shape[-1] // 2
    first = values[..., :half]
    second = values[..., half:]
    cosine = cosine[:, None, :]
    sine = sine[:, None, :] * direction
    return jnp.concatenate(
        [first * cosine - second * sine, second * cosine + first * sine], axis=-1
    )


def rms_scale(values):
    return lax.rsqrt(jnp.mean(values * values, axis=-1, keepdims=True) + EPS)


def norm_back(grad, values, scale, gain):
    scaled = grad * gain
    return scale * scaled - values * scale * scale * scale * jnp.mean(
        scaled * values, axis=-1, keepdims=True
    )


def low_dot(left, right, left_dim):
    return lax.dot_general(
        left.astype(BFLOAT),
        right.astype(BFLOAT),
        (((left_dim,), (0,)), ((), ())),
        preferred_element_type=FLOAT,
    )


def newton(block, group):
    same = (group[:, None] == group[None, :]).astype(FLOAT)
    width = jnp.sum(same, axis=0)
    eye = jnp.eye(same.shape[0], dtype=FLOAT)

    def squares(value):
        return jnp.dot(jnp.sum(value * value, axis=0), same, precision=HIGH)

    ortho = block.astype(FLOAT)
    ortho = ortho / (jnp.sqrt(squares(ortho)) + 1e-07)
    for step in range(NSI):
        shift = squares(ortho) / width
        gram = low_dot(ortho, ortho, 0) * same - eye * shift
        polynomial = (NS_B + 2.0 * NS_C * shift) * gram + NS_C * low_dot(gram, gram, 1)
        ortho = (NS_A + NS_B * shift + NS_C * shift * shift) * ortho + low_dot(
            ortho, polynomial, 1
        )
    return ortho


def vector_step(param, moment_new, rate):
    return param - rate * moment_new * lax.rsqrt(
        jnp.mean(moment_new * moment_new, axis=-1, keepdims=True) + EPS
    )


def bits_of(count):
    return [1 << bit for bit in range(count.bit_length() - 1)]


def swap(value, axis, stride):
    count = lax.axis_size(axis)
    return lax.ppermute(value, axis, [(at, at ^ stride) for at in range(count)])


def total_over(value, axis):
    for stride in bits_of(lax.axis_size(axis)):
        value = jax.tree.map(lambda a: a + swap(a, axis, stride), value)
    return value


def tensor_sum(value):
    value = value.astype(BFLOAT)
    if lax.axis_size("tensor") != 2:
        return lax.psum(value, "tensor").astype(FLOAT)
    return value.astype(FLOAT) + swap(value, "tensor", 1).astype(FLOAT)


def by_distance(value, order):
    count = lax.axis_size("dp")
    me = lax.axis_index("dp")
    bits = len(order)
    value = value.reshape((2,) * bits + (value.shape[0] // count,) + value.shape[1:])
    for at in range(bits):
        mine = (me >> (bits - 1 - at)) & 1
        value = jnp.where(mine == 1, jnp.flip(value, at), value)
    places = [bits - stride.bit_length() for stride in order]
    value = value.transpose(tuple(places) + tuple(range(bits, value.ndim)))
    return value.reshape((-1,) + value.shape[bits + 1 :])


def low_add(one, other):
    return (one.astype(FLOAT) + other.astype(FLOAT)).astype(BFLOAT)


def reduce_rows(left, right, order):
    half = left.shape[0] // 2
    sent = jnp.dot(left[half:], right, preferred_element_type=FLOAT).astype(BFLOAT)
    kept = jnp.dot(left[:half], right, preferred_element_type=FLOAT).astype(BFLOAT)
    for at, stride in enumerate(order):
        came = swap(sent, "dp", stride)
        if at == len(order) - 1:
            return kept.astype(FLOAT) + came.astype(FLOAT)
        half = kept.shape[0] // 2
        sent = low_add(kept[half:], came[half:])
        kept = low_add(kept[:half], came[:half])


def shards(
    tokens,
    cotangent,
    doc_ids,
    norm_gains,
    qkv_weight,
    qkv_bias,
    out_weight,
    gate_up_weight,
    down_weight,
    gains_moment,
    qkv_moment,
    bias_moment,
    out_moment,
    gate_up_moment,
    down_moment,
):
    rows = qkv_weight.shape[0]
    count = tokens.shape[0]
    query_width = out_weight.shape[1]
    heads = query_width // HD
    group_width = qkv_weight.shape[1]
    kv_heads = (group_width - query_width) // (2 * HD)
    share = heads // kv_heads
    kv_width = kv_heads * HD
    scale = HD ** (-0.5)
    devices = lax.axis_size("dp")
    me = lax.axis_index("dp")
    strides = bits_of(devices)
    x_first = tuple(strides)
    z_first = tuple(strides[:1] + strides[2:] + strides[1:2])
    attention_full = lax.all_gather(
        jnp.concatenate([qkv_weight.astype(BFLOAT), out_weight.astype(BFLOAT)], axis=1),
        "dp",
        axis=0,
        tiled=True,
    )
    qkv_full = attention_full[:, :group_width]
    out_full = attention_full[:, group_width:]
    gate_up_full = lax.all_gather(gate_up_weight.astype(BFLOAT), "dp", axis=1, tiled=True)
    down_full = lax.all_gather(down_weight.astype(BFLOAT), "dp", axis=0, tiled=True)
    live = (doc_ids >= 0).astype(FLOAT)
    grad_out = cotangent.astype(FLOAT) * live[:, None]
    grad_low = grad_out.astype(BFLOAT)
    grad_rows = by_distance(grad_low.T, x_first)
    positions = positions_of(doc_ids)
    freq = THETA ** (-(2.0 / HD) * jnp.arange(HD // 2, dtype=FLOAT))
    angle = positions.astype(FLOAT)[:, None] * freq[None, :]
    cosine = jnp.cos(angle)
    sine = jnp.sin(angle)
    index = jnp.arange(count)
    allowed = (doc_ids[:, None] == doc_ids[None, :]) & (index[None, :] <= index[:, None])
    inputs = tokens.astype(FLOAT)
    scale_one = rms_scale(inputs)
    normed = (inputs * scale_one * norm_gains[0]).astype(BFLOAT)
    normed_rows = by_distance(normed.T, z_first)
    qkv = (jnp.dot(normed, qkv_full, preferred_element_type=FLOAT) + qkv_bias).reshape(
        count, heads + 2 * kv_heads, HD
    )
    query = (
        rotate(qkv[:, :heads], cosine, sine, 1.0).astype(BFLOAT).reshape(count, kv_heads, share, HD)
    )
    keys = rotate(qkv[:, heads : heads + kv_heads], cosine, sine, 1.0).astype(BFLOAT)
    values = qkv[:, heads + kv_heads :].astype(BFLOAT)

    def scores_of():
        raw = jnp.einsum("qngd,knd->ngqk", query, keys, preferred_element_type=FLOAT) * scale
        return jnp.where(allowed[None, None], raw, -1e30)

    scores = scores_of()
    top = jnp.max(scores, axis=-1, keepdims=True)
    log_total = top + jnp.log(jnp.sum(jnp.exp(scores - top), axis=-1, keepdims=True))
    probs_low = jnp.exp(scores - log_total).astype(BFLOAT)
    attn = jnp.einsum("ngqk,knd->qngd", probs_low, values, preferred_element_type=FLOAT)
    attn = attn.reshape(count, query_width).astype(BFLOAT)
    branch = tensor_sum(contract(attn, out_full, 1, 1))
    hidden1 = inputs + branch
    scale_two = rms_scale(hidden1)
    normed2 = (hidden1 * scale_two * norm_gains[1]).astype(BFLOAT)
    normed2_rows = by_distance(normed2.T, x_first)
    gate = jnp.dot(normed2, gate_up_full[0], preferred_element_type=FLOAT)
    up = jnp.dot(normed2, gate_up_full[1], preferred_element_type=FLOAT)
    sigma = jax.nn.sigmoid(gate)
    activated = gate * sigma
    hid = (activated * up).astype(BFLOAT)
    down_shard = reduce_rows(grad_rows, hid, x_first)
    dhid = jnp.dot(grad_low, down_full, preferred_element_type=FLOAT)
    dgate = (dhid * up * sigma * (1.0 + gate * (1.0 - sigma))).astype(BFLOAT)
    dup = (dhid * activated).astype(BFLOAT)
    gate_shard = reduce_rows(normed2_rows, dgate, x_first)
    up_shard = reduce_rows(normed2_rows, dup, x_first)
    dnormed2 = contract(dgate, gate_up_full[0], 1, 1) + contract(dup, gate_up_full[1], 1, 1)
    dnormed2 = tensor_sum(dnormed2)
    layer_out = hidden1 + tensor_sum(contract(hid, down_full, 1, 1))
    dhidden1 = grad_out + norm_back(dnormed2, hidden1, scale_two, norm_gains[1])
    gain_two = jnp.sum(dnormed2 * hidden1 * scale_two, axis=0)
    dbranch = dhidden1.astype(BFLOAT)
    out_shard = reduce_rows(by_distance(dbranch.T, z_first), attn, z_first)
    dattn = (
        jnp.dot(dbranch, out_full, preferred_element_type=FLOAT)
        .astype(BFLOAT)
        .reshape(count, kv_heads, share, HD)
    )
    scores = scores_of()
    probs = jnp.exp(scores - log_total)
    probs_low = probs.astype(BFLOAT)
    dprobs = jnp.einsum("qngd,knd->ngqk", dattn, values, preferred_element_type=FLOAT)
    dscores = (probs * (dprobs - jnp.sum(probs * dprobs, axis=-1, keepdims=True))).astype(BFLOAT)
    dquery = jnp.einsum("ngqk,knd->qngd", dscores, keys, preferred_element_type=FLOAT) * scale
    dkeys = jnp.einsum("ngqk,qngd->knd", dscores, query, preferred_element_type=FLOAT) * scale
    dvalues = jnp.einsum("ngqk,qngd->knd", probs_low, dattn, preferred_element_type=FLOAT)
    dquery = rotate(dquery.reshape(count, heads, HD), cosine, sine, -1.0)
    dkeys = rotate(dkeys, cosine, sine, -1.0)
    dqkv = (
        jnp.concatenate([dquery, dkeys, dvalues], axis=1).reshape(count, group_width).astype(BFLOAT)
    )
    bias_term = jnp.sum(dqkv.astype(FLOAT), axis=0)
    qkv_shard = reduce_rows(normed_rows, dqkv, z_first)
    dnormed = tensor_sum(contract(dqkv, qkv_full, 1, 1))
    tokens_grad = dhidden1 + norm_back(dnormed, inputs, scale_one, norm_gains[0])
    gain_one = jnp.sum(dnormed * inputs * scale_one, axis=0)
    vectors = total_over(jnp.concatenate([gain_one, gain_two, bias_term]), "dp")
    gains_grad = vectors[: 2 * inputs.shape[1]].reshape(2, -1)
    bias_grad = vectors[2 * inputs.shape[1] :]
    gate_up_shard = jnp.stack([gate_shard, up_shard])
    gains_m = MOMENTUM * gains_moment + gains_grad
    bias_m = MOMENTUM * bias_moment + bias_grad
    qkv_m = MOMENTUM * qkv_moment + qkv_shard
    out_m = MOMENTUM * out_moment + out_shard
    gate_up_m = MOMENTUM * gate_up_moment + gate_up_shard
    down_m = MOMENTUM * down_moment + down_shard
    units = down_m.shape[1]
    runs = units // FFB

    def runs_of(matrix):
        return matrix.astype(BFLOAT).reshape(rows, runs, FFB).transpose(1, 0, 2)

    def unit_of(one, other):
        both = jnp.concatenate([one, other], axis=1).astype(BFLOAT)
        return jnp.pad(both, ((0, 0), (0, FFB - both.shape[1])))

    value_m = qkv_m[:, query_width + kv_width :]
    packed = jnp.concatenate(
        [
            runs_of(gate_up_m[0]),
            runs_of(gate_up_m[1]),
            runs_of(down_m),
            unit_of(out_m, value_m)[None],
        ]
    )
    total = packed.shape[0]
    per_owner = (total + devices - 1) // devices
    packed = jnp.pad(packed, ((0, per_owner * devices - total), (0, 0), (0, 0)))
    column = jnp.arange(FFB)
    paired = (column >= query_width).astype(jnp.int32) + (column >= query_width + kv_width).astype(jnp.int32)
    solved = []
    for turn in range(per_owner):
        unit = me + turn * devices
        block = lax.all_to_all(
            packed[turn * devices : (turn + 1) * devices], "dp", split_axis=0, concat_axis=0, tiled=True
        )
        group = jnp.where(unit == total - 1, paired, 0)
        ortho = newton(block.reshape(devices * rows, FFB), group)
        solved.append(
            lax.all_to_all(
                ortho.astype(BFLOAT).reshape(devices, rows, FFB), "dp", split_axis=0, concat_axis=0, tiled=True
            )
        )
    returned = jnp.concatenate(solved) if per_owner > 1 else solved[0]
    pair = newton(
        lax.all_gather(
            unit_of(qkv_m[:, :query_width], qkv_m[:, query_width : query_width + kv_width]),
            "dp",
            axis=0,
            tiled=True,
        ),
        paired,
    )
    pair = lax.dynamic_slice_in_dim(pair, me * rows, rows, 0)
    returned = returned.astype(FLOAT)

    def rows_of(first):
        return returned[first : first + runs].transpose(1, 0, 2).reshape(rows, units)

    last = returned[total - 1]
    qkv_update = jnp.concatenate(
        [pair[:, : query_width + kv_width], last[:, query_width : query_width + kv_width]], axis=1
    )
    out_update = last[:, :query_width]
    gate_up_update = jnp.stack([rows_of(0), rows_of(runs)])
    down_update = rows_of(2 * runs)
    gains_new = vector_step(norm_gains, gains_m, LR_VECTOR)
    bias_new = vector_step(qkv_bias, bias_m, LR_BIAS)
    return (
        layer_out,
        tokens_grad,
        gains_grad,
        qkv_shard,
        bias_grad,
        out_shard,
        gate_up_shard,
        down_shard,
        gains_new,
        qkv_weight - LR_MATRIX * qkv_update,
        bias_new,
        out_weight - LR_OUT * out_update,
        gate_up_weight - LR_MATRIX * gate_up_update,
        down_weight - LR_MATRIX * down_update,
        gains_m,
        qkv_m,
        bias_m,
        out_m,
        gate_up_m,
        down_m,
    )


def solution(mesh):
    placed = (
        P("dp", None),
        P("dp", None),
        P("dp"),
        P(),
        P("dp", "tensor"),
        P("tensor"),
        P("dp", "tensor"),
        P(None, "dp", "tensor"),
        P("dp", "tensor"),
        P(),
        P("dp", "tensor"),
        P("tensor"),
        P("dp", "tensor"),
        P(None, "dp", "tensor"),
        P("dp", "tensor"),
    )
    return jax.shard_map(
        shards,
        mesh=mesh,
        in_specs=placed,
        out_specs=(
            P("dp", None),
            P("dp", None),
            P(),
            P("dp", "tensor"),
            P("tensor"),
            P("dp", "tensor"),
            P(None, "dp", "tensor"),
            P("dp", "tensor"),
            P(),
            P("dp", "tensor"),
            P("tensor"),
            P("dp", "tensor"),
            P(None, "dp", "tensor"),
            P("dp", "tensor"),
            P(),
            P("dp", "tensor"),
            P("tensor"),
            P("dp", "tensor"),
            P(None, "dp", "tensor"),
            P("dp", "tensor"),
        ),
        check_vma=False,
    )
```

time: 2520 us -> 1320 us (0.52)
  waiting for transfers between devices: 1280 us -> 676 us
  matrix products: 784 us -> 404 us
  blocking collectives: 183 us -> 0 us
  local copies, waits for them, and re-layouts: 115 us -> 60.9 us
  starting transfers between devices: 6.67 us -> 35.9 us
    reduce_scatter x4 -> x0, waiting for transfers between devices: 813 us -> none  [the longest x1 506 us: shards(): lax.psum_scatter(jnp.stack([gate_term, up_term]), 'dp', scatter_dimension...]
    ppermute x0 -> x28, waiting for transfers between devices: none -> 412 us  [swap(): return lax.ppermute(value, axis, [(at, at ^ stride) for at in range(count)])]
    dot_general x15 -> x42, matrix products: 615 us -> 293 us  [the longest x20 230 us: low_dot(): lax.dot_general(left.astype(BFLOAT), right.astype(BFLOAT), (((left_dim,),...]
    psum x3 -> x0, waiting for transfers between devices: 176 us -> none  [the longest x1 77.7 us: shards(): lax.psum(contract(hid, down_full, 1, 1).astype(jnp.bfloat16), 'tensor')]
    all_to_all x1 -> x0, blocking collectives: 126 us -> none  [shards(): lax.all_to_all(packed.astype(jnp.bfloat16), 'dp', split_axis=1, concat_ax...]
    psum x1 -> x0, blocking collectives: 57.2 us -> none  [shards(): lax.psum((jnp.stack([gain_one, gain_two]), bias_term), 'dp')]
    dot_general x10 -> x5, matrix products: 97.8 us -> 45.7 us  [contract(): lax.dot_general(left, right, (((left_dim,), (right_dim,)), ((), ())), pre...]
    convert_element_type x4 -> x1, local copies, waits for them, and re-layouts: 50.1 us -> 2.47 us  [runs_of(): return matrix.astype(BFLOAT).reshape(rows, runs, FFB).transpose(1, 0, 2)]
  transfers between devices with their start and end apart: 12 -> 34, of which waited for: 10 -> 20; matrix products, arithmetic and copies ran while one was open for 9% -> 22% of each run, Pallas kernels for 0% -> 0%
where the time goes in v1:
time: 1320 us; the launch traced here: 1310 us
  waiting for transfers between devices  676 us (51%)
  matrix products  404 us (31%)
  other arithmetic  119 us (9%)
  local copies, waits for them, and re-layouts  60.9 us (5%)
  starting transfers between devices  35.9 us (3%)
  between operations  16.5 us (1%)
    ppermute x28, waiting for transfers between devices, swap(): return lax.ppermute(value, axis, [(at, at ^ stride) for at in range(count)])  412 us
    dot_general x20, matrix products, low_dot(): lax.dot_general(left.astype(BFLOAT), right.astype(BFLOAT), (((left_dim,),...  230 us
    all_gather x1, waiting for transfers between devices, shards(): lax.all_gather(gate_up_weight.astype(BFLOAT), 'dp', axis=1, tiled=True)  129 us
    all_gather x1, waiting for transfers between devices, shards(): lax.all_gather(down_weight.astype(BFLOAT), 'dp', axis=0, tiled=True)  50.8 us
    all_gather x1, waiting for transfers between devices, shards(): lax.all_gather(jnp.concatenate([qkv_weight.astype(BFLOAT), out_weight.ast...  49.3 us
    dot_general x5, matrix products, contract(): lax.dot_general(left, right, (((left_dim,), (right_dim,)), ((), ())), pre...  45.7 us
    convert_element_type x15, other arithmetic, low_add(): return (one.astype(FLOAT) + other.astype(FLOAT)).astype(BFLOAT)  33.5 us
    dot_general x5, matrix products, reduce_rows(): jnp.dot(left[half:], right, preferred_element_type=FLOAT).astype(BFLOAT)  27.4 us
  transfers between devices with their start and end apart: 34, of which 20 were waited for; matrix products, arithmetic and copies ran while one was open for 22% of the time, Pallas kernels for 0%

profile of v1, /device:TPU:27, one launch (start us, length us, event | category | flops | bytes accessed | tf_op | source)
XLA Modules:
  0.0 1312.8 jit_solution(6932695894094561081)
XLA Ops:
  18.1 49.3 %all-gather.5.cloned.1.call-done = bf16[1536,1792]{1,0:T(8,128)(2,1)} async-done(((bf16[96,1792]{1,0:T(8,128)(2,1)}), bf16[1536,1792]{1,0:T(8,128)(2,1)}) %all-gather.5.cloned.1.call-update) | async-done | bytes 5505040 | tf_op jit(solution)/shard_map/all_gather | solution.py:179
  94.3 28.2 %collective-permute-done = bf16[512,1536]{1,0:T(8,128)(2,1)} collective-permute-done((bf16[512,1536]{1,0:T(8,128)(2,1)}, bf16[512,1536]{1,0:T(8,128)(2,1)}, u32[]{:S(2)}, u32[]{:S(2)}) %collective-permute-start) | collective-permute-done | bytes 1572896 | tf_op jit(solution)/shard_map/ppermute | solution.py:102
  125.6 50.8 %all-gather.9.cloned.1.call-done = bf16[1536,4480]{1,0:T(8,128)(2,1)} async-done(((bf16[96,4480]{1,0:T(8,128)(2,1)}), bf16[1536,4480]{1,0:T(8,128)(2,1)}) %all-gather.9.cloned.1.call-update) | async-done | bytes 13762576 | tf_op jit(solution)/shard_map/all_gather | solution.py:188
  189.9 128.6 %all-gather.7.cloned.1.call-done = bf16[2,1536,4480]{2,1,0:T(8,128)(2,1)} async-done(((bf16[2,96,4480]{2,1,0:T(8,128)(2,1)}), bf16[2,1536,4480]{2,1,0:T(8,128)(2,1)}) %all-gather.7.cloned.1.call-update) | async-done | bytes 27525136 | tf_op jit(solution)/shard_map/all_gather | solution.py:187
  331.6 18.6 %multiply_convert_fusion = (bf16[512,4480]{1,0:T(8,128)(2,1)}, bf16[512,4480]{1,0:T(8,128)(2,1)}, bf16[512,4480]{1,0:T(8,128)(2,1)}) fusion(f32[512,4480]{1,0:T(8,128)S(1)} %copy-done.80, f32[512,4480]{1,0:T(8,128)} %fusion.27, bf16[2,1536,4480]{2,1,0:T(8,128)(2,1)} %all-gather.7.cloned.1.call-done, f32[512,1536]{1,0:T(8,128)S(1)} %get-tuple-element.108, ...), kind=kOutput, calls=%fused_computation.42 | convolution fusion | flops 7083196416 | bytes 49029120 | tf_op jit(solution)/shard_map/dot_general | solution.py:228
  394.5 18.9 %collective-permute-done.2 = bf16[512,1536]{1,0:T(8,128)(2,1)} collective-permute-done((bf16[512,1536]{1,0:T(8,128)(2,1)}, bf16[512,1536]{1,0:T(8,128)(2,1)}, u32[]{:S(2)}, u32[]{:S(2)}) %collective-permute-start.2) | collective-permute-done | bytes 1572896 | tf_op jit(solution)/shard_map/ppermute | solution.py:102
  416.3 30.8 %collective-permute-done.1 = bf16[512,1536]{1,0:T(8,128)(2,1)} collective-permute-done((bf16[512,1536]{1,0:T(8,128)(2,1)}, bf16[512,1536]{1,0:T(8,128)(2,1)}, u32[]{:S(2)}, u32[]{:S(2)}) %collective-permute-start.1) | collective-permute-done | bytes 1572896 | tf_op jit(solution)/shard_map/ppermute | solution.py:102
  577.6 15.4 %collective-permute-done.9 = bf16[384,1024]{1,0:T(8,128)(2,1)S(1)} collective-permute-done((bf16[384,1024]{1,0:T(8,128)(2,1)S(1)}, bf16[384,1024]{1,0:T(8,128)(2,1)S(1)}, u32[]{:S(2)}, u32[]{:S(2)}) %collective-permute-start.9) | collective-permute-done | bytes 786464 | tf_op jit(solution)/shard_map/ppermute | solution.py:102
  594.3 19.8 %collective-permute-done.13 = bf16[384,768]{1,0:T(8,128)(2,1)S(1)} collective-permute-done((bf16[384,768]{1,0:T(8,128)(2,1)S(1)}, bf16[384,768]{1,0:T(8,128)(2,1)S(1)}, u32[]{:S(2)}, u32[]{:S(2)}) %collective-permute-start.13) | collective-permute-done | bytes 589856 | tf_op jit(solution)/shard_map/ppermute | solution.py:102
  658.7 24.3 %all-gather.11.cloned.1.call-done = bf16[1536,896]{1,0:T(8,128)(2,1)} async-done(((bf16[96,896]{1,0:T(8,128)(2,1)}), bf16[1536,896]{1,0:T(8,128)(2,1)}) %all-gather.11.cloned.1.call-update) | async-done | bytes 2752528 | tf_op jit(solution)/shard_map/all_gather | solution.py:318
  693.3 33.5 %collective-permute-done.25 = bf16[384,4480]{1,0:T(8,128)(2,1)} collective-permute-done((bf16[384,4480]{1,0:T(8,128)(2,1)}, bf16[384,4480]{1,0:T(8,128)(2,1)}, u32[]{:S(2)}, u32[]{:S(2)}) %collective-permute-start.25) | collective-permute-done | bytes 3440672 | tf_op jit(solution)/shard_map/ppermute | solution.py:102
  729.8 70.7 %collective-permute-done.17 = bf16[384,4480]{1,0:T(8,128)(2,1)} collective-permute-done((bf16[384,4480]{1,0:T(8,128)(2,1)}, bf16[384,4480]{1,0:T(8,128)(2,1)}, u32[]{:S(2)}, u32[]{:S(2)}) %collective-permute-start.17) | collective-permute-done | bytes 3440672 | tf_op jit(solution)/shard_map/ppermute | solution.py:102
  803.4 70.8 %collective-permute-done.21 = bf16[384,4480]{1,0:T(8,128)(2,1)} collective-permute-done((bf16[384,4480]{1,0:T(8,128)(2,1)}, bf16[384,4480]{1,0:T(8,128)(2,1)}, u32[]{:S(2)}, u32[]{:S(2)}) %collective-permute-start.21) | collective-permute-done | bytes 3440672 | tf_op jit(solution)/shard_map/ppermute | solution.py:102
  880.9 70.7 %collective-permute-done.22 = bf16[192,4480]{1,0:T(8,128)(2,1)S(1)} collective-permute-done((bf16[192,4480]{1,0:T(8,128)(2,1)S(1)}, bf16[192,4480]{1,0:T(8,128)(2,1)S(1)}, u32[]{:S(2)}, u32[]{:S(2)}) %collective-permute-start.22) | collective-permute-done | bytes 1720352 | tf_op jit(solution)/shard_map/ppermute | solution.py:102
  959.8 32.7 %collective-permute-done.23 = bf16[96,4480]{1,0:T(8,128)(2,1)} collective-permute-done((bf16[96,4480]{1,0:T(8,128)(2,1)}, bf16[96,4480]{1,0:T(8,128)(2,1)}, u32[]{:S(2)}, u32[]{:S(2)}) %collective-permute-start.23) | collective-permute-done | bytes 860192 | tf_op jit(solution)/shard_map/ppermute | solution.py:102
  1016.9 13.9 %multiply_reduce_fusion.9 = (f32[896]{0:T(1024)S(1)}, f32[1536,896]{1,0:T(8,128)}) fusion(f32[896,896]{1,0:T(8,128)} %fusion.253, f32[896]{0:T(1024)S(1)} %get-tuple-element.78, f32[896]{0:T(1024)S(1)} %get-tuple-element.77, s32[896]{0:T(1024)S(1)} %copy-done.64, f32[896]{0:T(1024)S(1)} %sqrt_add_fusion.1, ...), kind=kOutput, calls=%fused_computation.93 | convolution fusion | flops 3929324544 | bytes 11490304 | tf_op jit(solution)/shard_map/dot_general | solution.py:62
  1040.9 15.5 %multiply_reduce_fusion.8 = (f32[896]{0:T(1024)S(1)}, f32[1536,896]{1,0:T(8,128)}) fusion(f32[896,896]{1,0:T(8,128)} %fusion.193, f32[896]{0:T(1024)S(1)} %get-tuple-element.76, f32[896]{0:T(1024)S(1)} %get-tuple-element.75, s32[896]{0:T(1024)S(1)} %copy-done.64, f32[1536,896]{1,0:T(8,128)} %get-tuple-element.177, f32[896]{0:T(1024)S(1)} %fusion.289), kind=kOutput, calls=%fused_computation.91 | convolution fusion | flops 3923819520 | bytes 14239232 | tf_op jit(solution)/shard_map/dot_general | solution.py:62
  1088.8 15.0 %multiply_reduce_fusion.3 = (f32[896]{0:T(1024)S(1)}, f32[1536,896]{1,0:T(8,128)}) fusion(f32[896,896,1]{1,0,2:T(8,128)} %fusion.69, f32[896]{0:T(1024)S(1)} %get-tuple-element.88, f32[896]{0:T(1024)S(1)} %get-tuple-element.87, s32[896]{0:T(1024)S(1)} %copy-done.66, f32[1536,896]{1,0:T(8,128)} %bitcast_divide_fusion, f32[896]{0:T(1024)S(1)} %fusion.293), kind=kOutput, calls=%fused_computation.83 | convolution fusion | flops 3923819520 | bytes 14239232 | tf_op jit(solution)/shard_map/dot_general | solution.py:62
  1113.8 15.4 %multiply_reduce_fusion.2 = (f32[896]{0:T(1024)S(1)}, f32[1536,896]{1,0:T(8,128)}) fusion(f32[896,896]{1,0:T(8,128)} %fusion.180, f32[896]{0:T(1024)S(1)} %get-tuple-element.86, f32[896]{0:T(1024)S(1)} %get-tuple-element.85, s32[896]{0:T(1024)S(1)} %copy-done.66, f32[1536,896]{1,0:T(8,128)} %get-tuple-element.169, f32[896]{0:T(1024)S(1)} %fusion.294), kind=kOutput, calls=%fused_computation.81 | convolution fusion | flops 3923819520 | bytes 14239232 | tf_op jit(solution)/shard_map/dot_general | solution.py:62
  1139.2 15.0 %multiply_reduce_fusion.1 = (f32[896]{0:T(1024)S(1)}, f32[1536,896]{1,0:T(8,128)}) fusion(f32[896,896]{1,0:T(8,128)} %fusion.177, f32[896]{0:T(1024)S(1)} %get-tuple-element.84, f32[896]{0:T(1024)S(1)} %get-tuple-element.83, s32[896]{0:T(1024)S(1)} %copy-done.66, f32[1536,896]{1,0:T(8,128)} %get-tuple-element.171, f32[896]{0:T(1024)S(1)} %fusion.295), kind=kOutput, calls=%fused_computation.79 | convolution fusion | flops 3923819520 | bytes 14239232 | tf_op jit(solution)/shard_map/dot_general | solution.py:62
  1164.7 15.2 %multiply_reduce_fusion = (f32[896]{0:T(1024)S(1)}, f32[1536,896]{1,0:T(8,128)}) fusion(f32[896,896]{1,0:T(8,128)} %fusion.174, f32[896]{0:T(1024)S(1)} %get-tuple-element.82, f32[896]{0:T(1024)S(1)} %get-tuple-element.81, s32[896]{0:T(1024)S(1)} %copy-done.66, f32[1536,896]{1,0:T(8,128)} %get-tuple-element.173, f32[896]{0:T(1024)S(1)} %fusion.296), kind=kOutput, calls=%fused_computation.77 | convolution fusion | flops 3923819520 | bytes 14239232 | tf_op jit(solution)/shard_map/dot_general | solution.py:62
  1189.9 14.3 %add_convert_fusion.6 = bf16[1536,896]{1,0:T(8,128)(2,1)} fusion(f32[1536,896]{1,0:T(8,128)} %get-tuple-element.175, f32[896]{0:T(1024)S(1)} %fusion.297, f32[896,896]{1,0:T(8,128)} %fusion.171, f32[896]{0:T(1024)S(1)} %get-tuple-element.80, f32[896]{0:T(1024)S(1)} %get-tuple-element.79, s32[896]{0:T(1024)S(1)} %copy-done.66), kind=kOutput, calls=%fused_computation.76 | convolution fusion | flops 3922444288 | bytes 11483136 | tf_op jit(solution)/shard_map/dot_general | solution.py:62
  1210.0 15.1 %multiply_reduce_fusion.7 = (f32[896]{0:T(1024)S(1)}, f32[1536,896]{1,0:T(8,128)}) fusion(f32[896,896]{1,0:T(8,128)} %fusion.190, f32[896]{0:T(1024)S(1)} %get-tuple-element.74, f32[896]{0:T(1024)S(1)} %get-tuple-element.73, s32[896]{0:T(1024)S(1)} %copy-done.64, f32[1536,896]{1,0:T(8,128)} %get-tuple-element.179, f32[896]{0:T(1024)S(1)} %fusion.290), kind=kOutput, calls=%fused_computation.89 | convolution fusion | flops 3923819520 | bytes 14239232 | tf_op jit(solution)/shard_map/dot_general | solution.py:62
  1235.2 15.5 %multiply_reduce_fusion.6 = (f32[896]{0:T(1024)S(1)}, f32[1536,896]{1,0:T(8,128)}) fusion(f32[896,896]{1,0:T(8,128)} %fusion.187, f32[896]{0:T(1024)S(1)} %get-tuple-element.72, f32[896]{0:T(1024)S(1)} %get-tuple-element.71, s32[896]{0:T(1024)S(1)} %copy-done.64, f32[1536,896]{1,0:T(8,128)} %get-tuple-element.181, f32[896]{0:T(1024)S(1)} %fusion.291), kind=kOutput, calls=%fused_computation.87 | convolution fusion | flops 3923819520 | bytes 14239232 | tf_op jit(solution)/shard_map/dot_general | solution.py:62
  (483 shorter events, 498.7 us)
Async XLA Ops:
  7.2 60.2 %all-gather.5.cloned.1.call-start = ((), (), s32[]{:S(2)}) async-start(), calls=%async_computation.2 | async-start | bytes 5849088 | tf_op jit(solution)/shard_map/all_gather | solution.py:179
  10.2 166.3 %all-gather.9.cloned.1.call-start = ((), (), s32[]{:S(2)}) async-start(), calls=%async_computation.4 | async-start | bytes 14622720 | tf_op jit(solution)/shard_map/all_gather | solution.py:188
  11.3 307.2 %all-gather.7.cloned.1.call-start = ((), (), s32[]{:S(2)}) async-start(), calls=%async_computation.3 | async-start | bytes 29245440 | tf_op jit(solution)/shard_map/all_gather | solution.py:187
  14.8 668.2 %all-gather.11.cloned.1.call-start = ((), (), s32[]{:S(2)}) async-start(), calls=%async_computation.5 | async-start | bytes 2924544 | tf_op jit(solution)/shard_map/all_gather | solution.py:318
  86.4 36.1 %collective-permute-start = (bf16[512,1536]{1,0:T(8,128)(2,1)}, bf16[512,1536]{1,0:T(8,128)(2,1)}, u32[]{:S(2)}, u32[]{:S(2)}) collective-permute-start(bf16[512,1536]{1,0:T(8,128)(2,1)} %convolution_convert_fusion.8), channel_id=1, source_target_pairs={{0,1},{1,0},{2,3},{3,2},{4,5},{5,4},{6,7},{7,6},{8,9},{9,8},{10,11... | collective-permute-start | bytes 4718600 | tf_op jit(solution)/shard_map/ppermute | solution.py:102
  377.4 36.0 %collective-permute-start.2 = (bf16[512,1536]{1,0:T(8,128)(2,1)}, bf16[512,1536]{1,0:T(8,128)(2,1)}, u32[]{:S(2)}, u32[]{:S(2)}) collective-permute-start(bf16[512,1536]{1,0:T(8,128)(2,1)} %fusion.63), channel_id=1, source_target_pairs={{0,1},{1,0},{2,3},{3,2},{4,5},{5,4},{6,7},{7,6},{8,9},{9,8},{10,11... | collective-permute-start | bytes 4718600 | tf_op jit(solution)/shard_map/ppermute | solution.py:102
  388.9 58.3 %collective-permute-start.1 = (bf16[512,1536]{1,0:T(8,128)(2,1)}, bf16[512,1536]{1,0:T(8,128)(2,1)}, u32[]{:S(2)}, u32[]{:S(2)}) collective-permute-start(bf16[512,1536]{1,0:T(8,128)(2,1)} %convolution_convert_fusion.6), channel_id=1, source_target_pairs={{0,1},{1,0},{2,3},{3,2},{4,5},{5,4},{6,7},{7,6},{8,9},{9,8},{10,11... | collective-permute-start | bytes 4718600 | tf_op jit(solution)/shard_map/ppermute | solution.py:102
  500.1 136.1 %collective-permute-start.24 = (bf16[768,4480]{1,0:T(8,128)(2,1)}, bf16[768,4480]{1,0:T(8,128)(2,1)}, u32[]{:S(2)}, u32[]{:S(2)}) collective-permute-start(bf16[768,4480]{1,0:T(8,128)(2,1)} %convolution_convert_fusion), channel_id=1, source_target_pairs={{0,2},{2,0},{4,6},{6,4},{8,10},{10,8},{12,14},{14,12},{16,18},{18,... | collective-permute-start | bytes 20643848 | tf_op jit(solution)/shard_map/ppermute | solution.py:102
  509.0 36.1 %collective-permute-start.3 = (bf16[512,1536]{1,0:T(8,128)(2,1)S(1)}, bf16[512,1536]{1,0:T(8,128)(2,1)S(1)}, u32[]{:S(2)}, u32[]{:S(2)}) collective-permute-start(bf16[512,1536]{1,0:T(8,128)(2,1)S(1)} %convolution_convert_fusion.7), channel_id=1, source_target_pairs={{0,1},{1,0},{2,3},{3,2},{4,5},{5,4},{6,7},{7,6},{8,9},{9,8},{10,11... | collective-permute-start | bytes 4718600 | tf_op jit(solution)/shard_map/ppermute | solution.py:102
  522.8 123.2 %collective-permute-start.16 = (bf16[768,4480]{1,0:T(8,128)(2,1)}, bf16[768,4480]{1,0:T(8,128)(2,1)}, u32[]{:S(2)}, u32[]{:S(2)}) collective-permute-start(bf16[768,4480]{1,0:T(8,128)(2,1)} %convolution_convert_fusion.4), channel_id=1, source_target_pairs={{0,2},{2,0},{4,6},{6,4},{8,10},{10,8},{12,14},{14,12},{16,18},{18,... | collective-permute-start | bytes 20643848 | tf_op jit(solution)/shard_map/ppermute | solution.py:102
  569.3 83.1 %collective-permute-start.20 = (bf16[768,4480]{1,0:T(8,128)(2,1)}, bf16[768,4480]{1,0:T(8,128)(2,1)}, u32[]{:S(2)}, u32[]{:S(2)}) collective-permute-start(bf16[768,4480]{1,0:T(8,128)(2,1)} %convolution_convert_fusion.2), channel_id=1, source_target_pairs={{0,2},{2,0},{4,6},{6,4},{8,10},{10,8},{12,14},{14,12},{16,18},{18,... | collective-permute-start | bytes 20643848 | tf_op jit(solution)/shard_map/ppermute | solution.py:102
  576.3 37.7 %collective-permute-start.13 = (bf16[384,768]{1,0:T(8,128)(2,1)S(1)}, bf16[384,768]{1,0:T(8,128)(2,1)S(1)}, u32[]{:S(2)}, u32[]{:S(2)}) collective-permute-start(bf16[384,768]{1,0:T(8,128)(2,1)S(1)} %get-tuple-element.133), channel_id=1, source_target_pairs={{0,8},{2,10},{4,12},{6,14},{8,0},{10,2},{12,4},{14,6},{16,24},{18,... | collective-permute-start | bytes 1769480 | tf_op jit(solution)/shard_map/ppermute | solution.py:102
  593.3 22.9 %collective-permute-start.10 = (bf16[192,1024]{1,0:T(8,128)(2,1)S(1)}, bf16[192,1024]{1,0:T(8,128)(2,1)S(1)}, u32[]{:S(2)}, u32[]{:S(2)}) collective-permute-start(bf16[192,1024]{1,0:T(8,128)(2,1)S(1)} %get-tuple-element.152), channel_id=1, source_target_pairs={{0,16},{2,18},{4,20},{6,22},{8,24},{10,26},{12,28},{14,30},{16,0},... | collective-permute-start | bytes 1179656 | tf_op jit(solution)/shard_map/ppermute | solution.py:102
  644.4 82.4 %collective-permute-start.25 = (bf16[384,4480]{1,0:T(8,128)(2,1)}, bf16[384,4480]{1,0:T(8,128)(2,1)}, u32[]{:S(2)}, u32[]{:S(2)}) collective-permute-start(bf16[384,4480]{1,0:T(8,128)(2,1)} %get-tuple-element.113), channel_id=1, source_target_pairs={{0,4},{2,6},{4,0},{6,2},{8,12},{10,14},{12,8},{14,10},{16,20},{18,... | collective-permute-start | bytes 10321928 | tf_op jit(solution)/shard_map/ppermute | solution.py:102
  651.7 148.8 %collective-permute-start.17 = (bf16[384,4480]{1,0:T(8,128)(2,1)}, bf16[384,4480]{1,0:T(8,128)(2,1)}, u32[]{:S(2)}, u32[]{:S(2)}) collective-permute-start(bf16[384,4480]{1,0:T(8,128)(2,1)} %get-tuple-element.115), channel_id=1, source_target_pairs={{0,4},{2,6},{4,0},{6,2},{8,12},{10,14},{12,8},{14,10},{16,20},{18,... | collective-permute-start | bytes 10321928 | tf_op jit(solution)/shard_map/ppermute | solution.py:102
  657.9 216.3 %collective-permute-start.21 = (bf16[384,4480]{1,0:T(8,128)(2,1)}, bf16[384,4480]{1,0:T(8,128)(2,1)}, u32[]{:S(2)}, u32[]{:S(2)}) collective-permute-start(bf16[384,4480]{1,0:T(8,128)(2,1)} %get-tuple-element.117), channel_id=1, source_target_pairs={{0,4},{2,6},{4,0},{6,2},{8,12},{10,14},{12,8},{14,10},{16,20},{18,... | collective-permute-start | bytes 10321928 | tf_op jit(solution)/shard_map/ppermute | solution.py:102
  729.7 147.3 %collective-permute-start.26 = (bf16[192,4480]{1,0:T(8,128)(2,1)S(1)}, bf16[192,4480]{1,0:T(8,128)(2,1)S(1)}, u32[]{:S(2)}, u32[]{:S(2)}) collective-permute-start(bf16[192,4480]{1,0:T(8,128)(2,1)S(1)} %get-tuple-element.119), channel_id=1, source_target_pairs={{0,8},{2,10},{4,12},{6,14},{8,0},{10,2},{12,4},{14,6},{16,24},{18,... | collective-permute-start | bytes 5160968 | tf_op jit(solution)/shard_map/ppermute | solution.py:102
  803.3 76.2 %collective-permute-start.18 = (bf16[192,4480]{1,0:T(8,128)(2,1)S(1)}, bf16[192,4480]{1,0:T(8,128)(2,1)S(1)}, u32[]{:S(2)}, u32[]{:S(2)}) collective-permute-start(bf16[192,4480]{1,0:T(8,128)(2,1)S(1)} %get-tuple-element.121), channel_id=1, source_target_pairs={{0,8},{2,10},{4,12},{6,14},{8,0},{10,2},{12,4},{14,6},{16,24},{18,... | collective-permute-start | bytes 5160968 | tf_op jit(solution)/shard_map/ppermute | solution.py:102
  877.0 74.6 %collective-permute-start.22 = (bf16[192,4480]{1,0:T(8,128)(2,1)S(1)}, bf16[192,4480]{1,0:T(8,128)(2,1)S(1)}, u32[]{:S(2)}, u32[]{:S(2)}) collective-permute-start(bf16[192,4480]{1,0:T(8,128)(2,1)S(1)} %get-tuple-element.123), channel_id=1, source_target_pairs={{0,8},{2,10},{4,12},{6,14},{8,0},{10,2},{12,4},{14,6},{16,24},{18,... | collective-permute-start | bytes 5160968 | tf_op jit(solution)/shard_map/ppermute | solution.py:102
  877.3 75.7 %collective-permute-start.27 = (bf16[96,4480]{1,0:T(8,128)(2,1)S(1)}, bf16[96,4480]{1,0:T(8,128)(2,1)S(1)}, u32[]{:S(2)}, u32[]{:S(2)}) collective-permute-start(bf16[96,4480]{1,0:T(8,128)(2,1)S(1)} %add_convert_fusion.23), channel_id=1, source_target_pairs={{0,16},{2,18},{4,20},{6,22},{8,24},{10,26},{12,28},{14,30},{16,0},... | collective-permute-start | bytes 2580488 | tf_op jit(solution)/shard_map/ppermute | solution.py:102
  880.9 77.1 %collective-permute-start.19 = (bf16[96,4480]{1,0:T(8,128)(2,1)}, bf16[96,4480]{1,0:T(8,128)(2,1)}, u32[]{:S(2)}, u32[]{:S(2)}) collective-permute-start(bf16[96,4480]{1,0:T(8,128)(2,1)} %add_convert_fusion.27), channel_id=1, source_target_pairs={{0,16},{2,18},{4,20},{6,22},{8,24},{10,26},{12,28},{14,30},{16,0},... | collective-permute-start | bytes 2580488 | tf_op jit(solution)/shard_map/ppermute | solution.py:102
  952.9 39.7 %collective-permute-start.23 = (bf16[96,4480]{1,0:T(8,128)(2,1)}, bf16[96,4480]{1,0:T(8,128)(2,1)}, u32[]{:S(2)}, u32[]{:S(2)}) collective-permute-start(bf16[96,4480]{1,0:T(8,128)(2,1)} %add_convert_fusion.25), channel_id=1, source_target_pairs={{0,16},{2,18},{4,20},{6,22},{8,24},{10,26},{12,28},{14,30},{16,0},... | collective-permute-start | bytes 2580488 | tf_op jit(solution)/shard_map/ppermute | solution.py:102
  1010.6 66.7 %all-to-all-start = ((bf16[16,96,896]{2,1,0:T(8,128)(2,1)}), bf16[16,96,896]{2,1,0:T(8,128)(2,1)S(1)}, u32[]{:S(2)}, u32[]{:S(2)}) async-start(bf16[16,96,896]{2,1,0:T(8,128)(2,1)} %copy.133), calls=%async_computation | async-start | bytes 5505024 | tf_op jit(solution)/shard_map/all_to_all | solution.py:306
  1204.2 71.1 %all-to-all-start.1 = ((bf16[16,96,896]{2,1,0:T(8,128)(2,1)}), bf16[16,96,896]{2,1,0:T(8,128)(2,1)S(1)}, u32[]{:S(2)}, u32[]{:S(2)}) async-start(bf16[16,96,896]{2,1,0:T(8,128)(2,1)} %bitcast.256), calls=%async_computation.1 | async-start | bytes 5505024 | tf_op jit(solution)/shard_map/all_to_all | solution.py:312
  (108 other events, 2351.5 us)
Sparse Core Ops, SparseCore 0:
  10.9 56.4 all-gather.4
  70.3 106.0 all-gather.8
  178.5 139.8 all-gather.6
  632.7 50.2 all-gather.10

commit v2 on v0

v2 whole, which is shorter than its diff:
```python
import functools

import jax
import jax.numpy as jnp
from jax import lax
from jax.experimental import pallas as pl
from jax.experimental.pallas import tpu as pltpu
from jax.sharding import PartitionSpec as P

HD = 128
FFB = 896
NSI = 5


EPS = 1e-06
THETA = 1000000.0
MOMENTUM = 0.5
LR_MATRIX = 0.2
LR_OUT = 0.8
LR_VECTOR = 0.1
LR_BIAS = 1.0
NS_A = 3.4445
NS_B = -4.775
NS_C = 2.0315
FLOAT = jnp.float32
BFLOAT = jnp.bfloat16


def contract(left, right, left_dim, right_dim):
    return lax.dot_general(
        left, right, (((left_dim,), (right_dim,)), ((), ())), preferred_element_type=FLOAT
    )


def positions_of(block_ids):
    index = jnp.arange(block_ids.shape[0], dtype=jnp.int32)
    change = jnp.concatenate([jnp.ones((1,), dtype=bool), block_ids[1:] != block_ids[:-1]])
    start = lax.cummax(jnp.where(change, index, jnp.zeros_like(index)), axis=0)
    return index - start


def rms_scale(values):
    return lax.rsqrt(jnp.mean(values * values, axis=-1, keepdims=True) + EPS)


def norm_back(grad, values, scale, gain):
    scaled = grad * gain
    return scale * scaled - values * scale * scale * scale * jnp.mean(
        scaled * values, axis=-1, keepdims=True
    )


def solve(width, split, depth, wide, tall, tall_low, gram, poly):
    tile = width // 2
    chunk = depth // 3

    def both(sums):
        if split:
            return sums
        total = sums[0] + sums[1]
        return total, total

    def squares(part):
        return jnp.sum(part[:tile] * part[:tile]), jnp.sum(part[tile:] * part[tile:])

    def rows_of(pair, columns):
        if not split:
            return pair[0]
        at = lax.broadcasted_iota(jnp.int32, (width, columns), 0)
        return jnp.where(at < tile, pair[0], pair[1])

    sums = (jnp.float32(0), jnp.float32(0))
    for at in range(3):
        part = wide[at * chunk : (at + 1) * chunk, :width].T
        tall[:width, at * chunk : (at + 1) * chunk] = part
        found = squares(part)
        sums = (sums[0] + found[0], sums[1] + found[1])
    sums = both(sums)
    inverse = tuple(1.0 / (jnp.sqrt(one) + 1e-07) for one in sums)
    factor = rows_of(inverse, chunk)
    for at in range(3):
        part = tall[:width, at * chunk : (at + 1) * chunk] * factor
        tall[:width, at * chunk : (at + 1) * chunk] = part
        tall_low[:width, at * chunk : (at + 1) * chunk] = part.astype(BFLOAT)
    start = tuple(one * by * by for one, by in zip(sums, inverse))

    def step(turn, sums):
        shifts = tuple(one / (tile if split else width) for one in sums)
        for at in range(2):
            mine = slice(at * tile, (at + 1) * tile)
            product = lax.dot_general(
                tall_low[mine, :],
                tall_low[:width, :],
                (((1,), (1,)), ((), ())),
                preferred_element_type=FLOAT,
            )
            row = lax.broadcasted_iota(jnp.int32, (tile, width), 0) + at * tile
            column = lax.broadcasted_iota(jnp.int32, (tile, width), 1)
            product = jnp.where(row == column, product - shifts[at], product)
            if split:
                product = jnp.where((column < tile) == (at == 0), product, 0.0)
            gram[mine, :width] = product.astype(BFLOAT)
        for at in range(2):
            mine = slice(at * tile, (at + 1) * tile)
            product = jnp.dot(
                gram[mine, :width], gram[:width, :width], preferred_element_type=FLOAT
            )
            linear = NS_B + 2.0 * NS_C * shifts[at]
            poly[mine, :width] = (
                linear * gram[mine, :width].astype(FLOAT) + NS_C * product
            ).astype(BFLOAT)
        factor = rows_of(tuple(NS_A + NS_B * s + NS_C * s * s for s in shifts), chunk)
        sums = (jnp.float32(0), jnp.float32(0))
        for at in range(3):
            span = slice(at * chunk, (at + 1) * chunk)
            part = factor * tall[:width, span] + jnp.dot(
                poly[:width, :width], tall_low[:width, span], preferred_element_type=FLOAT
            )
            tall[:width, span] = part
            tall_low[:width, span] = part.astype(BFLOAT)
            found = squares(part)
            sums = (sums[0] + found[0], sums[1] + found[1])
        return both(sums)

    lax.fori_loop(0, NSI, step, start)
    for at in range(3):
        wide[at * chunk : (at + 1) * chunk, :width] = tall[
            :width, at * chunk : (at + 1) * chunk
        ].T


def muon_kernel(
    devices,
    rows,
    blocks,
    query_width,
    keeper,
    units,
    vectors,
    units_new,
    vectors_sum,
    all_vectors,
    first,
    second,
    first_back,
    second_back,
    wide,
    tall,
    tall_low,
    gram,
    poly,
    here_sem,
    go_sem,
    come_sem,
    back_sem,
    home_sem,
    go_vector,
    come_vector,
):
    me = lax.axis_index("dp")
    depth = devices * rows
    mine = jnp.where(me < keeper, me, me - 1)
    keeps = me == keeper
    holds = jnp.logical_and(me != keeper, mine < blocks)
    key_width = FFB - query_width

    def block_of(device):
        return jnp.where(device < keeper, device, device - 1)

    def owner_of(block):
        return jnp.where(block < keeper, block, block + 1)

    def rows_of(array, unit):
        return array.at[:, pl.ds(pl.multiple_of(unit * FFB, 128), FFB)]

    def remote(source, target, send, receive, device):
        return pltpu.make_async_remote_copy(
            src_ref=source,
            dst_ref=target,
            send_sem=send,
            recv_sem=receive,
            device_id={"dp": device},
            device_id_type=pl.DeviceIdType.MESH,
        )

    def others(body):
        def step(turn, carry):
            body(lax.rem(me + turn, devices))
            return carry

        lax.fori_loop(1, devices, step, 0)

    barrier = pltpu.get_barrier_semaphore()

    def greet(device):
        pl.semaphore_signal(
            barrier, inc=1, device_id={"dp": device}, device_id_type=pl.DeviceIdType.MESH
        )

    others(greet)
    pl.semaphore_wait(barrier, devices - 1)

    def way_in(unit, at, sender, device):
        return remote(
            rows_of(units, unit),
            (first, second)[at].at[sender],
            go_sem.at[device, at],
            come_sem.at[sender, at],
            device,
        )

    def to_owner(device, what):
        @pl.when(device == keeper)
        def _():
            what(way_in(blocks, 0, me, device))
            what(way_in(blocks + 1, 1, me, device))

        @pl.when(jnp.logical_and(device != keeper, block_of(device) < blocks))
        def _():
            what(way_in(block_of(device), 0, me, device))

    def share(sender, device):
        return remote(
            vectors, all_vectors.at[sender], go_vector.at[device], come_vector.at[sender], device
        )

    others(lambda device: to_owner(device, lambda copy: copy.start()))
    others(lambda device: share(me, device).start())

    def own_in(what):
        @pl.when(keeps)
        def _():
            what(pltpu.make_async_copy(rows_of(units, blocks), first.at[me], here_sem.at[0]))
            what(pltpu.make_async_copy(rows_of(units, blocks + 1), second.at[me], here_sem.at[1]))

        @pl.when(holds)
        def _():
            what(pltpu.make_async_copy(rows_of(units, mine), first.at[me], here_sem.at[0]))

    own_in(lambda copy: copy.start())
    own_in(lambda copy: copy.wait())

    def arrived(device):
        @pl.when(jnp.logical_or(keeps, holds))
        def _():
            way_in(0, 0, device, me).wait_recv()

        @pl.when(keeps)
        def _():
            way_in(0, 1, device, me).wait_recv()

    others(arrived)

    def load(buffer, source_at, size, target_at):
        def step(at, carry):
            wide[pl.ds(pl.multiple_of(at * rows, 8), rows), target_at : target_at + size] = buffer[
                at, :, source_at : source_at + size
            ].astype(FLOAT)
            return carry

        lax.fori_loop(0, devices, step, 0)

    def store(buffer, source_at, size, target_at):
        def step(at, carry):
            buffer[at, :, target_at : target_at + size] = wide[
                pl.ds(pl.multiple_of(at * rows, 8), rows), source_at : source_at + size
            ].astype(buffer.dtype)
            return carry

        lax.fori_loop(0, devices, step, 0)

    def way_back(unit, at, device):
        return remote(
            (first_back, second_back)[at].at[device],
            rows_of(units_new, unit),
            back_sem.at[device, at],
            home_sem.at[unit],
            device,
        )

    def own_back(unit, at):
        return pltpu.make_async_copy(
            (first_back, second_back)[at].at[me], rows_of(units_new, unit), here_sem.at[at]
        )

    @pl.when(holds)
    def _():
        load(first, 0, FFB, 0)
        solve(FFB, False, depth, wide, tall, tall_low, gram, poly)
        store(first_back, 0, FFB, 0)
        others(lambda device: way_back(mine, 0, device).start())
        own_back(mine, 0).start()
        own_back(mine, 0).wait()

    @pl.when(keeps)
    def _():
        load(first, query_width, key_width, 0)
        load(second, query_width, key_width, key_width)
        solve(2 * key_width, True, depth, wide, tall, tall_low, gram, poly)
        store(first_back, 0, key_width, query_width)
        store(second_back, key_width, key_width, query_width)
        for at, buffer, back in ((0, first, first_back), (1, second, second_back)):
            load(buffer, 0, query_width, 0)
            solve(query_width, False, depth, wide, tall, tall_low, gram, poly)
            store(back, 0, query_width, 0)
            others(lambda device: way_back(blocks + at, at, device).start())
            own_back(blocks + at, at).start()
        own_back(blocks, 0).wait()
        own_back(blocks + 1, 1).wait()

    own_vectors = pltpu.make_async_copy(vectors, all_vectors.at[me], here_sem.at[2])
    own_vectors.start()
    own_vectors.wait()
    others(lambda device: share(device, me).wait_recv())
    vectors_sum[...] = lax.fori_loop(
        1, devices, lambda at, total: total + all_vectors[at], all_vectors[0]
    )
    others(lambda device: share(me, device).wait_send())

    def home(block, carry):
        @pl.when(owner_of(block) != me)
        def _():
            way_back(block, 0, me).wait_recv()

        return carry

    lax.fori_loop(0, blocks, home, 0)

    @pl.when(jnp.logical_not(keeps))
    def _():
        way_back(blocks, 0, me).wait_recv()
        way_back(blocks + 1, 1, me).wait_recv()

    others(lambda device: to_owner(device, lambda copy: copy.wait_send()))

    @pl.when(jnp.logical_or(keeps, holds))
    def _():
        others(lambda device: way_back(0, 0, device).wait_send())

    @pl.when(keeps)
    def _():
        others(lambda device: way_back(0, 1, device).wait_send())


def orthogonalize(units, vectors, query_width, devices):
    rows = units.shape[0]
    blocks = units.shape[1] // FFB - 2
    depth = devices * rows
    wire = units.dtype
    kernel = functools.partial(
        muon_kernel, devices, rows, blocks, query_width, min(devices // 2, blocks)
    )
    hbm = pl.BlockSpec(memory_space=pltpu.HBM)
    return pl.pallas_call(
        kernel,
        out_shape=[
            jax.ShapeDtypeStruct(units.shape, wire),
            jax.ShapeDtypeStruct(vectors.shape, FLOAT),
        ],
        in_specs=[hbm, pl.BlockSpec(memory_space=pltpu.VMEM)],
        out_specs=[hbm, pl.BlockSpec(memory_space=pltpu.VMEM)],
        scratch_shapes=[
            pltpu.VMEM((devices,) + vectors.shape, FLOAT),
            pltpu.VMEM((devices, rows, FFB), wire),
            pltpu.VMEM((devices, rows, FFB), wire),
            pltpu.VMEM((devices, rows, FFB), wire),
            pltpu.VMEM((devices, rows, FFB), wire),
            pltpu.VMEM((depth, FFB), FLOAT),
            pltpu.VMEM((FFB, depth), FLOAT),
            pltpu.VMEM((FFB, depth), BFLOAT),
            pltpu.VMEM((FFB, FFB), BFLOAT),
            pltpu.VMEM((FFB, FFB), BFLOAT),
            pltpu.SemaphoreType.DMA((3,)),
            pltpu.SemaphoreType.DMA((devices, 2)),
            pltpu.SemaphoreType.DMA((devices, 2)),
            pltpu.SemaphoreType.DMA((devices, 2)),
            pltpu.SemaphoreType.DMA((blocks + 2,)),
            pltpu.SemaphoreType.DMA((devices,)),
            pltpu.SemaphoreType.DMA((devices,)),
        ],
        compiler_params=pltpu.CompilerParams(
            collective_id=0, has_side_effects=True, vmem_limit_bytes=52 * 2**20
        ),
        cost_estimate=pl.CostEstimate(
            flops=64 * 10**9, bytes_accessed=16 * 2**20, transcendentals=0
        ),
    )(units, vectors)


LIGHT = pl.CostEstimate(flops=1024, bytes_accessed=1024, transcendentals=0)


def call_light(body, grid, ins, outs):
    return pl.pallas_call(
        body,
        grid=grid,
        in_specs=[pl.BlockSpec(block, at) for _, block, at in ins],
        out_specs=[pl.BlockSpec(block, at) for _, _, block, at in outs],
        out_shape=[jax.ShapeDtypeStruct(shape, dtype) for shape, dtype, _, _ in outs],
        compiler_params=pltpu.CompilerParams(vmem_limit_bytes=56 * 2**20),
        cost_estimate=LIGHT,
    )(*[array for array, _, _ in ins])


def spans(size, step):
    return [slice(at, min(at + step, size)) for at in range(0, size, step)]


def hidden_units(tokens, grads, weights, block=256):
    count, depth = tokens.shape
    part = weights.shape[1] // 3

    def body(x, y, w_gate, w_up, gate, up, hid, turned_x, turned_y):
        turned_x[...] = x[...].astype(FLOAT).T.astype(BFLOAT)
        turned_y[...] = y[...].astype(FLOAT).T.astype(BFLOAT)
        for span in spans(part, 512):
            g = jnp.dot(x[...], w_gate[:, span], preferred_element_type=FLOAT)
            u = jnp.dot(x[...], w_up[:, span], preferred_element_type=FLOAT)
            gate[:, span] = g
            up[:, span] = u
            hid[:, span] = (g * jax.nn.sigmoid(g) * u).astype(BFLOAT)

    rows = lambda at: (at, 0)
    columns = lambda at: (0, at)
    return call_light(
        body,
        (count // block,),
        [
            (tokens, (block, depth), rows),
            (grads, (block, depth), rows),
            (weights, (depth, part), lambda at: (0, 0)),
            (weights, (depth, part), lambda at: (0, 1)),
        ],
        [
            ((count, part), FLOAT, (block, part), rows),
            ((count, part), FLOAT, (block, part), rows),
            ((count, part), BFLOAT, (block, part), rows),
            ((depth, count), BFLOAT, (depth, block), columns),
            ((depth, count), BFLOAT, (depth, block), columns),
        ],
    )


def hidden_back(grads, weights, gate, up, block=256):
    count, depth = grads.shape
    part = weights.shape[1] // 3

    def body(x, w, gate, up, both):
        for span in spans(part, 512):
            dhid = jnp.dot(x[...], w[:, span], preferred_element_type=FLOAT)
            g = gate[:, span]
            sigma = jax.nn.sigmoid(g)
            both[:, span] = (dhid * up[:, span] * sigma * (1.0 + g * (1.0 - sigma))).astype(BFLOAT)
            both[:, part + span.start : part + span.stop] = (dhid * (g * sigma)).astype(BFLOAT)

    rows = lambda at: (at, 0)
    return call_light(
        body,
        (count // block,),
        [
            (grads, (block, depth), rows),
            (weights, (depth, part), lambda at: (0, 2)),
            (gate, (block, part), rows),
            (up, (block, part), rows),
        ],
        [((count, 2 * part), BFLOAT, (block, 2 * part), rows)],
    )[0]


def rows_by_width(units, weights, places, first, last, block=256):
    width = weights.shape[0]
    part = weights.shape[1] // 3

    def body(x, *refs):
        out = refs[-1]
        for span in spans(width, 512):
            out[:, span] = sum(
                lax.dot_general(
                    x[:, at * part : (at + 1) * part],
                    refs[at][span, :],
                    (((1,), (1,)), ((), ())),
                    preferred_element_type=FLOAT,
                )
                for at in range(len(places))
            ).astype(BFLOAT)

    def column(place):
        return (weights, (width, part), lambda at: (0, place))

    return call_light(
        body,
        ((last - first) // block,),
        [(units, (block, len(places) * part), lambda at: (at + first // block, 0))]
        + [column(place) for place in places],
        [((last - first, width), BFLOAT, (block, width), lambda at: (at, 0))],
    )[0]


def weight_term(left, right, blocks, place, width):
    count = left.shape[1]
    picked = blocks.shape[0]
    tall = left.shape[0] // (2 * picked)

    def body(blocks, x, y, out):
        for span in spans(width, 512):
            out[:, span] = jnp.dot(
                x[...], y[:, span], preferred_element_type=FLOAT
            ).astype(BFLOAT)

    return pl.pallas_call(
        body,
        grid_spec=pltpu.PrefetchScalarGridSpec(
            num_scalar_prefetch=1,
            grid=(picked,),
            in_specs=[
                pl.BlockSpec((tall, count), lambda at, blocks: (blocks[at], 0)),
                pl.BlockSpec((count, width), lambda at, blocks: (0, place)),
            ],
            out_specs=pl.BlockSpec((tall, width), lambda at, blocks: (at, 0)),
        ),
        out_shape=jax.ShapeDtypeStruct((picked * tall, width), BFLOAT),
        compiler_params=pltpu.CompilerParams(vmem_limit_bytes=48 * 2**20),
        cost_estimate=LIGHT,
    )(blocks, left, right)


def turned(value, cosine, sine):
    return value * cosine + pltpu.roll(value, HD // 2, 1) * sine


def softmax_of(query, keys, ids, key_ids, first):
    scores = lax.dot_general(
        query, keys, (((1,), (1,)), ((), ())), preferred_element_type=FLOAT
    ) * (HD ** (-0.5))
    row = lax.broadcasted_iota(jnp.int32, scores.shape, 0) + first
    column = lax.broadcasted_iota(jnp.int32, scores.shape, 1)
    scores = jnp.where((ids == key_ids) & (column <= row), scores, -1e30)
    expo = jnp.exp(scores - jnp.max(scores, axis=-1, keepdims=True))
    return expo / jnp.sum(expo, axis=-1, keepdims=True)


def attend(qkv, cosine, sine, doc_ids, heads, kv_heads):
    count = qkv.shape[0]
    share = heads // kv_heads
    half = count // 2

    def body(q, k, v, cosine, sine, ids, key_ids, attn, query, keys, values):
        query[...] = turned(q[...], cosine[...], sine[...]).astype(BFLOAT)
        keys[...] = turned(k[...], cosine[...], sine[...]).astype(BFLOAT)
        values[...] = v[...].astype(BFLOAT)
        for first in (0, half):
            last = first + half
            probs = softmax_of(
                query[first:last, :], keys[:last, :], ids[first:last, :], key_ids[:, :last], first
            )
            attn[first:last, :] = jnp.dot(
                probs.astype(BFLOAT), values[:last, :], preferred_element_type=FLOAT
            ).astype(BFLOAT)

    one = lambda at: (0, 0)
    head = lambda at: (0, at)
    group = lambda at: (0, at // share)
    block = (count, HD)
    return pl.pallas_call(
        body,
        grid=(heads,),
        in_specs=[
            pl.BlockSpec(block, head),
            pl.BlockSpec(block, lambda at: (0, heads + at // share)),
            pl.BlockSpec(block, lambda at: (0, heads + kv_heads + at // share)),
            pl.BlockSpec(block, one),
            pl.BlockSpec(block, one),
            pl.BlockSpec((count, 1), one),
            pl.BlockSpec((1, count), one),
        ],
        out_specs=[
            pl.BlockSpec(block, head),
            pl.BlockSpec(block, head),
            pl.BlockSpec(block, group),
            pl.BlockSpec(block, group),
        ],
        out_shape=[
            jax.ShapeDtypeStruct((count, heads * HD), BFLOAT),
            jax.ShapeDtypeStruct((count, heads * HD), BFLOAT),
            jax.ShapeDtypeStruct((count, kv_heads * HD), BFLOAT),
            jax.ShapeDtypeStruct((count, kv_heads * HD), BFLOAT),
        ],
        compiler_params=pltpu.CompilerParams(vmem_limit_bytes=32 * 2**20),
        cost_estimate=LIGHT,
    )(qkv, qkv, qkv, cosine, sine, doc_ids[:, None], doc_ids[None, :])


def forward_kernel(
    devices,
    heads,
    kv_heads,
    tokens,
    gains,
    bias,
    cosine,
    sine,
    ids,
    key_ids,
    shard,
    units,
    grads,
    normed,
    hidden,
    attn,
    query,
    keys,
    values,
    attention_out,
    ffn_full,
    tokens_all,
    grads_all,
    attention_full,
    qkv,
    branch,
    branch_came,
    normed_two,
    here_sem,
    z_send,
    z_come,
    x_send,
    x_come,
    core_send,
    core_come,
    group_send,
    group_come,
    right_send,
    left_send,
    plane_come,
    pair_send,
    pair_come,
):
    me = lax.axis_index("dp")
    side = lax.axis_index("tensor")
    planes = devices // 4
    rows = shard.shape[0]
    count = tokens.shape[0]
    place, plane = lax.rem(me, 4), me // 4
    across = me + 2 - 4 * (place // 2)
    beside = me + 1 - 2 * lax.rem(me, 2)
    part = ffn_full.shape[1] // 3
    share = heads // kv_heads
    depth = tokens.shape[1]
    half = count // 2

    def remote(source, target, send, come, device):
        return pltpu.make_async_remote_copy(
            src_ref=source,
            dst_ref=target,
            send_sem=send,
            recv_sem=come,
            device_id={"dp": device},
            device_id_type=pl.DeviceIdType.MESH,
        )

    def loop(first, last, body):
        def step(turn, carry):
            body(turn)
            return carry

        lax.fori_loop(first, last, step, 0)

    barrier = pltpu.get_barrier_semaphore()

    def greet(where):
        pl.semaphore_signal(barrier, inc=1, device_id=where, device_id_type=pl.DeviceIdType.MESH)

    def peer(turn):
        return lax.rem(plane + turn, planes) * 4 + place

    def plane_peer(turn):
        return plane * 4 + lax.rem(place + turn, 4)

    loop(1, planes, lambda turn: greet({"dp": peer(turn)}))
    loop(1, 4, lambda turn: greet({"dp": plane_peer(turn)}))
    greet({"tensor": 1 - side})
    pl.semaphore_wait(barrier, planes + 3)

    def block(owner):
        return attention_full.at[pl.ds(pl.multiple_of(owner * rows, 16), rows)]

    def owner_at(turn):
        return lax.rem(plane + planes - turn, planes) * 4

    def to_column(turn):
        return remote(shard, block(me), z_send.at[turn], z_come.at[turn], peer(turn))

    def from_column(turn):
        owner = owner_at(turn) + place
        return remote(block(owner), block(owner), z_send.at[turn], z_come.at[turn], me)

    def x_copy(turn):
        owner = owner_at(turn) + place
        return remote(block(owner), block(owner), x_send.at[turn], x_come.at[turn], across)

    def x_wait(turn):
        owner = owner_at(turn) + lax.rem(across, 4)
        return remote(block(owner), block(owner), x_send.at[turn], x_come.at[turn], across)

    def core_copy(turn, far):
        owner = owner_at(turn) + (lax.rem(across, 4) if far else place)
        return remote(
            block(owner), block(owner), core_send.at[turn, far], core_come.at[turn, far], beside
        )

    def core_wait(turn, far):
        owner = owner_at(turn) + lax.rem(beside, 4) + (2 - 4 * (place // 2) if far else 0)
        return remote(
            block(owner), block(owner), core_send.at[turn, far], core_come.at[turn, far], beside
        )

    def unit_rows(owner):
        return ffn_full.at[pl.ds(pl.multiple_of(owner * rows, 16), rows)]

    def group_copy(turn):
        return remote(
            units.at[lax.rem(place + turn, 4)],
            unit_rows(me),
            group_send.at[turn],
            group_come.at[turn],
            plane_peer(turn),
        )

    def group_wait(turn):
        owner = plane * 4 + lax.rem(place + 4 - turn, 4)
        return remote(
            units.at[0], unit_rows(owner), group_send.at[turn], group_come.at[turn], me
        )

    def slab(origin, third):
        return ffn_full.at[
            pl.ds(pl.multiple_of(origin * 4 * rows, 16), 4 * rows), third * part : (third + 1) * part
        ]

    def move(origin, third, right):
        send = right_send if right else left_send
        return remote(
            slab(origin, third),
            slab(origin, third),
            send.at[origin, third],
            plane_come.at[origin, third],
            me + 4 if right else me - 4,
        )

    def pump(hop, third):
        behind, ahead = plane - hop, plane + hop

        @pl.when(behind >= 0)
        def _():
            move(behind, third, True).wait_recv()

            @pl.when(plane < planes - 1)
            def _():
                move(behind, third, True).start()

        @pl.when(ahead < planes)
        def _():
            move(ahead, third, False).wait_recv()

            @pl.when(plane > 0)
            def _():
                move(ahead, third, False).start()

    def x_rows(array, at):
        return remote(
            array.at[0:count], array.at[count : 2 * count], pair_send.at[at], pair_come.at[at], across
        )

    def core_rows(array, at):
        return remote(
            array.at[0 : 2 * count],
            array.at[2 * count : 4 * count],
            pair_send.at[at],
            pair_come.at[at],
            beside,
        )

    loop(1, planes, lambda turn: to_column(turn).start())
    own_block = pltpu.make_async_copy(shard, block(me), here_sem.at[0])
    own_block.start()
    loop(1, 4, lambda turn: group_copy(turn).start())
    own_units = pltpu.make_async_copy(units.at[place], unit_rows(me), here_sem.at[1])
    own_units.start()
    own_grads = pltpu.make_async_copy(grads, grads_all.at[0:count], here_sem.at[2])
    own_grads.start()

    def norm(value, gain):
        scale = lax.rsqrt(jnp.mean(value * value, axis=-1, keepdims=True) + EPS)
        return (value * scale * gain).astype(BFLOAT)

    for first in range(0, count, 128):
        normed[first : first + 128, :] = norm(
            tokens[first : first + 128, :].astype(FLOAT), gains[0:1, :]
        )

    own_block.wait()
    x_copy(0).start()
    core_copy(0, 0).start()

    def forward(turn):
        from_column(turn).wait_recv()
        x_copy(turn).start()
        core_copy(turn, 0).start()

    loop(1, planes, forward)
    own_units.wait()
    loop(1, 4, lambda turn: group_wait(turn).wait_recv())
    for third in range(3):

        @pl.when(plane < planes - 1)
        def _():
            move(plane, third, True).start()

        @pl.when(plane > 0)
        def _():
            move(plane, third, False).start()

    own_grads.wait()
    x_rows(grads_all, 0).start()

    def forward_far(turn):
        x_wait(turn).wait_recv()
        core_copy(turn, 1).start()

    loop(0, planes, forward_far)
    pump(1, 0)

    def arrive(turn):
        core_wait(turn, 0).wait_recv()
        core_wait(turn, 1).wait_recv()

    loop(0, planes, arrive)
    attention_copy = pltpu.make_async_copy(attention_full, attention_out, here_sem.at[0])
    attention_copy.start()

    query_width = heads * HD
    group_width = qkv.shape[1]
    for first in range(0, group_width, 256):
        qkv[:, first : first + 256] = (
            jnp.dot(
                normed[...], attention_full[:, first : first + 256], preferred_element_type=FLOAT
            )
            + bias[:, first : first + 256]
        )

    def columns(at):
        return pl.ds(pl.multiple_of(at * HD, HD), HD)

    def key_head(at):
        keys[:, columns(at)] = turned(
            qkv[:, columns(heads + at)], cosine[...], sine[...]
        ).astype(BFLOAT)
        values[:, columns(at)] = qkv[:, columns(heads + kv_heads + at)].astype(BFLOAT)

    loop(0, kv_heads, key_head)

    def head(at):
        query[:, columns(at)] = turned(qkv[:, columns(at)], cosine[...], sine[...]).astype(BFLOAT)
        group = columns(at // share)
        for first in (0, half):
            last = first + half
            probs = softmax_of(
                query[first:last, columns(at)],
                keys[:last, group],
                ids[first:last, :],
                key_ids[:, :last],
                first,
            )
            attn[first:last, columns(at)] = jnp.dot(
                probs.astype(BFLOAT), values[:last, group], preferred_element_type=FLOAT
            ).astype(BFLOAT)

    loop(0, heads, head)
    for first in range(0, depth, 256):
        branch[:, first : first + 256] = lax.dot_general(
            attn[...],
            attention_full[first : first + 256, group_width:],
            (((1,), (1,)), ((), ())),
            preferred_element_type=FLOAT,
        ).astype(BFLOAT)
    sum_copy = pltpu.make_async_remote_copy(
        src_ref=branch,
        dst_ref=branch_came,
        send_sem=here_sem.at[3],
        recv_sem=here_sem.at[4],
        device_id={"tensor": 1 - side},
        device_id_type=pl.DeviceIdType.MESH,
    )
    sum_copy.start()
    pump(1, 1)
    pump(1, 2)
    x_rows(grads_all, 0).wait()
    core_rows(grads_all, 1).start()
    pump(2, 0)
    sum_copy.wait()
    for first in range(0, count, 128):
        span = slice(first, first + 128)
        value = tokens[span, :].astype(FLOAT) + (
            branch[span, :].astype(FLOAT) + branch_came[span, :].astype(FLOAT)
        )
        hidden[span, :] = value
        normed_two[span, :] = norm(value, gains[1:2, :])
    own_tokens = pltpu.make_async_copy(normed_two, tokens_all.at[0:count], here_sem.at[1])
    own_tokens.start()
    own_tokens.wait()
    x_rows(tokens_all, 2).start()
    pump(2, 1)
    pump(2, 2)
    x_rows(tokens_all, 2).wait()
    core_rows(tokens_all, 3).start()
    for hop in range(3, planes):
        for third in range(3):
            pump(hop, third)
    core_rows(grads_all, 1).wait()
    core_rows(tokens_all, 3).wait()
    attention_copy.wait()

    loop(1, planes, lambda turn: to_column(turn).wait_send())

    def sent(turn):
        x_copy(turn).wait_send()
        core_copy(turn, 0).wait_send()
        core_copy(turn, 1).wait_send()

    loop(0, planes, sent)
    loop(1, 4, lambda turn: group_copy(turn).wait_send())
    for third in range(3):

        @pl.when(plane < planes - 1)
        def _():
            loop(0, plane + 1, lambda origin: move(origin, third, True).wait_send())

        @pl.when(plane > 0)
        def _():
            loop(plane, planes, lambda origin: move(origin, third, False).wait_send())


def forward_part(
    tokens, gains, bias, cosine, sine, doc_ids, shard, units, grads, devices, heads, kv_heads
):
    count, depth = tokens.shape
    rows, width = shard.shape
    planes = devices // 4
    group_width = bias.shape[0]
    query_width = heads * HD
    hbm = pl.BlockSpec(memory_space=pltpu.HBM)
    vmem = pl.BlockSpec(memory_space=pltpu.VMEM)
    dma = pltpu.SemaphoreType.DMA
    return pl.pallas_call(
        functools.partial(forward_kernel, devices, heads, kv_heads),
        out_shape=[
            jax.ShapeDtypeStruct((count, depth), BFLOAT),
            jax.ShapeDtypeStruct((count, depth), FLOAT),
            jax.ShapeDtypeStruct((count, query_width), BFLOAT),
            jax.ShapeDtypeStruct((count, query_width), BFLOAT),
            jax.ShapeDtypeStruct((count, kv_heads * HD), BFLOAT),
            jax.ShapeDtypeStruct((count, kv_heads * HD), BFLOAT),
            jax.ShapeDtypeStruct((devices * rows, width), BFLOAT),
            jax.ShapeDtypeStruct((devices * rows, units.shape[2]), BFLOAT),
            jax.ShapeDtypeStruct((4 * count, depth), BFLOAT),
            jax.ShapeDtypeStruct((4 * count, depth), BFLOAT),
        ],
        in_specs=[vmem] * 7 + [hbm] * 3,
        out_specs=[vmem] * 6 + [hbm] * 4,
        scratch_shapes=[
            pltpu.VMEM((devices * rows, width), BFLOAT),
            pltpu.VMEM((count, group_width), FLOAT),
            pltpu.VMEM((count, depth), BFLOAT),
            pltpu.VMEM((count, depth), BFLOAT),
            pltpu.VMEM((count, depth), BFLOAT),
            dma((5,)),
            dma((planes,)),
            dma((planes,)),
            dma((planes,)),
            dma((planes,)),
            dma((planes, 2)),
            dma((planes, 2)),
            dma((4,)),
            dma((4,)),
            dma((planes, 3)),
            dma((planes, 3)),
            dma((planes, 3)),
            dma((4,)),
            dma((4,)),
        ],
        compiler_params=pltpu.CompilerParams(
            collective_id=1, has_side_effects=True, vmem_limit_bytes=48 * 2**20
        ),
        cost_estimate=LIGHT,
    )(
        tokens,
        gains,
        bias[None, :],
        cosine,
        sine,
        doc_ids[:, None],
        doc_ids[None, :],
        shard,
        units,
        grads,
    )


def backward_part(
    back,
    came,
    hidden,
    cotangent,
    live,
    gain,
    weights,
    normed,
    attn,
    query,
    keys,
    values,
    cosine,
    sine,
    doc_ids,
    devices,
    order,
):
    count, depth = hidden.shape
    rows = depth // devices
    heads, kv_heads = query.shape[1] // HD, keys.shape[1] // HD
    share = heads // kv_heads
    query_width = heads * HD
    group_width = (heads + 2 * kv_heads) * HD
    width = weights.shape[1]
    half = count // 2
    scale = HD ** (-0.5)

    def body(
        back,
        came,
        hidden,
        cotangent,
        live,
        gain,
        weights,
        normed,
        attn,
        query,
        keys,
        values,
        cosine,
        sine,
        ids,
        key_ids,
        dhidden,
        gain_term,
        bias_term,
        dnormed,
        near,
        far,
        dbranch,
        dattn,
        dqkv,
        dkeys,
        dvalues,
        term,
    ):
        total = jnp.zeros((1, depth), FLOAT)
        for first in range(0, count, 128):
            span = slice(first, first + 128)
            grad = back[span, :].astype(FLOAT) + came[span, :].astype(FLOAT)
            value = hidden[span, :]
            root = lax.rsqrt(jnp.mean(value * value, axis=-1, keepdims=True) + EPS)
            scaled = grad * gain[...]
            result = cotangent[span, :].astype(FLOAT) * live[span, :] + (
                root * scaled
                - value * root * root * root * jnp.mean(scaled * value, axis=-1, keepdims=True)
            )
            dhidden[span, :] = result
            dbranch[span, :] = result.astype(BFLOAT)
            total = total + jnp.sum(grad * value * root, axis=0, keepdims=True)
        gain_term[...] = total
        for first in range(0, query_width, 256):
            dattn[:, first : first + 256] = jnp.dot(
                dbranch[...],
                weights[:, group_width + first : group_width + first + 256],
                preferred_element_type=FLOAT,
            ).astype(BFLOAT)

        def columns(at):
            return pl.ds(pl.multiple_of(at * HD, HD), HD)

        def one_head(at, carry):
            group = at // share

            @pl.when(lax.rem(at, share) == 0)
            def _():
                dkeys[...] = jnp.zeros_like(dkeys)
                dvalues[...] = jnp.zeros_like(dvalues)

            for first in (0, half):
                last = first + half
                rows_here = slice(first, last)
                probs = softmax_of(
                    query[rows_here, columns(at)],
                    keys[:last, columns(group)],
                    ids[rows_here, :],
                    key_ids[:, :last],
                    first,
                )
                dprobs = lax.dot_general(
                    dattn[rows_here, columns(at)],
                    values[:last, columns(group)],
                    (((1,), (1,)), ((), ())),
                    preferred_element_type=FLOAT,
                )
                dscores = (
                    probs * (dprobs - jnp.sum(probs * dprobs, axis=-1, keepdims=True))
                ).astype(BFLOAT)
                dquery = scale * jnp.dot(
                    dscores, keys[:last, columns(group)], preferred_element_type=FLOAT
                )
                dqkv[rows_here, columns(at)] = turned(
                    dquery, cosine[rows_here, :], -sine[rows_here, :]
                ).astype(BFLOAT)
                dkeys[:last, :] += lax.dot_general(
                    dscores,
                    query[rows_here, columns(at)],
                    (((0,), (0,)), ((), ())),
                    preferred_element_type=FLOAT,
                )
                dvalues[:last, :] += lax.dot_general(
                    probs.astype(BFLOAT),
                    dattn[rows_here, columns(at)],
                    (((0,), (0,)), ((), ())),
                    preferred_element_type=FLOAT,
                )

            @pl.when(lax.rem(at, share) == share - 1)
            def _():
                dqkv[:, columns(heads + group)] = turned(
                    dkeys[...] * scale, cosine[...], -sine[...]
                ).astype(BFLOAT)
                dqkv[:, columns(heads + kv_heads + group)] = dvalues[...].astype(BFLOAT)

            return carry

        lax.fori_loop(0, heads, one_head, 0)
        bias_term[...] = jnp.sum(dqkv[...].astype(FLOAT), axis=0, keepdims=True)
        for first in range(0, depth, 256):
            span = slice(first, first + 256)
            dnormed[:, span] = lax.dot_general(
                dqkv[...],
                weights[span, :group_width],
                (((1,), (1,)), ((), ())),
                preferred_element_type=FLOAT,
            ).astype(BFLOAT)
            term[span, :group_width] = lax.dot_general(
                normed[:, span], dqkv[...], (((0,), (0,)), ((), ())), preferred_element_type=FLOAT
            )
            term[span, group_width:] = lax.dot_general(
                dbranch[:, span], attn[...], (((0,), (0,)), ((), ())), preferred_element_type=FLOAT
            )
        me = lax.axis_index("dp")
        for place in range(devices):
            block = 0
            for at, stride in enumerate(order):
                bit = (place >> (len(order) - 1 - at)) & 1
                block = block + lax.rem(me // stride + bit, 2) * stride
            target = near if place < devices // 2 else far
            target[place % (devices // 2)] = term[
                pl.ds(pl.multiple_of(block * rows, 8), rows), :
            ].astype(BFLOAT)

    vmem = pl.BlockSpec(memory_space=pltpu.VMEM)
    outs = pl.pallas_call(
        body,
        out_shape=[
            jax.ShapeDtypeStruct((count, depth), FLOAT),
            jax.ShapeDtypeStruct((1, depth), FLOAT),
            jax.ShapeDtypeStruct((1, group_width), FLOAT),
            jax.ShapeDtypeStruct((count, depth), BFLOAT),
            jax.ShapeDtypeStruct((devices // 2, rows, width), BFLOAT),
            jax.ShapeDtypeStruct((devices // 2, rows, width), BFLOAT),
        ],
        in_specs=[vmem] * 16,
        out_specs=[vmem] * 6,
        scratch_shapes=[
            pltpu.VMEM((count, depth), BFLOAT),
            pltpu.VMEM((count, query_width), BFLOAT),
            pltpu.VMEM((count, group_width), BFLOAT),
            pltpu.VMEM((count, HD), FLOAT),
            pltpu.VMEM((count, HD), FLOAT),
            pltpu.VMEM((depth, width), FLOAT),
        ],
        compiler_params=pltpu.CompilerParams(vmem_limit_bytes=56 * 2**20),
        cost_estimate=LIGHT,
    )(
        back,
        came,
        hidden,
        cotangent,
        live,
        gain,
        weights,
        normed,
        attn,
        query,
        keys,
        values,
        cosine,
        sine,
        doc_ids[:, None],
        doc_ids[None, :],
    )
    dhidden, gain_term, bias_term, dnormed, near, far = outs
    return (
        dhidden,
        gain_term[0],
        bias_term[0],
        dnormed,
        near.reshape(-1, width),
        far.reshape(-1, width),
    )


def vector_step(param, moment_new, rate):
    return param - rate * moment_new * lax.rsqrt(
        jnp.mean(moment_new * moment_new, axis=-1, keepdims=True) + EPS
    )


def bits_of(count):
    return [1 << bit for bit in range(count.bit_length() - 1)]


def swap(value, axis, stride):
    count = lax.axis_size(axis)
    return lax.ppermute(value, axis, [(at, at ^ stride) for at in range(count)])


def low_add(one, other):
    return (one.astype(FLOAT) + other.astype(FLOAT)).astype(BFLOAT)


def after(value, *others):
    return lax.optimization_barrier((value,) + others)[0]


def by_distance(value, order):
    me = lax.axis_index("dp")
    down = sorted(order, reverse=True)
    bits = len(order)
    value = value.reshape((2,) * bits + (value.shape[0] >> bits,) + value.shape[1:])
    for at, stride in enumerate(down):
        value = jnp.where((me // stride) % 2 == 1, jnp.flip(value, at), value)
    places = [down.index(stride) for stride in order]
    value = value.transpose(tuple(places) + tuple(range(bits, value.ndim)))
    return value.reshape((-1,) + value.shape[bits + 1 :])


def by_index(value, order):
    me = lax.axis_index("dp")
    down = sorted(order, reverse=True)
    bits = len(order)
    value = value.reshape((2,) * bits + (value.shape[0] >> bits,) + value.shape[1:])
    places = [order.index(stride) for stride in down]
    value = value.transpose(tuple(places) + tuple(range(bits, value.ndim)))
    for at, stride in enumerate(down):
        value = jnp.where((me // stride) % 2 == 1, jnp.flip(value, at), value)
    return value.reshape((-1,) + value.shape[bits + 1 :])


def gather_plane(value, strides):
    for stride in reversed(strides):
        value = jnp.concatenate([value, swap(value, "dp", stride)])
    return value


def regroup(value, strides):
    order = tuple(reversed(strides))
    count = value.shape[0]
    value = by_distance(value, order)
    came = [value[:1]] + [swap(value[at : at + 1], "dp", at) for at in range(1, count)]
    return by_distance(jnp.concatenate(came), order)


def halves_by_distance(order):
    me = lax.axis_index("dp")
    down = sorted(order, reverse=True)
    blocks = []
    for place in range(1 << len(order)):
        block = 0
        for at, stride in enumerate(order):
            far = (place >> (len(order) - 1 - at)) & 1
            bit = (me // stride + far) % 2
            block = block + (bit << (len(order) - 1 - down.index(stride)))
        blocks.append(block)
    blocks = jnp.stack(blocks).astype(jnp.int32)
    half = len(order) and (1 << (len(order) - 1))
    return blocks[:half], blocks[half:]


class Chain:
    def __init__(self, kept, sent, order):
        self.kept, self.order = kept, list(order)
        self.send(sent)

    def send(self, sent):
        self.sent = sent
        self.coming = swap(sent, "dp", self.order.pop(0))

    def come(self, *others):
        came = after(self.coming, *others)
        if not self.order:
            self.total = self.kept.astype(FLOAT) + came.astype(FLOAT)
            return self.total
        half = self.kept.shape[0] // 2
        sent = low_add(self.kept[half:], came[half:])
        self.kept = low_add(self.kept[:half], came[:half])
        self.send(sent)
        return sent

    def finish(self, *others):
        while self.order:
            self.come(*others)
            others = ()
        return self.come(*others)


def shards(
    tokens,
    cotangent,
    doc_ids,
    norm_gains,
    qkv_weight,
    qkv_bias,
    out_weight,
    gate_up_weight,
    down_weight,
    gains_moment,
    qkv_moment,
    bias_moment,
    out_moment,
    gate_up_moment,
    down_moment,
):
    rows = qkv_weight.shape[0]
    count = tokens.shape[0]
    query_width = out_weight.shape[1]
    heads = query_width // HD
    group_width = qkv_weight.shape[1]
    kv_heads = (group_width - query_width) // (2 * HD)
    devices = lax.axis_size("dp")
    me = lax.axis_index("dp")
    strides = bits_of(devices)
    every = tuple(strides)
    plane = 4
    near = strides[:2]
    far = tuple(strides[2:])
    units = down_weight.shape[1]
    part = -(-units // (plane * 128)) * 128
    extra = part * plane - units

    def fetch_rows(value, order):
        for stride in reversed(order):
            value = jnp.concatenate([value, swap(value, "dp", stride)])
        return by_index(value, order)

    def split_units(matrix):
        matrix = jnp.pad(matrix, ((0, 0), (0, extra)))
        return matrix.reshape(rows, plane, part).transpose(1, 0, 2)

    def join_units(value):
        value = value.transpose(1, 0, 2).reshape(rows, plane * part)
        return value[:, :units]

    attention_low = jnp.concatenate([qkv_weight.astype(BFLOAT), out_weight.astype(BFLOAT)], axis=1)
    unit_weights = jnp.concatenate(
        [split_units(one.astype(BFLOAT)) for one in (gate_up_weight[0], gate_up_weight[1], down_weight)],
        axis=2,
    )
    live = (doc_ids >= 0).astype(FLOAT)
    grad_out = cotangent.astype(FLOAT) * live[:, None]
    grad_low = grad_out.astype(BFLOAT)
    near_blocks, far_blocks = halves_by_distance(far)
    positions = positions_of(doc_ids)
    freq = THETA ** (-(2.0 / HD) * jnp.arange(HD // 2, dtype=FLOAT))
    angle = positions.astype(FLOAT)[:, None] * freq[None, :]
    cosine = jnp.cos(angle)
    sine = jnp.sin(angle)
    cosine_two = jnp.concatenate([cosine, cosine], axis=1)
    sine_two = jnp.concatenate([-sine, sine], axis=1)
    inputs = tokens.astype(FLOAT)
    scale_one = rms_scale(inputs)
    if rows % 16 == 0:
        (
            normed,
            hidden1,
            attn,
            query,
            keys,
            values,
            attention_full,
            ffn_full,
            normed2_all,
            grad_all,
        ) = forward_part(
            tokens,
            norm_gains,
            qkv_bias,
            cosine_two,
            sine_two,
            doc_ids,
            attention_low,
            unit_weights,
            grad_low,
            devices,
            heads,
            kv_heads,
        )
    else:
        attention_full = fetch_rows(attention_low, every)
        ffn_full = fetch_rows(regroup(unit_weights, near).reshape(plane * rows, -1), far)
        normed = (inputs * scale_one * norm_gains[0]).astype(BFLOAT)
        qkv = contract(normed, attention_full[:, :group_width], 1, 0) + qkv_bias
        attn, query, keys, values = attend(qkv, cosine_two, sine_two, doc_ids, heads, kv_heads)
        branch = contract(attn, attention_full[:, group_width:], 1, 1).astype(BFLOAT)
        hidden1 = inputs + (branch.astype(FLOAT) + swap(branch, "tensor", 1).astype(FLOAT))
        normed2_all = gather_plane(
            (hidden1 * rms_scale(hidden1) * norm_gains[1]).astype(BFLOAT), near
        )
        grad_all = gather_plane(grad_low, near)
    gate, up, hid, normed2_rows, grad_rows = hidden_units(normed2_all, grad_all, ffn_full)
    down_sent = weight_term(grad_rows, hid, far_blocks, 0, part)
    down_kept = weight_term(grad_rows, after(hid, down_sent), near_blocks, 0, part)
    down_chain = Chain(down_kept, down_sent, far)
    both = hidden_back(after(grad_all, down_kept), ffn_full, gate, up)
    gate_sent = weight_term(normed2_rows, both, far_blocks, 0, part)
    up_sent = weight_term(after(normed2_rows, gate_sent), both, far_blocks, 1, part)
    down_sent = down_chain.come(up_sent)
    both = after(both, down_sent)
    half = plane * count // 2
    back_sent = rows_by_width(both, ffn_full, (0, 1), half, 2 * half)
    back_kept = rows_by_width(after(both, back_sent), ffn_full, (0, 1), 0, half)
    back_chain = Chain(back_kept, back_sent, near)
    back_sent = back_chain.come(back_kept)
    gate_kept = weight_term(after(normed2_rows, back_sent), both, near_blocks, 0, part)
    gate_chain = Chain(gate_kept, gate_sent, far)
    gate_sent = gate_chain.come(gate_kept)
    up_kept = weight_term(after(normed2_rows, gate_sent), both, near_blocks, 1, part)
    up_chain = Chain(up_kept, up_sent, far)
    back = back_chain.come(up_kept).astype(BFLOAT)
    back_came = swap(back, "tensor", 1)
    layer_sent = rows_by_width(after(hid, back), ffn_full, (2,), half, 2 * half)
    layer_kept = rows_by_width(after(hid, layer_sent), ffn_full, (2,), 0, half)
    layer_chain = Chain(layer_kept, layer_sent, near)
    layer_sent = layer_chain.come(layer_kept)
    down_total = down_chain.finish(layer_sent)
    up_sent = up_chain.come(down_total)

    def own_rows(value):
        return join_units(regroup(value.astype(BFLOAT).reshape(plane, rows, part), near)).astype(FLOAT)

    down_shard = own_rows(down_total)
    dhidden1, gain_two, bias_term, dnormed, kept, sent = backward_part(
        back,
        after(back_came, up_sent),
        hidden1,
        cotangent,
        live[:, None],
        norm_gains[1:2],
        attention_full,
        normed,
        attn,
        query,
        keys,
        values,
        cosine_two,
        sine_two,
        doc_ids,
        devices,
        every,
    )
    chain = Chain(kept, sent, every)
    dnormed_came = swap(dnormed, "tensor", 1)
    gate_total = gate_chain.finish(dnormed)
    token = chain.come(gate_total)
    gate_shard = own_rows(gate_total)
    layer = layer_chain.come(token).astype(BFLOAT)
    layer_came = swap(layer, "tensor", 1)
    up_total = up_chain.finish(layer)
    token = chain.come(up_total)
    up_shard = own_rows(up_total)
    token = chain.come(token)
    dnormed = dnormed.astype(FLOAT) + after(dnormed_came, token).astype(FLOAT)
    attention_shard = chain.finish(dnormed)
    qkv_shard = attention_shard[:, :group_width]
    out_shard = attention_shard[:, group_width:]
    tokens_grad = dhidden1 + norm_back(dnormed, inputs, scale_one, norm_gains[0])
    gain_one = jnp.sum(dnormed * inputs * scale_one, axis=0)
    gate_up_shard = jnp.stack([gate_shard, up_shard])
    qkv_m = MOMENTUM * qkv_moment + qkv_shard
    out_m = MOMENTUM * out_moment + out_shard
    gate_up_m = MOMENTUM * gate_up_moment + gate_up_shard
    down_m = MOMENTUM * down_moment + down_shard
    wire = BFLOAT if rows % 16 == 0 else FLOAT
    pair = query_width + (group_width - query_width) // 2
    vectors = jnp.concatenate([gain_one, gain_two, bias_term])
    solved, vectors = orthogonalize(
        jnp.concatenate(
            [gate_up_m[0], gate_up_m[1], down_m, qkv_m[:, :pair], out_m, qkv_m[:, pair:]], axis=1
        ).astype(wire),
        vectors.reshape(-1, 128),
        query_width,
        devices,
    )
    vectors = vectors.reshape(-1)
    gains_grad = vectors[: 2 * inputs.shape[1]].reshape(2, -1)
    bias_grad = vectors[2 * inputs.shape[1] :]
    gains_m = MOMENTUM * gains_moment + gains_grad
    bias_m = MOMENTUM * bias_moment + bias_grad
    layer_out = hidden1 + (layer.astype(FLOAT) + after(layer_came, solved).astype(FLOAT))
    gate_up_update = jnp.stack([solved[:, :units], solved[:, units : 2 * units]]).astype(FLOAT)
    down_update = solved[:, 2 * units : 3 * units].astype(FLOAT)
    last = solved[:, 3 * units :].astype(FLOAT)
    qkv_update = jnp.concatenate([last[:, :pair], last[:, pair + query_width :]], axis=1)
    out_update = last[:, pair : pair + query_width]
    gains_new = vector_step(norm_gains, gains_m, LR_VECTOR)
    bias_new = vector_step(qkv_bias, bias_m, LR_BIAS)
    return (
        layer_out,
        tokens_grad,
        gains_grad,
        qkv_shard,
        bias_grad,
        out_shard,
        gate_up_shard,
        down_shard,
        gains_new,
        qkv_weight - LR_MATRIX * qkv_update,
        bias_new,
        out_weight - LR_OUT * out_update,
        gate_up_weight - LR_MATRIX * gate_up_update,
        down_weight - LR_MATRIX * down_update,
        gains_m,
        qkv_m,
        bias_m,
        out_m,
        gate_up_m,
        down_m,
    )


def solution(mesh):
    placed = (
        P("dp", None),
        P("dp", None),
        P("dp"),
        P(),
        P("dp", "tensor"),
        P("tensor"),
        P("dp", "tensor"),
        P(None, "dp", "tensor"),
        P("dp", "tensor"),
        P(),
        P("dp", "tensor"),
        P("tensor"),
        P("dp", "tensor"),
        P(None, "dp", "tensor"),
        P("dp", "tensor"),
    )
    return jax.shard_map(
        shards,
        mesh=mesh,
        in_specs=placed,
        out_specs=(
            P("dp", None),
            P("dp", None),
            P(),
            P("dp", "tensor"),
            P("tensor"),
            P("dp", "tensor"),
            P(None, "dp", "tensor"),
            P("dp", "tensor"),
            P(),
            P("dp", "tensor"),
            P("tensor"),
            P("dp", "tensor"),
            P(None, "dp", "tensor"),
            P("dp", "tensor"),
            P(),
            P("dp", "tensor"),
            P("tensor"),
            P("dp", "tensor"),
            P(None, "dp", "tensor"),
            P("dp", "tensor"),
        ),
        check_vma=False,
    )
```

time: 2520 us -> 834 us (0.33)
  waiting for transfers between devices: 1280 us -> 172 us
  matrix products: 784 us -> 0 us
  Pallas kernels: 0 us -> 539 us
  blocking collectives: 183 us -> 0 us
  local copies, waits for them, and re-layouts: 115 us -> 24 us
  other arithmetic: 124 us -> 68.5 us
    reduce_scatter x4 -> x0, waiting for transfers between devices: 813 us -> none  [the longest x1 506 us: shards(): lax.psum_scatter(jnp.stack([gate_term, up_term]), 'dp', scatter_dimension...]
    dot_general x36 -> x0, matrix products: 784 us -> none  [the longest x5 260 us: newton(): jnp.dot(ortho, polynomial, precision=HIGH, preferred_element_type=FLOAT)]
    pallas_call x0 -> x15, Pallas kernels: none -> 539 us  [the longest x1 206 us: forward_part(): pl.pallas_call(functools.partial(forward_kernel, devices, heads, kv_heads...]
    all_gather x4 -> x0, waiting for transfers between devices: 286 us -> none  [the longest x1 137 us: fetch_ffn(): lax.all_gather(gate_up_weight.astype(BFLOAT), 'dp', axis=1, tiled=True)]
    psum x3 -> x0, waiting for transfers between devices: 176 us -> none  [the longest x1 77.7 us: shards(): lax.psum(contract(hid, down_full, 1, 1).astype(jnp.bfloat16), 'tensor')]
    ppermute x0 -> x26, waiting for transfers between devices: none -> 172 us  [swap(): return lax.ppermute(value, axis, [(at, at ^ stride) for at in range(count)])]
    all_to_all x1 -> x0, blocking collectives: 126 us -> none  [shards(): lax.all_to_all(packed.astype(jnp.bfloat16), 'dp', split_axis=1, concat_ax...]
    psum x1 -> x0, blocking collectives: 57.2 us -> none  [shards(): lax.psum((jnp.stack([gain_one, gain_two]), bias_term), 'dp')]
  transfers between devices with their start and end apart: 12 -> 26, of which waited for: 10 -> 14; matrix products, arithmetic and copies ran while one was open for 9% -> 7% of each run, Pallas kernels for 0% -> 34%
where the time goes in v2:
time: 834 us; the launch traced here: 827 us
  Pallas kernels  539 us (65%)
  waiting for transfers between devices  172 us (21%)
  other arithmetic  68.5 us (8%)
  local copies, waits for them, and re-layouts  24 us (3%)
  starting transfers between devices  20.4 us (2%)
    pallas_call x1, Pallas kernels, forward_part(): pl.pallas_call(functools.partial(forward_kernel, devices, heads, kv_heads...  206 us
    ppermute x26, waiting for transfers between devices, swap(): return lax.ppermute(value, axis, [(at, at ^ stride) for at in range(count)])  172 us
    pallas_call x1, Pallas kernels, orthogonalize(): pl.pallas_call(kernel, out_shape=[jax.ShapeDtypeStruct(units.shape, wire)...  170 us
    pallas_call x6, Pallas kernels, call_light(): pl.pallas_call(body, grid=grid, in_specs=[pl.BlockSpec(block, at) for _,...  86.8 us
    pallas_call x6, Pallas kernels, weight_term(): pl.pallas_call(body, grid_spec=pltpu.PrefetchScalarGridSpec(num_scalar_pr...  48 us
    pallas_call x1, Pallas kernels, backward_part(): pl.pallas_call(body, out_shape=[jax.ShapeDtypeStruct((count, depth), FLOA...  27.3 us
    ppermute x26, starting transfers between devices, swap(): return lax.ppermute(value, axis, [(at, at ^ stride) for at in range(count)])  20.4 us
  transfers between devices with their start and end apart: 26, of which 14 were waited for; matrix products, arithmetic and copies ran while one was open for 7% of the time, Pallas kernels for 34%

profile of v2, /device:TPU:27, one launch (start us, length us, event | category | flops | bytes accessed | tf_op | source)
XLA Modules:
  0.0 826.5 jit_solution(14350599431291260870)
XLA Ops:
  13.9 206.3 %shard_map.302 = (bf16[512,1536]{1,0:T(8,128)(2,1)S(1)}, f32[512,1536]{1,0:T(8,128)}, bf16[512,768]{1,0:T(8,128)(2,1)S(1)}, bf16[512,768]{1,0:T(8,128)(2,1)S(1)}...) custom-call(bf16[512,1536]{1,0:T(8,128)(2,1)S(1)} %copy-done, ...), custom_call_target="tpu_custom_call" | custom-call | flops 1024 | bytes 1024 | tf_op jit(solution)/shard_map/pallas_call | solution.py:953
  224.5 24.7 %shard_map.303 = (f32[2048,1152]{1,0:T(8,128)}, f32[2048,1152]{1,0:T(8,128)}, bf16[2048,1152]{1,0:T(8,128)(2,1)}, bf16[1536,2048]{1,0:T(8,128)(2,1)}, bf16[1536,2048]{1,0:T(8,128)(2,1)}) custom-call(bf16[2048,1536]{1,0:T(8,128)(2,1)} %get-tuple-element.70.x, bf16[2048,1536]{1,0:T(8,128)(2,1)} %get-tuple-element.76.y.x, ...), custom_call_target="tpu_custom_call" | custom-call | flops 1024 | bytes 1024 | tf_op jit(solution)/shard_map/pallas_call | solution.py:394
  249.2 7.8 shard_map.304
  257.2 7.8 shard_map.305
  265.0 18.9 %shard_map.306.y.x = bf16[2048,2304]{1,0:T(8,128)(2,1)} custom-call(bf16[2048,1536]{1,0:T(8,128)(2,1)} %get-tuple-element.76.y.x, bf16[1536,3456]{1,0:T(8,128)(2,1)} %get-tuple-element.72.w_gate.w_up.w.refs_0_.refs_1_, f32[2048,1152]{1,0:T(8,128)} %get-tuple-element.77.gate, f32[2048,1152]{1,0:T(8,128)} %get-tuple-element.78.up), custom_call_target="tpu_custom_call" | custom-call | flops 1024 | bytes 1024 | tf_op jit(solution)/shard_map/pallas_call | solution.py:394
  283.9 7.8 shard_map.307
  291.7 8.7 %shard_map.308 = bf16[768,1152]{1,0:T(8,128)(2,1)} custom-call(s32[2]{0:T(128)S(1)} %pad_add_fusion.1.blocks, bf16[1536,2048]{1,0:T(8,128)(2,1)} %get-tuple-element.87.x, bf16[2048,2304]{1,0:T(8,128)(2,1)} %shard_map.306.y.x), custom_call_target="tpu_custom_call" | custom-call | flops 1024 | bytes 1024 | tf_op jit(solution)/shard_map/pallas_call | solution.py:510
  302.8 13.3 %shard_map.309 = bf16[1024,1536]{1,0:T(8,128)(2,1)} custom-call(bf16[2048,2304]{1,0:T(8,128)(2,1)} %shard_map.306.y.x, bf16[1536,3456]{1,0:T(8,128)(2,1)} %get-tuple-element.72.w_gate.w_up.w.refs_0_.refs_1_, bf16[1536,3456]{1,0:T(8,128)(2,1)} %get-tuple-element.72.w_gate.w_up.w.refs_0_.refs_1_), custom_call_target="tpu_custom_call" | custom-call | flops 1024 | bytes 1024 | tf_op jit(solution)/shard_map/pallas_call | solution.py:394
  317.5 13.7 %shard_map.310 = bf16[1024,1536]{1,0:T(8,128)(2,1)} custom-call(bf16[2048,2304]{1,0:T(8,128)(2,1)} %shard_map.306.y.x, bf16[1536,3456]{1,0:T(8,128)(2,1)} %get-tuple-element.72.w_gate.w_up.w.refs_0_.refs_1_, bf16[1536,3456]{1,0:T(8,128)(2,1)} %get-tuple-element.72.w_gate.w_up.w.refs_0_.refs_1_), custom_call_target="tpu_custom_call" | custom-call | flops 1024 | bytes 1024 | tf_op jit(solution)/shard_map/pallas_call | solution.py:394
  335.5 7.8 shard_map.311
  343.3 12.4 %collective-permute-done.3 = bf16[768,1152]{1,0:T(8,128)(2,1)S(1)} collective-permute-done((bf16[768,1152]{1,0:T(8,128)(2,1)S(1)}, bf16[768,1152]{1,0:T(8,128)(2,1)S(1)}, u32[]{:S(2)}, u32[]{:S(2)}) %collective-permute-start.3) | collective-permute-done | bytes 1769504 | tf_op jit(solution)/shard_map/ppermute | solution.py:1238
  358.1 8.1 shard_map.312
  372.3 8.1 shard_map.313
  390.1 8.1 shard_map.314
  402.3 37.3 %collective-permute-done.8 = bf16[384,1152]{1,0:T(8,128)(2,1)} collective-permute-done((bf16[384,1152]{1,0:T(8,128)(2,1)}, bf16[384,1152]{1,0:T(8,128)(2,1)}, u32[]{:S(2)}, u32[]{:S(2)}) %collective-permute-start.8) | collective-permute-done | bytes 884768 | tf_op jit(solution)/shard_map/ppermute | solution.py:1238
  441.3 18.6 %collective-permute-done.7 = bf16[768,1152]{1,0:T(8,128)(2,1)} collective-permute-done((bf16[768,1152]{1,0:T(8,128)(2,1)}, bf16[768,1152]{1,0:T(8,128)(2,1)}, u32[]{:S(2)}, u32[]{:S(2)}) %collective-permute-start.7) | collective-permute-done | bytes 1769504 | tf_op jit(solution)/shard_map/ppermute | solution.py:1238
  463.5 27.3 %shard_map.315 = (f32[512,1536]{1,0:T(8,128)}, f32[1,1536]{1,0:T(1,128)}, f32[1,1024]{1,0:T(1,128)}, bf16[512,1536]{1,0:T(8,128)(2,1)}, bf16[8,96,1792]{2,1,0:T(8,128)(2,1)}, /*index=5*/bf16[8,96,1792]{2,1,0:T(8,128)(2,1)}) custom-call(bf16[512,1536]{1,0:T(8,128)(2,1)} %add_convert_fusion.3.back, bf16[512,1536]{1,0:T(8,128)(2,1)} %copy-done.37, ...), custom_call_target="tpu_custom_call" | custom-call | flops 1024 | bytes 1024 | tf_op jit(solution)/shard_map/pallas_call | solution.py:1175
  504.5 5.5 collective-permute-done.14
  525.7 27.4 %collective-permute-done.15 = bf16[384,1152]{1,0:T(8,128)(2,1)S(1)} collective-permute-done((bf16[384,1152]{1,0:T(8,128)(2,1)S(1)}, bf16[384,1152]{1,0:T(8,128)(2,1)S(1)}, u32[]{:S(2)}, u32[]{:S(2)}) %collective-permute-start.15) | collective-permute-done | bytes 884768 | tf_op jit(solution)/shard_map/ppermute | solution.py:1238
  562.7 5.8 collective-permute-done.18
  574.5 22.4 %collective-permute-done.22 = bf16[384,1792]{1,0:T(8,128)(2,1)S(1)} collective-permute-done((bf16[384,1792]{1,0:T(8,128)(2,1)S(1)}, bf16[384,1792]{1,0:T(8,128)(2,1)S(1)}, u32[]{:S(2)}, u32[]{:S(2)}) %collective-permute-start.22) | collective-permute-done | bytes 1376288 | tf_op jit(solution)/shard_map/ppermute | solution.py:1238
  599.4 14.0 %collective-permute-done.23 = bf16[192,1792]{1,0:T(8,128)(2,1)S(1)} collective-permute-done((bf16[192,1792]{1,0:T(8,128)(2,1)S(1)}, bf16[192,1792]{1,0:T(8,128)(2,1)S(1)}, u32[]{:S(2)}, u32[]{:S(2)}) %collective-permute-start.23) | collective-permute-done | bytes 688160 | tf_op jit(solution)/shard_map/ppermute | solution.py:1238
  618.9 12.9 %collective-permute-done.24 = bf16[96,1792]{1,0:T(8,128)(2,1)S(1)} collective-permute-done((bf16[96,1792]{1,0:T(8,128)(2,1)S(1)}, bf16[96,1792]{1,0:T(8,128)(2,1)S(1)}, u32[]{:S(2)}, u32[]{:S(2)}) %collective-permute-start.24) | collective-permute-done | bytes 344096 | tf_op jit(solution)/shard_map/ppermute | solution.py:1238
  635.4 170.4 %shard_map.316 = (bf16[96,15232]{1,0:T(8,128)(2,1)}, f32[32,128]{1,0:T(8,128)S(1)}) custom-call(bf16[96,15232]{1,0:T(8,128)(2,1)} %copy-done.44, f32[32,128]{1,0:T(8,128)S(1)} %maximum_bitcast_fusion.vectors), custom_call_target="tpu_custom_call" | custom-call | flops 64000000000 | bytes 16777216 | tf_op jit(solution)/shard_map/pallas_call | solution.py:354
  (250 shorter events, 128.8 us)
Async XLA Ops:
  257.0 43.5 %collective-permute-start = (bf16[768,1152]{1,0:T(8,128)(2,1)S(1)}, bf16[768,1152]{1,0:T(8,128)(2,1)}, u32[]{:S(2)}, u32[]{:S(2)}) collective-permute-start(bf16[768,1152]{1,0:T(8,128)(2,1)S(1)} %shard_map.304), channel_id=1, source_target_pairs={{0,8},{2,10},{4,12},{6,14},{8,0},{10,2},{12,4},{14,6},{16,24},{18,... | collective-permute-start | bytes 5308424 | tf_op jit(solution)/shard_map/ppermute | solution.py:1238
  316.1 15.1 %collective-permute-start.1 = (bf16[1024,1536]{1,0:T(8,128)(2,1)}, bf16[1024,1536]{1,0:T(8,128)(2,1)S(1)}, u32[]{:S(2)}, u32[]{:S(2)}) collective-permute-start(bf16[1024,1536]{1,0:T(8,128)(2,1)} %shard_map.309), channel_id=1, source_target_pairs={{0,2},{2,0},{4,6},{6,4},{8,10},{10,8},{12,14},{14,12},{16,18},{18,... | collective-permute-start | bytes 9437192 | tf_op jit(solution)/shard_map/ppermute | solution.py:1238
  316.1 39.7 %collective-permute-start.3 = (bf16[768,1152]{1,0:T(8,128)(2,1)S(1)}, bf16[768,1152]{1,0:T(8,128)(2,1)S(1)}, u32[]{:S(2)}, u32[]{:S(2)}) collective-permute-start(bf16[768,1152]{1,0:T(8,128)(2,1)S(1)} %shard_map.307), channel_id=1, source_target_pairs={{0,8},{2,10},{4,12},{6,14},{8,0},{10,2},{12,4},{14,6},{16,24},{18,... | collective-permute-start | bytes 5308424 | tf_op jit(solution)/shard_map/ppermute | solution.py:1238
  335.2 35.3 %collective-permute-start.2 = (bf16[512,1536]{1,0:T(8,128)(2,1)}, bf16[512,1536]{1,0:T(8,128)(2,1)S(1)}, u32[]{:S(2)}, u32[]{:S(2)}) collective-permute-start(bf16[512,1536]{1,0:T(8,128)(2,1)} %add_convert_fusion.4), channel_id=1, source_target_pairs={{0,4},{2,6},{4,0},{6,2},{8,12},{10,14},{12,8},{14,10},{16,20},{18,... | collective-permute-start | bytes 4718600 | tf_op jit(solution)/shard_map/ppermute | solution.py:1238
  380.5 17.7 %collective-permute-start.4 = (bf16[1024,1536]{1,0:T(8,128)(2,1)}, bf16[1024,1536]{1,0:T(8,128)(2,1)}, u32[]{:S(2)}, u32[]{:S(2)}) collective-permute-start(bf16[1024,1536]{1,0:T(8,128)(2,1)} %shard_map.313), channel_id=1, source_target_pairs={{0,2},{2,0},{4,6},{6,4},{8,10},{10,8},{12,14},{14,12},{16,18},{18,... | collective-permute-start | bytes 9437192 | tf_op jit(solution)/shard_map/ppermute | solution.py:1238
  382.2 77.8 %collective-permute-start.7 = (bf16[768,1152]{1,0:T(8,128)(2,1)}, bf16[768,1152]{1,0:T(8,128)(2,1)}, u32[]{:S(2)}, u32[]{:S(2)}) collective-permute-start(bf16[768,1152]{1,0:T(8,128)(2,1)} %shard_map.308), channel_id=1, source_target_pairs={{0,8},{2,10},{4,12},{6,14},{8,0},{10,2},{12,4},{14,6},{16,24},{18,... | collective-permute-start | bytes 5308424 | tf_op jit(solution)/shard_map/ppermute | solution.py:1238
  382.6 57.0 %collective-permute-start.8 = (bf16[384,1152]{1,0:T(8,128)(2,1)}, bf16[384,1152]{1,0:T(8,128)(2,1)}, u32[]{:S(2)}, u32[]{:S(2)}) collective-permute-start(bf16[384,1152]{1,0:T(8,128)(2,1)} %add_convert_fusion.11), channel_id=1, source_target_pairs={{0,16},{2,18},{4,20},{6,22},{8,24},{10,26},{12,28},{14,30},{16,0},... | collective-permute-start | bytes 2654216 | tf_op jit(solution)/shard_map/ppermute | solution.py:1238
  388.8 102.0 %collective-permute-start.10 = (bf16[384,1152]{1,0:T(8,128)(2,1)}, bf16[384,1152]{1,0:T(8,128)(2,1)}, u32[]{:S(2)}, u32[]{:S(2)}) collective-permute-start(bf16[384,1152]{1,0:T(8,128)(2,1)} %add_convert_fusion.10), channel_id=1, source_target_pairs={{0,16},{2,18},{4,20},{6,22},{8,24},{10,26},{12,28},{14,30},{16,0},... | collective-permute-start | bytes 2654216 | tf_op jit(solution)/shard_map/ppermute | solution.py:1238
  388.8 73.5 %collective-permute-start.6 = (bf16[512,1536]{1,0:T(8,128)(2,1)}, bf16[512,1536]{1,0:T(8,128)(2,1)S(1)}, u32[]{:S(2)}, u32[]{:S(2)}) collective-permute-start(bf16[512,1536]{1,0:T(8,128)(2,1)} %add_convert_fusion.3.back), channel_id=1, source_target_pairs={{0,1},{1,0},{2,3},{3,2},{4,5},{5,4},{6,7},{7,6},{8,9},{9,8},{10,11... | collective-permute-start | bytes 4718600 | tf_op jit(solution)/shard_map/ppermute | solution.py:1238
  401.7 120.4 %collective-permute-start.5 = (bf16[512,1536]{1,0:T(8,128)(2,1)}, bf16[512,1536]{1,0:T(8,128)(2,1)}, u32[]{:S(2)}, u32[]{:S(2)}) collective-permute-start(bf16[512,1536]{1,0:T(8,128)(2,1)} %add_convert_fusion.1), channel_id=1, source_target_pairs={{0,4},{2,6},{4,0},{6,2},{8,12},{10,14},{12,8},{14,10},{16,20},{18,... | collective-permute-start | bytes 4718600 | tf_op jit(solution)/shard_map/ppermute | solution.py:1238
  492.8 26.6 %collective-permute-start.9 = (bf16[768,1792]{1,0:T(8,128)(2,1)}, bf16[768,1792]{1,0:T(8,128)(2,1)}, u32[]{:S(2)}, u32[]{:S(2)}) collective-permute-start(bf16[768,1792]{1,0:T(8,128)(2,1)} %bitcast.115), channel_id=1, source_target_pairs={{0,2},{2,0},{4,6},{6,4},{8,10},{10,8},{12,14},{14,12},{16,18},{18,... | collective-permute-start | bytes 8257544 | tf_op jit(solution)/shard_map/ppermute | solution.py:1238
  497.2 7.1 collective-permute-start.13
  497.4 12.6 %collective-permute-start.14 = (bf16[1,96,1152]{2,1,0:T(8,128)(2,1)}, bf16[1,96,1152]{2,1,0:T(8,128)(2,1)}, u32[]{:S(2)}, u32[]{:S(2)}) collective-permute-start(bf16[1,96,1152]{2,1,0:T(8,128)(2,1)} %get-tuple-element.152), channel_id=1, source_target_pairs={{0,6},{2,4},{4,2},{6,0},{8,14},{10,12},{12,10},{14,8},{16,22},{18,... | collective-permute-start | bytes 663560 | tf_op jit(solution)/shard_map/ppermute | solution.py:1238
  500.0 12.4 %collective-permute-start.19 = (bf16[1,96,1152]{2,1,0:T(8,128)(2,1)}, bf16[1,96,1152]{2,1,0:T(8,128)(2,1)S(1)}, u32[]{:S(2)}, u32[]{:S(2)}) collective-permute-start(bf16[1,96,1152]{2,1,0:T(8,128)(2,1)} %get-tuple-element.150), channel_id=1, source_target_pairs={{0,2},{2,0},{4,6},{6,4},{8,10},{10,8},{12,14},{14,12},{16,18},{18,... | collective-permute-start | bytes 663560 | tf_op jit(solution)/shard_map/ppermute | solution.py:1238
  504.2 9.4 %collective-permute-start.20 = (bf16[1,96,1152]{2,1,0:T(8,128)(2,1)}, bf16[1,96,1152]{2,1,0:T(8,128)(2,1)S(1)}, u32[]{:S(2)}, u32[]{:S(2)}) collective-permute-start(bf16[1,96,1152]{2,1,0:T(8,128)(2,1)} %get-tuple-element.149), channel_id=1, source_target_pairs={{0,4},{2,6},{4,0},{6,2},{8,12},{10,14},{12,8},{14,10},{16,20},{18,... | collective-permute-start | bytes 663560 | tf_op jit(solution)/shard_map/ppermute | solution.py:1238
  510.0 9.0 %collective-permute-start.21 = (bf16[1,96,1152]{2,1,0:T(8,128)(2,1)}, bf16[1,96,1152]{2,1,0:T(8,128)(2,1)S(1)}, u32[]{:S(2)}, u32[]{:S(2)}) collective-permute-start(bf16[1,96,1152]{2,1,0:T(8,128)(2,1)} %get-tuple-element.148), channel_id=1, source_target_pairs={{0,6},{2,4},{4,2},{6,0},{8,14},{10,12},{12,10},{14,8},{16,22},{18,... | collective-permute-start | bytes 663560 | tf_op jit(solution)/shard_map/ppermute | solution.py:1238
  512.8 40.4 %collective-permute-start.15 = (bf16[384,1152]{1,0:T(8,128)(2,1)S(1)}, bf16[384,1152]{1,0:T(8,128)(2,1)S(1)}, u32[]{:S(2)}, u32[]{:S(2)}) collective-permute-start(bf16[384,1152]{1,0:T(8,128)(2,1)S(1)} %copy-done.41), channel_id=1, source_target_pairs={{0,16},{2,18},{4,20},{6,22},{8,24},{10,26},{12,28},{14,30},{16,0},... | collective-permute-start | bytes 2654216 | tf_op jit(solution)/shard_map/ppermute | solution.py:1238
  513.6 101.0 %collective-permute-start.25 = (bf16[512,1536]{1,0:T(8,128)(2,1)S(1)}, bf16[512,1536]{1,0:T(8,128)(2,1)S(1)}, u32[]{:S(2)}, u32[]{:S(2)}) collective-permute-start(bf16[512,1536]{1,0:T(8,128)(2,1)S(1)} %copy-done.22), channel_id=1, source_target_pairs={{0,1},{1,0},{2,3},{3,2},{4,5},{5,4},{6,7},{7,6},{8,9},{9,8},{10,11... | collective-permute-start | bytes 4718600 | tf_op jit(solution)/shard_map/ppermute | solution.py:1238
  555.7 7.0 collective-permute-start.17
  556.4 12.0 %collective-permute-start.18 = (bf16[1,96,1152]{2,1,0:T(8,128)(2,1)S(1)}, bf16[1,96,1152]{2,1,0:T(8,128)(2,1)S(1)}, u32[]{:S(2)}, u32[]{:S(2)}) collective-permute-start(bf16[1,96,1152]{2,1,0:T(8,128)(2,1)S(1)} %get-tuple-element.156), channel_id=1, source_target_pairs={{0,6},{2,4},{4,2},{6,0},{8,14},{10,12},{12,10},{14,8},{16,22},{18,... | collective-permute-start | bytes 663560 | tf_op jit(solution)/shard_map/ppermute | solution.py:1238
  558.1 38.8 %collective-permute-start.22 = (bf16[384,1792]{1,0:T(8,128)(2,1)S(1)}, bf16[384,1792]{1,0:T(8,128)(2,1)S(1)}, u32[]{:S(2)}, u32[]{:S(2)}) collective-permute-start(bf16[384,1792]{1,0:T(8,128)(2,1)S(1)} %get-tuple-element.142), channel_id=1, source_target_pairs={{0,4},{2,6},{4,0},{6,2},{8,12},{10,14},{12,8},{14,10},{16,20},{18,... | collective-permute-start | bytes 4128776 | tf_op jit(solution)/shard_map/ppermute | solution.py:1238
  558.9 257.9 %collective-permute-start.11 = (bf16[512,1536]{1,0:T(8,128)(2,1)}, bf16[512,1536]{1,0:T(8,128)(2,1)}, u32[]{:S(2)}, u32[]{:S(2)}) collective-permute-start(bf16[512,1536]{1,0:T(8,128)(2,1)} %add_convert_fusion), channel_id=1, source_target_pairs={{0,1},{1,0},{2,3},{3,2},{4,5},{5,4},{6,7},{7,6},{8,9},{9,8},{10,11... | collective-permute-start | bytes 4718600 | tf_op jit(solution)/shard_map/ppermute | solution.py:1238
  597.2 16.2 %collective-permute-start.23 = (bf16[192,1792]{1,0:T(8,128)(2,1)S(1)}, bf16[192,1792]{1,0:T(8,128)(2,1)S(1)}, u32[]{:S(2)}, u32[]{:S(2)}) collective-permute-start(bf16[192,1792]{1,0:T(8,128)(2,1)S(1)} %get-tuple-element.139), channel_id=1, source_target_pairs={{0,8},{2,10},{4,12},{6,14},{8,0},{10,2},{12,4},{14,6},{16,24},{18,... | collective-permute-start | bytes 2064392 | tf_op jit(solution)/shard_map/ppermute | solution.py:1238
  613.5 18.3 %collective-permute-start.24 = (bf16[96,1792]{1,0:T(8,128)(2,1)S(1)}, bf16[96,1792]{1,0:T(8,128)(2,1)S(1)}, u32[]{:S(2)}, u32[]{:S(2)}) collective-permute-start(bf16[96,1792]{1,0:T(8,128)(2,1)S(1)} %add_convert_fusion.14), channel_id=1, source_target_pairs={{0,16},{2,18},{4,20},{6,22},{8,24},{10,26},{12,28},{14,30},{16,0},... | collective-permute-start | bytes 1032200 | tf_op jit(solution)/shard_map/ppermute | solution.py:1238
  (56 other events, 368.3 us)

commit v3 on v2

--- a/solution.py
+++ b/solution.py
@@ -1005,6 +1005,154 @@
     )
 
 
+def exchange_kernel(
+    near, far, pieces, total, joined, came, work, chain_send, chain_come, group_send, group_come, here_sem
+):
+    me = lax.axis_index("dp")
+    place, plane = lax.rem(me, 4), me // 4
+    size = pieces.shape[3]
+    width = near.shape[2] // 2
+
+    def flip(stride):
+        return me + stride - 2 * stride * lax.rem(me // stride, 2)
+
+    def plane_peer(turn):
+        return plane * 4 + lax.rem(place + turn, 4)
+
+    def remote(source, target, send, receive, device):
+        return pltpu.make_async_remote_copy(
+            src_ref=source,
+            dst_ref=target,
+            send_sem=send,
+            recv_sem=receive,
+            device_id={"dp": device},
+            device_id_type=pl.DeviceIdType.MESH,
+        )
+
+    barrier = pltpu.get_barrier_semaphore()
+    for device in [plane_peer(turn) for turn in (1, 2, 3)] + [flip(stride) for stride in HALVES[0][2:]]:
+        pl.semaphore_signal(
+            barrier, inc=1, device_id={"dp": device}, device_id_type=pl.DeviceIdType.MESH
+        )
+    pl.semaphore_wait(barrier, 3 + len(HALVES[0][2:]))
+
+    def columns(at):
+        return slice(at * width, (at + 1) * width)
+
+    def blocks(step):
+        return near.shape[0] >> step
+
+    def offset(step):
+        return 2 * near.shape[0] - 2 * blocks(step)
+
+    def move(step, at):
+        count = blocks(step)
+        if step == 0:
+            source = far.at[:, :, columns(at)]
+        else:
+            first = offset(step - 1) + count
+            source = work.at[first : first + count, :, columns(at)]
+        first = offset(step)
+        return remote(
+            source,
+            came.at[first : first + count, :, columns(at)],
+            chain_send.at[step, at],
+            chain_come.at[step, at],
+            flip(HALVES[at][step]),
+        )
+
+    def regroup(kind, turn):
+        owner = lax.rem(place + turn, 4)
+        return remote(
+            pieces.at[kind, owner],
+            joined.at[kind, :, pl.ds(pl.multiple_of(place * size, 128), size)],
+            group_send.at[kind, turn],
+            group_come.at[kind, turn],
+            plane_peer(turn),
+        )
+
+    def regroup_wait(kind, turn):
+        sender = lax.rem(place + 4 - turn, 4)
+        return remote(
+            pieces.at[kind, 0],
+            joined.at[kind, :, pl.ds(pl.multiple_of(sender * size, 128), size)],
+            group_send.at[kind, turn],
+            group_come.at[kind, turn],
+            me,
+        )
+
+    def own(kind):
+        return pltpu.make_async_copy(
+            pieces.at[kind, place],
+            joined.at[kind, :, pl.ds(pl.multiple_of(place * size, 128), size)],
+            here_sem.at[kind],
+        )
+
+    steps = len(HALVES[0])
+    for at in range(2):
+        move(0, at).start()
+    kinds = range(pieces.shape[0])
+    for kind in kinds:
+        for turn in (1, 2, 3):
+            regroup(kind, turn).start()
+        own(kind).start()
+    for step in range(steps):
+        for at in range(2):
+            move(step, at).wait()
+            count = blocks(step)
+            first = offset(step)
+            held = near if step == 0 else work
+            begin = 0 if step == 0 else offset(step - 1)
+            for block in range(count):
+                value = held[begin + block, :, columns(at)].astype(FLOAT) + came[
+                    first + block, :, columns(at)
+                ].astype(FLOAT)
+                if step == steps - 1:
+                    total[:, columns(at)] = value
+                else:
+                    work[first + block, :, columns(at)] = value.astype(BFLOAT)
+            if step < steps - 1:
+                move(step + 1, at).start()
+    for kind in kinds:
+        for turn in (1, 2, 3):
+            regroup_wait(kind, turn).wait_recv()
+            regroup(kind, turn).wait_send()
+        own(kind).wait()
+
+
+HALVES = ((1, 2, 4, 8), (1, 4, 8, 2))
+
+
+def exchange(near, far, pieces):
+    count, rows, width = near.shape
+    kinds, _, _, size = pieces.shape
+    hbm = pl.BlockSpec(memory_space=pltpu.HBM)
+    vmem = pl.BlockSpec(memory_space=pltpu.VMEM)
+    dma = pltpu.SemaphoreType.DMA
+    return pl.pallas_call(
+        exchange_kernel,
+        out_shape=[
+            jax.ShapeDtypeStruct((rows, width), FLOAT),
+            jax.ShapeDtypeStruct((kinds, rows, 4 * size), BFLOAT),
+        ],
+        in_specs=[vmem, vmem, hbm],
+        out_specs=[vmem, hbm],
+        scratch_shapes=[
+            pltpu.VMEM((2 * count, rows, width), BFLOAT),
+            pltpu.VMEM((2 * count, rows, width), BFLOAT),
+            dma((4, 2)),
+            dma((4, 2)),
+            dma((kinds, 4)),
+            dma((kinds, 4)),
+            dma((kinds,)),
+        ],
+        compiler_params=pltpu.CompilerParams(
+            collective_id=2, has_side_effects=True, vmem_limit_bytes=40 * 2**20
+        ),
+        cost_estimate=LIGHT,
+    )(near, far, pieces)
+
+
 def backward_part(
     back,
     came,
@@ -1022,7 +1170,7 @@
     sine,
     doc_ids,
     devices,
-    order,
+    orders,
 ):
     count, depth = hidden.shape
     rows = depth // devices
@@ -1161,15 +1309,17 @@
                 dbranch[:, span], attn[...], (((0,), (0,)), ((), ())), preferred_element_type=FLOAT
             )
         me = lax.axis_index("dp")
-        for place in range(devices):
-            block = 0
-            for at, stride in enumerate(order):
-                bit = (place >> (len(order) - 1 - at)) & 1
-                block = block + lax.rem(me // stride + bit, 2) * stride
-            target = near if place < devices // 2 else far
-            target[place % (devices // 2)] = term[
-                pl.ds(pl.multiple_of(block * rows, 8), rows), :
-            ].astype(BFLOAT)
+        for side, order in enumerate(orders):
+            span = slice(side * width // 2, (side + 1) * width // 2)
+            for place in range(devices):
+                block = 0
+                for at, stride in enumerate(order):
+                    bit = (place >> (len(order) - 1 - at)) & 1
+                    block = block + lax.rem(me // stride + bit, 2) * stride
+                target = near if place < devices // 2 else far
+                target[place % (devices // 2), :, span] = term[
+                    pl.ds(pl.multiple_of(block * rows, 8), rows), span
+                ].astype(BFLOAT)
 
     vmem = pl.BlockSpec(memory_space=pltpu.VMEM)
     outs = pl.pallas_call(
@@ -1218,8 +1368,8 @@
         gain_term[0],
         bias_term[0],
         dnormed,
-        near.reshape(-1, width),
-        far.reshape(-1, width),
+        near,
+        far,
     )
 
 
@@ -1479,21 +1629,29 @@
         sine_two,
         doc_ids,
         devices,
-        every,
+        HALVES if devices == 16 else (every, every),
     )
-    chain = Chain(kept, sent, every)
     dnormed_came = swap(dnormed, "tensor", 1)
-    gate_total = gate_chain.finish(dnormed)
-    token = chain.come(gate_total)
-    gate_shard = own_rows(gate_total)
-    layer = layer_chain.come(token).astype(BFLOAT)
-    layer_came = swap(layer, "tensor", 1)
-    up_total = up_chain.finish(layer)
-    token = chain.come(up_total)
-    up_shard = own_rows(up_total)
-    token = chain.come(token)
+    if devices == 16:
+        gate_total = gate_chain.finish(dnormed)
+        layer = layer_chain.come(gate_total).astype(BFLOAT)
+        layer_came = swap(layer, "tensor", 1)
+        up_total = up_chain.finish(layer)
+        pieces = jnp.stack([gate_total, up_total]).astype(BFLOAT)
+        attention_shard, joined = exchange(kept, sent, pieces.reshape(2, plane, rows, part))
+        layer_came = after(layer_came, attention_shard)
+        attention_shard = after(attention_shard, layer_came)
+        joined = joined[:, :, :units].astype(FLOAT)
+        gate_shard, up_shard = joined[0], joined[1]
+        token = attention_shard
+    else:
+        chain = Chain(kept.reshape(-1, kept.shape[2]), sent.reshape(-1, sent.shape[2]), every)
+        gate_total, up_total = gate_chain.finish(dnormed), up_chain.finish(dnormed)
+        gate_shard, up_shard = own_rows(gate_total), own_rows(up_total)
+        layer = layer_chain.come(up_total).astype(BFLOAT)
+        layer_came = swap(layer, "tensor", 1)
+        token = attention_shard = chain.finish(layer)
     dnormed = dnormed.astype(FLOAT) + after(dnormed_came, token).astype(FLOAT)
-    attention_shard = chain.finish(dnormed)
     qkv_shard = attention_shard[:, :group_width]
     out_shard = attention_shard[:, group_width:]
     tokens_grad = dhidden1 + norm_back(dnormed, inputs, scale_one, norm_gains[0])
@@ -1519,7 +1677,7 @@
     bias_grad = vectors[2 * inputs.shape[1] :]
     gains_m = MOMENTUM * gains_moment + gains_grad
     bias_m = MOMENTUM * bias_moment + bias_grad
-    layer_out = hidden1 + (layer.astype(FLOAT) + after(layer_came, solved).astype(FLOAT))
+    layer_out = hidden1 + (layer.astype(FLOAT) + layer_came.astype(FLOAT))
     gate_up_update = jnp.stack([solved[:, :units], solved[:, units : 2 * units]]).astype(FLOAT)
     down_update = solved[:, 2 * units : 3 * units].astype(FLOAT)
     last = solved[:, 3 * units :].astype(FLOAT)

time: 834 us -> 795 us (0.953)
  waiting for transfers between devices: 172 us -> 80.9 us
  Pallas kernels: 539 us -> 602 us
    ppermute x26 -> x16, waiting for transfers between devices: 172 us -> 80.9 us  [swap(): return lax.ppermute(value, axis, [(at, at ^ stride) for at in range(count)])]
    pallas_call x0 -> x1, Pallas kernels: none -> 61.8 us  [exchange(): pl.pallas_call(exchange_kernel, out_shape=[jax.ShapeDtypeStruct((rows, wi...]
    ppermute x26 -> x16, starting transfers between devices: 20.4 us -> 15.1 us  [swap(): return lax.ppermute(value, axis, [(at, at ^ stride) for at in range(count)])]
  transfers between devices with their start and end apart: 26 -> 16, of which waited for: 14 -> 6; matrix products, arithmetic and copies ran while one was open for 7% -> 4% of each run, Pallas kernels for 34% -> 22%
where the time goes in v3:
time: 795 us; the launch traced here: 783 us
  Pallas kernels  602 us (76%)
  waiting for transfers between devices  80.9 us (10%)
  other arithmetic  60.9 us (8%)
  local copies, waits for them, and re-layouts  21.9 us (3%)
  starting transfers between devices  15.1 us (2%)
    pallas_call x1, Pallas kernels, forward_part(): pl.pallas_call(functools.partial(forward_kernel, devices, heads, kv_heads...  206 us
    pallas_call x1, Pallas kernels, orthogonalize(): pl.pallas_call(kernel, out_shape=[jax.ShapeDtypeStruct(units.shape, wire)...  171 us
    pallas_call x6, Pallas kernels, call_light(): pl.pallas_call(body, grid=grid, in_specs=[pl.BlockSpec(block, at) for _,...  86.8 us
    ppermute x16, waiting for transfers between devices, swap(): return lax.ppermute(value, axis, [(at, at ^ stride) for at in range(count)])  80.9 us
    pallas_call x1, Pallas kernels, exchange(): pl.pallas_call(exchange_kernel, out_shape=[jax.ShapeDtypeStruct((rows, wi...  61.8 us
    pallas_call x6, Pallas kernels, weight_term(): pl.pallas_call(body, grid_spec=pltpu.PrefetchScalarGridSpec(num_scalar_pr...  48 us
    pallas_call x1, Pallas kernels, backward_part(): pl.pallas_call(body, out_shape=[jax.ShapeDtypeStruct((count, depth), FLOA...  27.3 us
  transfers between devices with their start and end apart: 16, of which 6 were waited for; matrix products, arithmetic and copies ran while one was open for 4% of the time, Pallas kernels for 22%

profile of v3, /device:TPU:27, one launch (start us, length us, event | category | flops | bytes accessed | tf_op | source)
XLA Modules:
  0.0 782.7 jit_solution(3055530988784578257)
XLA Ops:
  15.7 206.4 %shard_map.302 = (bf16[512,1536]{1,0:T(8,128)(2,1)S(1)}, f32[512,1536]{1,0:T(8,128)}, bf16[512,768]{1,0:T(8,128)(2,1)S(1)}, bf16[512,768]{1,0:T(8,128)(2,1)S(1)}...) custom-call(bf16[512,1536]{1,0:T(8,128)(2,1)S(1)} %copy-done, ...), custom_call_target="tpu_custom_call" | custom-call | flops 1024 | bytes 1024 | tf_op jit(solution)/shard_map/pallas_call | solution.py:953
  226.4 24.7 %shard_map.303 = (f32[2048,1152]{1,0:T(8,128)}, f32[2048,1152]{1,0:T(8,128)}, bf16[2048,1152]{1,0:T(8,128)(2,1)}, bf16[1536,2048]{1,0:T(8,128)(2,1)}, bf16[1536,2048]{1,0:T(8,128)(2,1)}) custom-call(bf16[2048,1536]{1,0:T(8,128)(2,1)} %get-tuple-element.69.x, bf16[2048,1536]{1,0:T(8,128)(2,1)} %get-tuple-element.75.y.x, ...), custom_call_target="tpu_custom_call" | custom-call | flops 1024 | bytes 1024 | tf_op jit(solution)/shard_map/pallas_call | solution.py:394
  251.1 7.8 shard_map.304
  259.1 7.8 shard_map.305
  266.9 18.9 %shard_map.306.y.x = bf16[2048,2304]{1,0:T(8,128)(2,1)} custom-call(bf16[2048,1536]{1,0:T(8,128)(2,1)} %get-tuple-element.75.y.x, bf16[1536,3456]{1,0:T(8,128)(2,1)} %get-tuple-element.71.w_gate.w_up.w.refs_0_.refs_1_, f32[2048,1152]{1,0:T(8,128)} %get-tuple-element.76.gate, f32[2048,1152]{1,0:T(8,128)} %get-tuple-element.77.up), custom_call_target="tpu_custom_call" | custom-call | flops 1024 | bytes 1024 | tf_op jit(solution)/shard_map/pallas_call | solution.py:394
  285.8 7.8 shard_map.307
  293.6 8.7 %shard_map.308 = bf16[768,1152]{1,0:T(8,128)(2,1)} custom-call(s32[2]{0:T(128)S(1)} %pad_add_fusion.1.blocks, bf16[1536,2048]{1,0:T(8,128)(2,1)} %get-tuple-element.86.x, bf16[2048,2304]{1,0:T(8,128)(2,1)} %shard_map.306.y.x), custom_call_target="tpu_custom_call" | custom-call | flops 1024 | bytes 1024 | tf_op jit(solution)/shard_map/pallas_call | solution.py:510
  304.6 13.3 %shard_map.309 = bf16[1024,1536]{1,0:T(8,128)(2,1)} custom-call(bf16[2048,2304]{1,0:T(8,128)(2,1)} %shard_map.306.y.x, bf16[1536,3456]{1,0:T(8,128)(2,1)} %get-tuple-element.71.w_gate.w_up.w.refs_0_.refs_1_, bf16[1536,3456]{1,0:T(8,128)(2,1)} %get-tuple-element.71.w_gate.w_up.w.refs_0_.refs_1_), custom_call_target="tpu_custom_call" | custom-call | flops 1024 | bytes 1024 | tf_op jit(solution)/shard_map/pallas_call | solution.py:394
  319.3 13.7 %shard_map.310 = bf16[1024,1536]{1,0:T(8,128)(2,1)} custom-call(bf16[2048,2304]{1,0:T(8,128)(2,1)} %shard_map.306.y.x, bf16[1536,3456]{1,0:T(8,128)(2,1)} %get-tuple-element.71.w_gate.w_up.w.refs_0_.refs_1_, bf16[1536,3456]{1,0:T(8,128)(2,1)} %get-tuple-element.71.w_gate.w_up.w.refs_0_.refs_1_), custom_call_target="tpu_custom_call" | custom-call | flops 1024 | bytes 1024 | tf_op jit(solution)/shard_map/pallas_call | solution.py:394
  333.0 4.0 add_convert_fusion.4
  337.4 7.8 shard_map.311
  345.2 12.4 %collective-permute-done.3 = bf16[768,1152]{1,0:T(8,128)(2,1)S(1)} collective-permute-done((bf16[768,1152]{1,0:T(8,128)(2,1)S(1)}, bf16[768,1152]{1,0:T(8,128)(2,1)S(1)}, u32[]{:S(2)}, u32[]{:S(2)}) %collective-permute-start.3) | collective-permute-done | bytes 1769504 | tf_op jit(solution)/shard_map/ppermute | solution.py:1388
  359.9 8.1 %shard_map.312 = bf16[768,1152]{1,0:T(8,128)(2,1)S(1)} custom-call(s32[2]{0:T(128)S(1)} %pad_add_fusion.blocks, bf16[1536,2048]{1,0:T(8,128)(2,1)} %get-tuple-element.86.x, bf16[2048,2304]{1,0:T(8,128)(2,1)} %shard_map.306.y.x), custom_call_target="tpu_custom_call" | custom-call | flops 1024 | bytes 1024 | tf_op jit(solution)/shard_map/pallas_call | solution.py:510
  368.0 4.4 collective-permute-done.2
  374.2 8.1 %shard_map.313 = bf16[1024,1536]{1,0:T(8,128)(2,1)} custom-call(bf16[2048,1152]{1,0:T(8,128)(2,1)} %get-tuple-element.89.y.x, bf16[1536,3456]{1,0:T(8,128)(2,1)} %get-tuple-element.71.w_gate.w_up.w.refs_0_.refs_1_), custom_call_target="tpu_custom_call" | custom-call | flops 1024 | bytes 1024 | tf_op jit(solution)/shard_map/pallas_call | solution.py:394
  384.4 4.7 collective-permute-start.9
  391.9 8.1 %shard_map.314 = bf16[1024,1536]{1,0:T(8,128)(2,1)} custom-call(bf16[2048,1152]{1,0:T(8,128)(2,1)} %get-tuple-element.89.y.x, bf16[1536,3456]{1,0:T(8,128)(2,1)} %get-tuple-element.71.w_gate.w_up.w.refs_0_.refs_1_), custom_call_target="tpu_custom_call" | custom-call | flops 1024 | bytes 1024 | tf_op jit(solution)/shard_map/pallas_call | solution.py:394
  404.1 37.3 %collective-permute-done.9 = bf16[384,1152]{1,0:T(8,128)(2,1)} collective-permute-done((bf16[384,1152]{1,0:T(8,128)(2,1)}, bf16[384,1152]{1,0:T(8,128)(2,1)}, u32[]{:S(2)}, u32[]{:S(2)}) %collective-permute-start.9) | collective-permute-done | bytes 884768 | tf_op jit(solution)/shard_map/ppermute | solution.py:1388
  443.2 18.6 %collective-permute-done.8 = bf16[768,1152]{1,0:T(8,128)(2,1)} collective-permute-done((bf16[768,1152]{1,0:T(8,128)(2,1)}, bf16[768,1152]{1,0:T(8,128)(2,1)}, u32[]{:S(2)}, u32[]{:S(2)}) %collective-permute-start.8) | collective-permute-done | bytes 1769504 | tf_op jit(solution)/shard_map/ppermute | solution.py:1388
  465.3 27.3 %shard_map.315 = (f32[512,1536]{1,0:T(8,128)}, f32[1,1536]{1,0:T(1,128)}, f32[1,1024]{1,0:T(1,128)}, bf16[512,1536]{1,0:T(8,128)(2,1)}, bf16[8,96,1792]{2,1,0:T(8,128)(2,1)}, /*index=5*/bf16[8,96,1792]{2,1,0:T(8,128)(2,1)}) custom-call(bf16[512,1536]{1,0:T(8,128)(2,1)} %add_convert_fusion.3.back, bf16[512,1536]{1,0:T(8,128)(2,1)} %copy-done.42, ...), custom_call_target="tpu_custom_call" | custom-call | flops 1024 | bytes 1024 | tf_op jit(solution)/shard_map/pallas_call | solution.py:1325
  502.0 5.0 collective-permute-done.15
  516.8 61.8 %shard_map.316 = (f32[96,1792]{1,0:T(8,128)S(1)}, bf16[2,96,4608]{2,1,0:T(8,128)(2,1)S(1)}) custom-call(bf16[8,96,1792]{2,1,0:T(8,128)(2,1)S(1)} %copy-done.5, bf16[8,96,1792]{2,1,0:T(8,128)(2,1)S(1)} %copy-done.6, bf16[2,4,96,1152]{3,2,1,0:T(8,128)(2,1)S(1)} %pad_maximum_fusion.1.pieces), custom_call_target="tpu_custom_call" | custom-call | flops 1024 | bytes 1024 | tf_op jit(solution)/shard_map/pallas_call | solution.py:1132
  589.6 171.2 %shard_map.317 = (bf16[96,15232]{1,0:T(8,128)(2,1)}, f32[32,128]{1,0:T(8,128)S(1)}) custom-call(bf16[96,15232]{1,0:T(8,128)(2,1)} %copy-done.47, f32[32,128]{1,0:T(8,128)S(1)} %maximum_bitcast_fusion.vectors), custom_call_target="tpu_custom_call" | custom-call | flops 64000000000 | bytes 16777216 | tf_op jit(solution)/shard_map/pallas_call | solution.py:354
  772.7 4.7 multiply_subtract_fusion
  (215 shorter events, 87.5 us)
Async XLA Ops:
  13.1 209.0 %copy-start.7 = (f32[512,128]{1,0:T(8,128)}, f32[512,128]{1,0:T(8,128)S(1)}, u32[]{:S(2)}) copy-start(f32[512,128]{1,0:T(8,128)S(1)} %get-tuple-element.148.cosine) | copy-start | bytes 786436
  13.2 209.0 %copy-start.8 = (f32[512,128]{1,0:T(8,128)}, f32[512,128]{1,0:T(8,128)S(1)}, u32[]{:S(2)}) copy-start(f32[512,128]{1,0:T(8,128)S(1)} %get-tuple-element.149.sine) | copy-start | bytes 786436
  258.9 43.4 %collective-permute-start = (bf16[768,1152]{1,0:T(8,128)(2,1)S(1)}, bf16[768,1152]{1,0:T(8,128)(2,1)}, u32[]{:S(2)}, u32[]{:S(2)}) collective-permute-start(bf16[768,1152]{1,0:T(8,128)(2,1)S(1)} %shard_map.304), channel_id=1, source_target_pairs={{0,8},{2,10},{4,12},{6,14},{8,0},{10,2},{12,4},{14,6},{16,24},{18,... | collective-permute-start | bytes 5308424 | tf_op jit(solution)/shard_map/ppermute | solution.py:1388
  266.9 35.4 %copy-start.3 = (bf16[768,1152]{1,0:T(8,128)(2,1)}, bf16[768,1152]{1,0:T(8,128)(2,1)S(1)}, u32[]{:S(2)}) copy-start(bf16[768,1152]{1,0:T(8,128)(2,1)S(1)} %shard_map.305) | copy-start | bytes 5308420
  317.9 15.1 %collective-permute-start.1 = (bf16[1024,1536]{1,0:T(8,128)(2,1)}, bf16[1024,1536]{1,0:T(8,128)(2,1)S(1)}, u32[]{:S(2)}, u32[]{:S(2)}) collective-permute-start(bf16[1024,1536]{1,0:T(8,128)(2,1)} %shard_map.309), channel_id=1, source_target_pairs={{0,2},{2,0},{4,6},{6,4},{8,10},{10,8},{12,14},{14,12},{16,18},{18,... | collective-permute-start | bytes 9437192 | tf_op jit(solution)/shard_map/ppermute | solution.py:1388
  317.9 39.7 %collective-permute-start.3 = (bf16[768,1152]{1,0:T(8,128)(2,1)S(1)}, bf16[768,1152]{1,0:T(8,128)(2,1)S(1)}, u32[]{:S(2)}, u32[]{:S(2)}) collective-permute-start(bf16[768,1152]{1,0:T(8,128)(2,1)S(1)} %shard_map.307), channel_id=1, source_target_pairs={{0,8},{2,10},{4,12},{6,14},{8,0},{10,2},{12,4},{14,6},{16,24},{18,... | collective-permute-start | bytes 5308424 | tf_op jit(solution)/shard_map/ppermute | solution.py:1388
  337.1 35.3 %collective-permute-start.2 = (bf16[512,1536]{1,0:T(8,128)(2,1)}, bf16[512,1536]{1,0:T(8,128)(2,1)S(1)}, u32[]{:S(2)}, u32[]{:S(2)}) collective-permute-start(bf16[512,1536]{1,0:T(8,128)(2,1)} %add_convert_fusion.4), channel_id=1, source_target_pairs={{0,4},{2,6},{4,0},{6,2},{8,12},{10,14},{12,8},{14,10},{16,20},{18,... | collective-permute-start | bytes 4718600 | tf_op jit(solution)/shard_map/ppermute | solution.py:1388
  345.2 22.8 %copy-start.1 = (bf16[768,1152]{1,0:T(8,128)(2,1)}, bf16[768,1152]{1,0:T(8,128)(2,1)S(1)}, u32[]{:S(2)}) copy-start(bf16[768,1152]{1,0:T(8,128)(2,1)S(1)} %shard_map.311) | copy-start | bytes 5308420
  359.9 12.5 %copy-start.20 = (bf16[1024,1536]{1,0:T(8,128)(2,1)S(1)}, bf16[1024,1536]{1,0:T(8,128)(2,1)}, u32[]{:S(2)}) copy-start(bf16[1024,1536]{1,0:T(8,128)(2,1)} %shard_map.310) | copy-start | bytes 9437188
  359.9 12.5 %copy-start.33 = (bf16[1024,1536]{1,0:T(8,128)(2,1)S(1)}, bf16[1024,1536]{1,0:T(8,128)(2,1)}, u32[]{:S(2)}) copy-start(bf16[1024,1536]{1,0:T(8,128)(2,1)} %copy-done.32) | copy-start | bytes 9437188
  382.3 17.7 %collective-permute-start.4 = (bf16[1024,1536]{1,0:T(8,128)(2,1)}, bf16[1024,1536]{1,0:T(8,128)(2,1)}, u32[]{:S(2)}, u32[]{:S(2)}) collective-permute-start(bf16[1024,1536]{1,0:T(8,128)(2,1)} %shard_map.313), channel_id=1, source_target_pairs={{0,2},{2,0},{4,6},{6,4},{8,10},{10,8},{12,14},{14,12},{16,18},{18,... | collective-permute-start | bytes 9437192 | tf_op jit(solution)/shard_map/ppermute | solution.py:1388
  384.0 77.8 %collective-permute-start.8 = (bf16[768,1152]{1,0:T(8,128)(2,1)}, bf16[768,1152]{1,0:T(8,128)(2,1)}, u32[]{:S(2)}, u32[]{:S(2)}) collective-permute-start(bf16[768,1152]{1,0:T(8,128)(2,1)} %shard_map.308), channel_id=1, source_target_pairs={{0,8},{2,10},{4,12},{6,14},{8,0},{10,2},{12,4},{14,6},{16,24},{18,... | collective-permute-start | bytes 5308424 | tf_op jit(solution)/shard_map/ppermute | solution.py:1388
  384.4 57.0 %collective-permute-start.9 = (bf16[384,1152]{1,0:T(8,128)(2,1)}, bf16[384,1152]{1,0:T(8,128)(2,1)}, u32[]{:S(2)}, u32[]{:S(2)}) collective-permute-start(bf16[384,1152]{1,0:T(8,128)(2,1)} %add_convert_fusion.12), channel_id=1, source_target_pairs={{0,16},{2,18},{4,20},{6,22},{8,24},{10,26},{12,28},{14,30},{16,0},... | collective-permute-start | bytes 2654216 | tf_op jit(solution)/shard_map/ppermute | solution.py:1388
  390.6 101.9 %collective-permute-start.6 = (bf16[384,1152]{1,0:T(8,128)(2,1)}, bf16[384,1152]{1,0:T(8,128)(2,1)S(1)}, u32[]{:S(2)}, u32[]{:S(2)}) collective-permute-start(bf16[384,1152]{1,0:T(8,128)(2,1)} %add_convert_fusion.11), channel_id=1, source_target_pairs={{0,16},{2,18},{4,20},{6,22},{8,24},{10,26},{12,28},{14,30},{16,0},... | collective-permute-start | bytes 2654216 | tf_op jit(solution)/shard_map/ppermute | solution.py:1388
  390.7 73.5 %collective-permute-start.7 = (bf16[512,1536]{1,0:T(8,128)(2,1)}, bf16[512,1536]{1,0:T(8,128)(2,1)S(1)}, u32[]{:S(2)}, u32[]{:S(2)}) collective-permute-start(bf16[512,1536]{1,0:T(8,128)(2,1)} %add_convert_fusion.3.back), channel_id=1, source_target_pairs={{0,1},{1,0},{2,3},{3,2},{4,5},{5,4},{6,7},{7,6},{8,9},{9,8},{10,11... | collective-permute-start | bytes 4718600 | tf_op jit(solution)/shard_map/ppermute | solution.py:1388
  400.1 41.4 %copy-start.4 = (bf16[768,1152]{1,0:T(8,128)(2,1)S(1)}, bf16[768,1152]{1,0:T(8,128)(2,1)}, u32[]{:S(2)}) copy-start(bf16[768,1152]{1,0:T(8,128)(2,1)} %copy-done.3) | copy-start | bytes 5308420
  403.6 105.7 %collective-permute-start.5 = (bf16[512,1536]{1,0:T(8,128)(2,1)}, bf16[512,1536]{1,0:T(8,128)(2,1)}, u32[]{:S(2)}, u32[]{:S(2)}) collective-permute-start(bf16[512,1536]{1,0:T(8,128)(2,1)} %add_convert_fusion.1), channel_id=1, source_target_pairs={{0,4},{2,6},{4,0},{6,2},{8,12},{10,14},{12,8},{14,10},{16,20},{18,... | collective-permute-start | bytes 4718600 | tf_op jit(solution)/shard_map/ppermute | solution.py:1388
  464.1 50.4 %collective-permute-start.11 = (bf16[384,1152]{1,0:T(8,128)(2,1)}, bf16[384,1152]{1,0:T(8,128)(2,1)}, u32[]{:S(2)}, u32[]{:S(2)}) collective-permute-start(bf16[384,1152]{1,0:T(8,128)(2,1)} %add_convert_fusion.8), channel_id=1, source_target_pairs={{0,16},{2,18},{4,20},{6,22},{8,24},{10,26},{12,28},{14,30},{16,0},... | collective-permute-start | bytes 2654216 | tf_op jit(solution)/shard_map/ppermute | solution.py:1388
  493.8 3.7 collective-permute-start.13
  494.6 7.4 collective-permute-start.14
  494.9 12.1 %collective-permute-start.15 = (bf16[1,96,1152]{2,1,0:T(8,128)(2,1)}, bf16[1,96,1152]{2,1,0:T(8,128)(2,1)}, u32[]{:S(2)}, u32[]{:S(2)}) collective-permute-start(bf16[1,96,1152]{2,1,0:T(8,128)(2,1)} %get-tuple-element.140), channel_id=1, source_target_pairs={{0,6},{2,4},{4,2},{6,0},{8,14},{10,12},{12,10},{14,8},{16,22},{18,... | collective-permute-start | bytes 663560 | tf_op jit(solution)/shard_map/ppermute | solution.py:1388
  497.6 88.2 %collective-permute-start.12 = (bf16[512,1536]{1,0:T(8,128)(2,1)}, bf16[512,1536]{1,0:T(8,128)(2,1)S(1)}, u32[]{:S(2)}, u32[]{:S(2)}) collective-permute-start(bf16[512,1536]{1,0:T(8,128)(2,1)} %get-tuple-element.100), channel_id=1, source_target_pairs={{0,1},{1,0},{2,3},{3,2},{4,5},{5,4},{6,7},{7,6},{8,9},{9,8},{10,11... | collective-permute-start | bytes 4718600 | tf_op jit(solution)/shard_map/ppermute | solution.py:1388
  513.2 72.6 %collective-permute-start.10 = (bf16[512,1536]{1,0:T(8,128)(2,1)S(1)}, bf16[512,1536]{1,0:T(8,128)(2,1)S(1)}, u32[]{:S(2)}, u32[]{:S(2)}) collective-permute-start(bf16[512,1536]{1,0:T(8,128)(2,1)S(1)} %add_convert_fusion), channel_id=1, source_target_pairs={{0,1},{1,0},{2,3},{3,2},{4,5},{5,4},{6,7},{7,6},{8,9},{9,8},{10,11... | collective-permute-start | bytes 4718600 | tf_op jit(solution)/shard_map/ppermute | solution.py:1388
  516.8 61.9 %copy-start.30 = (f32[2,96,4480]{2,1,0:T(8,128)S(1)}, f32[2,96,4480]{2,1,0:T(8,128)}, u32[]{:S(2)}) copy-start(f32[2,96,4480]{2,1,0:T(8,128)} %param.28) | copy-start | bytes 10321924
  (49 other events, 162.2 us)

commit v4 on v3

--- a/solution.py
+++ b/solution.py
@@ -209,12 +209,13 @@
             device,
         )
 
+    def to_keeper(what):
+        @pl.when(jnp.logical_not(keeps))
+        def _():
+            what(way_in(blocks, 0, me, keeper))
+            what(way_in(blocks + 1, 1, me, keeper))
+
     def to_owner(device, what):
-        @pl.when(device == keeper)
-        def _():
-            what(way_in(blocks, 0, me, device))
-            what(way_in(blocks + 1, 1, me, device))
-
         @pl.when(jnp.logical_and(device != keeper, block_of(device) < blocks))
         def _():
             what(way_in(block_of(device), 0, me, device))
@@ -224,6 +225,7 @@
             vectors, all_vectors.at[sender], go_vector.at[device], come_vector.at[sender], device
         )
 
+    to_keeper(lambda copy: copy.start())
     others(lambda device: to_owner(device, lambda copy: copy.start()))
     others(lambda device: share(me, device).start())
 
@@ -331,6 +333,7 @@
         way_back(blocks, 0, me).wait_recv()
         way_back(blocks + 1, 1, me).wait_recv()
 
+    to_keeper(lambda copy: copy.wait_send())
     others(lambda device: to_owner(device, lambda copy: copy.wait_send()))
 
     @pl.when(jnp.logical_or(keeps, holds))
@@ -713,22 +716,28 @@
             block(owner), block(owner), core_send.at[turn, far], core_come.at[turn, far], beside
         )
 
-    def unit_rows(owner):
-        return ffn_full.at[pl.ds(pl.multiple_of(owner * rows, 16), rows)]
-
-    def group_copy(turn):
+    def third_of(owner, third):
+        return ffn_full.at[
+            pl.ds(pl.multiple_of(owner * rows, 16), rows), third * part : (third + 1) * part
+        ]
+
+    def group_copy(turn, third):
         return remote(
-            units.at[lax.rem(place + turn, 4)],
-            unit_rows(me),
-            group_send.at[turn],
-            group_come.at[turn],
+            units.at[lax.rem(place + turn, 4), :, third * part : (third + 1) * part],
+            third_of(me, third),
+            group_send.at[turn, third],
+            group_come.at[turn, third],
             plane_peer(turn),
         )
 
-    def group_wait(turn):
+    def group_wait(turn, third):
         owner = plane * 4 + lax.rem(place + 4 - turn, 4)
         return remote(
-            units.at[0], unit_rows(owner), group_send.at[turn], group_come.at[turn], me
+            third_of(owner, third),
+            third_of(owner, third),
+            group_send.at[turn, third],
+            group_come.at[turn, third],
+            me,
         )
 
     def slab(origin, third):
@@ -782,8 +791,11 @@
     loop(1, planes, lambda turn: to_column(turn).start())
     own_block = pltpu.make_async_copy(shard, block(me), here_sem.at[0])
     own_block.start()
-    loop(1, 4, lambda turn: group_copy(turn).start())
-    own_units = pltpu.make_async_copy(units.at[place], unit_rows(me), here_sem.at[1])
+    for third in range(3):
+        loop(1, 4, lambda turn: group_copy(turn, third).start())
+    own_units = pltpu.make_async_copy(
+        units.at[place], ffn_full.at[pl.ds(pl.multiple_of(me * rows, 16), rows)], here_sem.at[1]
+    )
     own_units.start()
     own_grads = pltpu.make_async_copy(grads, grads_all.at[0:count], here_sem.at[2])
     own_grads.start()
@@ -797,6 +809,19 @@
             tokens[first : first + 128, :].astype(FLOAT), gains[0:1, :]
         )
 
+    def slabs(third):
+        loop(1, 4, lambda turn: group_wait(turn, third).wait_recv())
+
+        @pl.when(plane < planes - 1)
+        def _():
+            move(plane, third, True).start()
+
+        @pl.when(plane > 0)
+        def _():
+            move(plane, third, False).start()
+
+    own_units.wait()
+    slabs(0)
     own_block.wait()
     x_copy(0).start()
     core_copy(0, 0).start()
@@ -807,18 +832,8 @@
         core_copy(turn, 0).start()
 
     loop(1, planes, forward)
-    own_units.wait()
-    loop(1, 4, lambda turn: group_wait(turn).wait_recv())
-    for third in range(3):
-
-        @pl.when(plane < planes - 1)
-        def _():
-            move(plane, third, True).start()
-
-        @pl.when(plane > 0)
-        def _():
-            move(plane, third, False).start()
-
+    slabs(1)
+    slabs(2)
     own_grads.wait()
     x_rows(grads_all, 0).start()
 
@@ -927,7 +942,8 @@
         core_copy(turn, 1).wait_send()
 
     loop(0, planes, sent)
-    loop(1, 4, lambda turn: group_copy(turn).wait_send())
+    for third in range(3):
+        loop(1, 4, lambda turn: group_copy(turn, third).wait_send())
     for third in range(3):
 
         @pl.when(plane < planes - 1)
@@ -979,8 +995,8 @@
             dma((planes,)),
             dma((planes, 2)),
             dma((planes, 2)),
-            dma((4,)),
-            dma((4,)),
+            dma((4, 3)),
+            dma((4, 3)),
             dma((planes, 3)),
             dma((planes, 3)),
             dma((planes, 3)),

time: 795 us -> 792 us (level)
  no operation moved by 1% of the time
where the time goes in v4:
time: 792 us; the launch traced here: 777 us
  Pallas kernels  603 us (76%)
  waiting for transfers between devices  76.6 us (10%)
  other arithmetic  61.2 us (8%)
  local copies, waits for them, and re-layouts  21.9 us (3%)
  starting transfers between devices  12.6 us (2%)
    pallas_call x1, Pallas kernels, forward_part(): pl.pallas_call(functools.partial(forward_kernel, devices, heads, kv_heads...  207 us
    pallas_call x1, Pallas kernels, orthogonalize(): pl.pallas_call(kernel, out_shape=[jax.ShapeDtypeStruct(units.shape, wire)...  171 us
    pallas_call x6, Pallas kernels, call_light(): pl.pallas_call(body, grid=grid, in_specs=[pl.BlockSpec(block, at) for _,...  86.8 us
    ppermute x16, waiting for transfers between devices, swap(): return lax.ppermute(value, axis, [(at, at ^ stride) for at in range(count)])  76.6 us
    pallas_call x1, Pallas kernels, exchange(): pl.pallas_call(exchange_kernel, out_shape=[jax.ShapeDtypeStruct((rows, wi...  62.9 us
    pallas_call x6, Pallas kernels, weight_term(): pl.pallas_call(body, grid_spec=pltpu.PrefetchScalarGridSpec(num_scalar_pr...  48 us
    pallas_call x1, Pallas kernels, backward_part(): pl.pallas_call(body, out_shape=[jax.ShapeDtypeStruct((count, depth), FLOA...  27.3 us
  transfers between devices with their start and end apart: 16, of which 6 were waited for; matrix products, arithmetic and copies ran while one was open for 4% of the time, Pallas kernels for 22%

profile of v4, /device:TPU:27, one launch (start us, length us, event | category | flops | bytes accessed | tf_op | source)
XLA Modules:
  0.0 777.2 jit_solution(15712613842455894840)
XLA Ops:
  15.7 206.7 %shard_map.302 = (bf16[512,1536]{1,0:T(8,128)(2,1)S(1)}, f32[512,1536]{1,0:T(8,128)}, bf16[512,768]{1,0:T(8,128)(2,1)S(1)}, bf16[512,768]{1,0:T(8,128)(2,1)S(1)}...) custom-call(bf16[512,1536]{1,0:T(8,128)(2,1)S(1)} %copy-done, ...), custom_call_target="tpu_custom_call" | custom-call | flops 1024 | bytes 1024 | tf_op jit(solution)/shard_map/pallas_call | solution.py:969
  226.7 24.7 %shard_map.303 = (f32[2048,1152]{1,0:T(8,128)}, f32[2048,1152]{1,0:T(8,128)}, bf16[2048,1152]{1,0:T(8,128)(2,1)}, bf16[1536,2048]{1,0:T(8,128)(2,1)}, bf16[1536,2048]{1,0:T(8,128)(2,1)}) custom-call(bf16[2048,1536]{1,0:T(8,128)(2,1)} %get-tuple-element.69.x, bf16[2048,1536]{1,0:T(8,128)(2,1)} %get-tuple-element.75.y.x, ...), custom_call_target="tpu_custom_call" | custom-call | flops 1024 | bytes 1024 | tf_op jit(solution)/shard_map/pallas_call | solution.py:397
  251.4 7.8 %shard_map.304 = bf16[768,1152]{1,0:T(8,128)(2,1)S(1)} custom-call(s32[2]{0:T(128)S(1)} %pad_add_fusion.1.blocks, bf16[1536,2048]{1,0:T(8,128)(2,1)} %get-tuple-element.73.x, bf16[2048,1152]{1,0:T(8,128)(2,1)} %get-tuple-element.89.y.x), custom_call_target="tpu_custom_call" | custom-call | flops 1024 | bytes 1024 | tf_op jit(solution)/shard_map/pallas_call | solution.py:513
  259.4 7.8 %shard_map.305 = bf16[768,1152]{1,0:T(8,128)(2,1)S(1)} custom-call(s32[2]{0:T(128)S(1)} %pad_add_fusion.blocks, bf16[1536,2048]{1,0:T(8,128)(2,1)} %get-tuple-element.73.x, bf16[2048,1152]{1,0:T(8,128)(2,1)} %get-tuple-element.89.y.x), custom_call_target="tpu_custom_call" | custom-call | flops 1024 | bytes 1024 | tf_op jit(solution)/shard_map/pallas_call | solution.py:513
  267.2 18.9 %shard_map.306.y.x = bf16[2048,2304]{1,0:T(8,128)(2,1)} custom-call(bf16[2048,1536]{1,0:T(8,128)(2,1)} %get-tuple-element.75.y.x, bf16[1536,3456]{1,0:T(8,128)(2,1)} %get-tuple-element.71.w_gate.w_up.w.refs_0_.refs_1_, f32[2048,1152]{1,0:T(8,128)} %get-tuple-element.76.gate, f32[2048,1152]{1,0:T(8,128)} %get-tuple-element.77.up), custom_call_target="tpu_custom_call" | custom-call | flops 1024 | bytes 1024 | tf_op jit(solution)/shard_map/pallas_call | solution.py:397
  286.1 7.8 %shard_map.307 = bf16[768,1152]{1,0:T(8,128)(2,1)S(1)} custom-call(s32[2]{0:T(128)S(1)} %pad_add_fusion.1.blocks, bf16[1536,2048]{1,0:T(8,128)(2,1)} %get-tuple-element.86.x, bf16[2048,2304]{1,0:T(8,128)(2,1)} %shard_map.306.y.x), custom_call_target="tpu_custom_call" | custom-call | flops 1024 | bytes 1024 | tf_op jit(solution)/shard_map/pallas_call | solution.py:513
  293.9 8.7 %shard_map.308 = bf16[768,1152]{1,0:T(8,128)(2,1)} custom-call(s32[2]{0:T(128)S(1)} %pad_add_fusion.1.blocks, bf16[1536,2048]{1,0:T(8,128)(2,1)} %get-tuple-element.86.x, bf16[2048,2304]{1,0:T(8,128)(2,1)} %shard_map.306.y.x), custom_call_target="tpu_custom_call" | custom-call | flops 1024 | bytes 1024 | tf_op jit(solution)/shard_map/pallas_call | solution.py:513
  304.9 13.3 %shard_map.309 = bf16[1024,1536]{1,0:T(8,128)(2,1)} custom-call(bf16[2048,2304]{1,0:T(8,128)(2,1)} %shard_map.306.y.x, bf16[1536,3456]{1,0:T(8,128)(2,1)} %get-tuple-element.71.w_gate.w_up.w.refs_0_.refs_1_, bf16[1536,3456]{1,0:T(8,128)(2,1)} %get-tuple-element.71.w_gate.w_up.w.refs_0_.refs_1_), custom_call_target="tpu_custom_call" | custom-call | flops 1024 | bytes 1024 | tf_op jit(solution)/shard_map/pallas_call | solution.py:397
  320.4 13.7 %shard_map.310 = bf16[1024,1536]{1,0:T(8,128)(2,1)} custom-call(bf16[2048,2304]{1,0:T(8,128)(2,1)} %shard_map.306.y.x, bf16[1536,3456]{1,0:T(8,128)(2,1)} %get-tuple-element.71.w_gate.w_up.w.refs_0_.refs_1_, bf16[1536,3456]{1,0:T(8,128)(2,1)} %get-tuple-element.71.w_gate.w_up.w.refs_0_.refs_1_), custom_call_target="tpu_custom_call" | custom-call | flops 1024 | bytes 1024 | tf_op jit(solution)/shard_map/pallas_call | solution.py:397
  334.1 4.0 add_convert_fusion.4
  338.4 7.8 %shard_map.311 = bf16[768,1152]{1,0:T(8,128)(2,1)S(1)} custom-call(s32[2]{0:T(128)S(1)} %pad_add_fusion.blocks, bf16[1536,2048]{1,0:T(8,128)(2,1)} %get-tuple-element.86.x, bf16[2048,2304]{1,0:T(8,128)(2,1)} %shard_map.306.y.x), custom_call_target="tpu_custom_call" | custom-call | flops 1024 | bytes 1024 | tf_op jit(solution)/shard_map/pallas_call | solution.py:513
  346.3 13.1 %collective-permute-done.3 = bf16[768,1152]{1,0:T(8,128)(2,1)S(1)} collective-permute-done((bf16[768,1152]{1,0:T(8,128)(2,1)S(1)}, bf16[768,1152]{1,0:T(8,128)(2,1)S(1)}, u32[]{:S(2)}, u32[]{:S(2)}) %collective-permute-start.3) | collective-permute-done | bytes 1769504 | tf_op jit(solution)/shard_map/ppermute | solution.py:1404
  361.7 8.1 %shard_map.312 = bf16[768,1152]{1,0:T(8,128)(2,1)S(1)} custom-call(s32[2]{0:T(128)S(1)} %pad_add_fusion.blocks, bf16[1536,2048]{1,0:T(8,128)(2,1)} %get-tuple-element.86.x, bf16[2048,2304]{1,0:T(8,128)(2,1)} %shard_map.306.y.x), custom_call_target="tpu_custom_call" | custom-call | flops 1024 | bytes 1024 | tf_op jit(solution)/shard_map/pallas_call | solution.py:513
  369.8 4.3 collective-permute-done.2
  375.9 8.1 %shard_map.313 = bf16[1024,1536]{1,0:T(8,128)(2,1)} custom-call(bf16[2048,1152]{1,0:T(8,128)(2,1)} %get-tuple-element.89.y.x, bf16[1536,3456]{1,0:T(8,128)(2,1)} %get-tuple-element.71.w_gate.w_up.w.refs_0_.refs_1_), custom_call_target="tpu_custom_call" | custom-call | flops 1024 | bytes 1024 | tf_op jit(solution)/shard_map/pallas_call | solution.py:397
  390.6 8.1 %shard_map.314 = bf16[1024,1536]{1,0:T(8,128)(2,1)} custom-call(bf16[2048,1152]{1,0:T(8,128)(2,1)} %get-tuple-element.89.y.x, bf16[1536,3456]{1,0:T(8,128)(2,1)} %get-tuple-element.71.w_gate.w_up.w.refs_0_.refs_1_), custom_call_target="tpu_custom_call" | custom-call | flops 1024 | bytes 1024 | tf_op jit(solution)/shard_map/pallas_call | solution.py:397
  398.7 3.5 add_convert_fusion.1
  402.5 39.9 %collective-permute-done.9 = bf16[384,1152]{1,0:T(8,128)(2,1)} collective-permute-done((bf16[384,1152]{1,0:T(8,128)(2,1)}, bf16[384,1152]{1,0:T(8,128)(2,1)}, u32[]{:S(2)}, u32[]{:S(2)}) %collective-permute-start.9) | collective-permute-done | bytes 884768 | tf_op jit(solution)/shard_map/ppermute | solution.py:1404
  444.2 10.8 %collective-permute-done.8 = bf16[768,1152]{1,0:T(8,128)(2,1)} collective-permute-done((bf16[768,1152]{1,0:T(8,128)(2,1)}, bf16[768,1152]{1,0:T(8,128)(2,1)}, u32[]{:S(2)}, u32[]{:S(2)}) %collective-permute-start.8) | collective-permute-done | bytes 1769504 | tf_op jit(solution)/shard_map/ppermute | solution.py:1404
  458.7 27.3 %shard_map.315 = (f32[512,1536]{1,0:T(8,128)}, f32[1,1536]{1,0:T(1,128)}, f32[1,1024]{1,0:T(1,128)}, bf16[512,1536]{1,0:T(8,128)(2,1)}, bf16[8,96,1792]{2,1,0:T(8,128)(2,1)}, /*index=5*/bf16[8,96,1792]{2,1,0:T(8,128)(2,1)}) custom-call(bf16[512,1536]{1,0:T(8,128)(2,1)} %add_convert_fusion.3.back, bf16[512,1536]{1,0:T(8,128)(2,1)} %copy-done.42, ...), custom_call_target="tpu_custom_call" | custom-call | flops 1024 | bytes 1024 | tf_op jit(solution)/shard_map/pallas_call | solution.py:1341
  495.7 5.1 collective-permute-done.15
  510.6 62.9 %shard_map.316 = (f32[96,1792]{1,0:T(8,128)S(1)}, bf16[2,96,4608]{2,1,0:T(8,128)(2,1)S(1)}) custom-call(bf16[8,96,1792]{2,1,0:T(8,128)(2,1)S(1)} %copy-done.5, bf16[8,96,1792]{2,1,0:T(8,128)(2,1)S(1)} %copy-done.6, bf16[2,4,96,1152]{3,2,1,0:T(8,128)(2,1)S(1)} %pad_maximum_fusion.1.pieces), custom_call_target="tpu_custom_call" | custom-call | flops 1024 | bytes 1024 | tf_op jit(solution)/shard_map/pallas_call | solution.py:1148
  584.4 170.9 %shard_map.317 = (bf16[96,15232]{1,0:T(8,128)(2,1)}, f32[32,128]{1,0:T(8,128)S(1)}) custom-call(bf16[96,15232]{1,0:T(8,128)(2,1)} %copy-done.47, f32[32,128]{1,0:T(8,128)S(1)} %maximum_bitcast_fusion.vectors), custom_call_target="tpu_custom_call" | custom-call | flops 64000000000 | bytes 16777216 | tf_op jit(solution)/shard_map/pallas_call | solution.py:357
  767.3 4.7 multiply_subtract_fusion
  (215 shorter events, 86.7 us)
Async XLA Ops:
  13.1 209.3 %copy-start.7 = (f32[512,128]{1,0:T(8,128)}, f32[512,128]{1,0:T(8,128)S(1)}, u32[]{:S(2)}) copy-start(f32[512,128]{1,0:T(8,128)S(1)} %get-tuple-element.148.cosine) | copy-start | bytes 786436
  13.2 209.3 %copy-start.8 = (f32[512,128]{1,0:T(8,128)}, f32[512,128]{1,0:T(8,128)S(1)}, u32[]{:S(2)}) copy-start(f32[512,128]{1,0:T(8,128)S(1)} %get-tuple-element.149.sine) | copy-start | bytes 786436
  259.2 43.4 %collective-permute-start = (bf16[768,1152]{1,0:T(8,128)(2,1)S(1)}, bf16[768,1152]{1,0:T(8,128)(2,1)}, u32[]{:S(2)}, u32[]{:S(2)}) collective-permute-start(bf16[768,1152]{1,0:T(8,128)(2,1)S(1)} %shard_map.304), channel_id=1, source_target_pairs={{0,8},{2,10},{4,12},{6,14},{8,0},{10,2},{12,4},{14,6},{16,24},{18,... | collective-permute-start | bytes 5308424 | tf_op jit(solution)/shard_map/ppermute | solution.py:1404
  267.2 35.4 %copy-start.3 = (bf16[768,1152]{1,0:T(8,128)(2,1)}, bf16[768,1152]{1,0:T(8,128)(2,1)S(1)}, u32[]{:S(2)}) copy-start(bf16[768,1152]{1,0:T(8,128)(2,1)S(1)} %shard_map.305) | copy-start | bytes 5308420
  318.2 15.9 %collective-permute-start.1 = (bf16[1024,1536]{1,0:T(8,128)(2,1)}, bf16[1024,1536]{1,0:T(8,128)(2,1)S(1)}, u32[]{:S(2)}, u32[]{:S(2)}) collective-permute-start(bf16[1024,1536]{1,0:T(8,128)(2,1)} %shard_map.309), channel_id=1, source_target_pairs={{0,2},{2,0},{4,6},{6,4},{8,10},{10,8},{12,14},{14,12},{16,18},{18,... | collective-permute-start | bytes 9437192 | tf_op jit(solution)/shard_map/ppermute | solution.py:1404
  318.7 40.7 %collective-permute-start.3 = (bf16[768,1152]{1,0:T(8,128)(2,1)S(1)}, bf16[768,1152]{1,0:T(8,128)(2,1)S(1)}, u32[]{:S(2)}, u32[]{:S(2)}) collective-permute-start(bf16[768,1152]{1,0:T(8,128)(2,1)S(1)} %shard_map.307), channel_id=1, source_target_pairs={{0,8},{2,10},{4,12},{6,14},{8,0},{10,2},{12,4},{14,6},{16,24},{18,... | collective-permute-start | bytes 5308424 | tf_op jit(solution)/shard_map/ppermute | solution.py:1404
  338.2 35.9 %collective-permute-start.2 = (bf16[512,1536]{1,0:T(8,128)(2,1)}, bf16[512,1536]{1,0:T(8,128)(2,1)S(1)}, u32[]{:S(2)}, u32[]{:S(2)}) collective-permute-start(bf16[512,1536]{1,0:T(8,128)(2,1)} %add_convert_fusion.4), channel_id=1, source_target_pairs={{0,4},{2,6},{4,0},{6,2},{8,12},{10,14},{12,8},{14,10},{16,20},{18,... | collective-permute-start | bytes 4718600 | tf_op jit(solution)/shard_map/ppermute | solution.py:1404
  346.3 23.5 %copy-start.1 = (bf16[768,1152]{1,0:T(8,128)(2,1)}, bf16[768,1152]{1,0:T(8,128)(2,1)S(1)}, u32[]{:S(2)}) copy-start(bf16[768,1152]{1,0:T(8,128)(2,1)S(1)} %shard_map.311) | copy-start | bytes 5308420
  361.7 12.4 %copy-start.20 = (bf16[1024,1536]{1,0:T(8,128)(2,1)S(1)}, bf16[1024,1536]{1,0:T(8,128)(2,1)}, u32[]{:S(2)}) copy-start(bf16[1024,1536]{1,0:T(8,128)(2,1)} %shard_map.310) | copy-start | bytes 9437188
  361.7 12.4 %copy-start.33 = (bf16[1024,1536]{1,0:T(8,128)(2,1)S(1)}, bf16[1024,1536]{1,0:T(8,128)(2,1)}, u32[]{:S(2)}) copy-start(bf16[1024,1536]{1,0:T(8,128)(2,1)} %copy-done.32) | copy-start | bytes 9437188
  384.0 14.7 %collective-permute-start.4 = (bf16[1024,1536]{1,0:T(8,128)(2,1)}, bf16[1024,1536]{1,0:T(8,128)(2,1)}, u32[]{:S(2)}, u32[]{:S(2)}) collective-permute-start(bf16[1024,1536]{1,0:T(8,128)(2,1)} %shard_map.313), channel_id=1, source_target_pairs={{0,2},{2,0},{4,6},{6,4},{8,10},{10,8},{12,14},{14,12},{16,18},{18,... | collective-permute-start | bytes 9437192 | tf_op jit(solution)/shard_map/ppermute | solution.py:1404
  385.1 69.9 %collective-permute-start.8 = (bf16[768,1152]{1,0:T(8,128)(2,1)}, bf16[768,1152]{1,0:T(8,128)(2,1)}, u32[]{:S(2)}, u32[]{:S(2)}) collective-permute-start(bf16[768,1152]{1,0:T(8,128)(2,1)} %shard_map.308), channel_id=1, source_target_pairs={{0,8},{2,10},{4,12},{6,14},{8,0},{10,2},{12,4},{14,6},{16,24},{18,... | collective-permute-start | bytes 5308424 | tf_op jit(solution)/shard_map/ppermute | solution.py:1404
  385.5 57.0 %collective-permute-start.9 = (bf16[384,1152]{1,0:T(8,128)(2,1)}, bf16[384,1152]{1,0:T(8,128)(2,1)}, u32[]{:S(2)}, u32[]{:S(2)}) collective-permute-start(bf16[384,1152]{1,0:T(8,128)(2,1)} %add_convert_fusion.12), channel_id=1, source_target_pairs={{0,16},{2,18},{4,20},{6,22},{8,24},{10,26},{12,28},{14,30},{16,0},... | collective-permute-start | bytes 2654216 | tf_op jit(solution)/shard_map/ppermute | solution.py:1404
  387.1 98.9 %collective-permute-start.6 = (bf16[384,1152]{1,0:T(8,128)(2,1)}, bf16[384,1152]{1,0:T(8,128)(2,1)S(1)}, u32[]{:S(2)}, u32[]{:S(2)}) collective-permute-start(bf16[384,1152]{1,0:T(8,128)(2,1)} %add_convert_fusion.11), channel_id=1, source_target_pairs={{0,16},{2,18},{4,20},{6,22},{8,24},{10,26},{12,28},{14,30},{16,0},... | collective-permute-start | bytes 2654216 | tf_op jit(solution)/shard_map/ppermute | solution.py:1404
  389.4 68.2 %collective-permute-start.7 = (bf16[512,1536]{1,0:T(8,128)(2,1)}, bf16[512,1536]{1,0:T(8,128)(2,1)S(1)}, u32[]{:S(2)}, u32[]{:S(2)}) collective-permute-start(bf16[512,1536]{1,0:T(8,128)(2,1)} %add_convert_fusion.3.back), channel_id=1, source_target_pairs={{0,1},{1,0},{2,3},{3,2},{4,5},{5,4},{6,7},{7,6},{8,9},{9,8},{10,11... | collective-permute-start | bytes 4718600 | tf_op jit(solution)/shard_map/ppermute | solution.py:1404
  398.7 43.7 %copy-start.4 = (bf16[768,1152]{1,0:T(8,128)(2,1)S(1)}, bf16[768,1152]{1,0:T(8,128)(2,1)}, u32[]{:S(2)}) copy-start(bf16[768,1152]{1,0:T(8,128)(2,1)} %copy-done.3) | copy-start | bytes 5308420
  402.3 100.8 %collective-permute-start.5 = (bf16[512,1536]{1,0:T(8,128)(2,1)}, bf16[512,1536]{1,0:T(8,128)(2,1)}, u32[]{:S(2)}, u32[]{:S(2)}) collective-permute-start(bf16[512,1536]{1,0:T(8,128)(2,1)} %add_convert_fusion.1), channel_id=1, source_target_pairs={{0,4},{2,6},{4,0},{6,2},{8,12},{10,14},{12,8},{14,10},{16,20},{18,... | collective-permute-start | bytes 4718600 | tf_op jit(solution)/shard_map/ppermute | solution.py:1404
  457.4 50.7 %collective-permute-start.11 = (bf16[384,1152]{1,0:T(8,128)(2,1)}, bf16[384,1152]{1,0:T(8,128)(2,1)}, u32[]{:S(2)}, u32[]{:S(2)}) collective-permute-start(bf16[384,1152]{1,0:T(8,128)(2,1)} %add_convert_fusion.8), channel_id=1, source_target_pairs={{0,16},{2,18},{4,20},{6,22},{8,24},{10,26},{12,28},{14,30},{16,0},... | collective-permute-start | bytes 2654216 | tf_op jit(solution)/shard_map/ppermute | solution.py:1404
  487.3 4.0 collective-permute-start.13
  488.3 7.4 collective-permute-start.14
  488.8 12.1 %collective-permute-start.15 = (bf16[1,96,1152]{2,1,0:T(8,128)(2,1)}, bf16[1,96,1152]{2,1,0:T(8,128)(2,1)}, u32[]{:S(2)}, u32[]{:S(2)}) collective-permute-start(bf16[1,96,1152]{2,1,0:T(8,128)(2,1)} %get-tuple-element.140), channel_id=1, source_target_pairs={{0,6},{2,4},{4,2},{6,0},{8,14},{10,12},{12,10},{14,8},{16,22},{18,... | collective-permute-start | bytes 663560 | tf_op jit(solution)/shard_map/ppermute | solution.py:1404
  491.3 89.3 %collective-permute-start.12 = (bf16[512,1536]{1,0:T(8,128)(2,1)}, bf16[512,1536]{1,0:T(8,128)(2,1)S(1)}, u32[]{:S(2)}, u32[]{:S(2)}) collective-permute-start(bf16[512,1536]{1,0:T(8,128)(2,1)} %get-tuple-element.100), channel_id=1, source_target_pairs={{0,1},{1,0},{2,3},{3,2},{4,5},{5,4},{6,7},{7,6},{8,9},{9,8},{10,11... | collective-permute-start | bytes 4718600 | tf_op jit(solution)/shard_map/ppermute | solution.py:1404
  507.0 73.6 %collective-permute-start.10 = (bf16[512,1536]{1,0:T(8,128)(2,1)S(1)}, bf16[512,1536]{1,0:T(8,128)(2,1)S(1)}, u32[]{:S(2)}, u32[]{:S(2)}) collective-permute-start(bf16[512,1536]{1,0:T(8,128)(2,1)S(1)} %add_convert_fusion), channel_id=1, source_target_pairs={{0,1},{1,0},{2,3},{3,2},{4,5},{5,4},{6,7},{7,6},{8,9},{9,8},{10,11... | collective-permute-start | bytes 4718600 | tf_op jit(solution)/shard_map/ppermute | solution.py:1404
  510.6 62.9 %copy-start.30 = (f32[2,96,4480]{2,1,0:T(8,128)S(1)}, f32[2,96,4480]{2,1,0:T(8,128)}, u32[]{:S(2)}) copy-start(f32[2,96,4480]{2,1,0:T(8,128)} %param.28) | copy-start | bytes 10321924
  (49 other events, 163.0 us)
